TPU v7x, 128 devices: a whole 4x4x4 slice. The times are simulated.
128 devices in a mesh: rows: 4 (over x_lo, core), cols: 32 (over x_hi, y, z).
Axes of the slice: x: 4 (x_hi: 2, x_lo: 2; x = x_hi * 2 + x_lo), y: 4, z: 4, core: 2. Of those that a mesh axis runs over, the one named last changes fastest.
Arguments:
- atm_flux: bfloat16 [8192, 32, 128], P(('rows', 'cols')), may hold values from -6 to 6
- remap_weights: bfloat16 [64, 3, 128, 4096], P('rows', None, None, 'cols'), may hold values from -0.3125 to 0.3125
- intersection: int32 [64, 32, 3], P('rows', 'cols'), may hold values from 0 to 8191, as said below
- tracers: float32 [2, 62, 64, 4096], P(None, None, 'rows', 'cols'), may hold values from -6 to 6
- east_speed: float32 [62, 64, 4096], P(None, 'rows', 'cols'), may hold values from -0.25 to 0.25
- north_speed: float32 [62, 64, 4096], P(None, 'rows', 'cols'), may hold values from -0.25 to 0.25
- mixing: float32 [62, 64, 4096], P(None, 'rows', 'cols'), may hold values from 0.05 to 20
- level_count: int32 [64, 4096], P('rows', 'cols'), may hold values from 0 to 62
Outputs:
- ocean_flux: float32 [32, 64, 4096], P(None, 'rows', 'cols')
- tracers_out: float32 [2, 62, 64, 4096], P(None, None, 'rows', 'cols')
Inputs may be any that keep to these rules, and one draw needn't show every extreme that they name: `intersection`: slot s of ocean row y in longitude tile c names an atmosphere block held by the device of row group y // 16 and column index (c + 16 + s - 1) mod 32, blocks numbered device by device in the mesh order.
All inputs are finite; a program needn't handle non-finite values.
Results may differ from a plain program's by a relative error of at most 0.00075.
Values may be sent and summed in bfloat16 or wider, within the bound.
No kernel may reach another device: no remote copies, remote signals or barrier semaphores. Data moves between devices by JAX's collectives and lax.ppermute only.
A program may use at most 128 MiB of HBM per device.

v0:
```python
import jax
import jax.numpy as jnp
from jax import lax
from jax.experimental import pallas as pl
from jax.experimental.pallas import tpu as pltpu
from jax.sharding import PartitionSpec as P

F32 = jnp.float32
BF16 = jnp.bfloat16
VMEM = pl.BlockSpec(memory_space=pltpu.VMEM)
SMEM = pl.BlockSpec(memory_space=pltpu.SMEM)
INTERPRET = False
LIMIT = 24 * 1024 * 1024


def lanes(shape):
    return lax.broadcasted_iota(jnp.int32, shape, len(shape) - 1)


def sublanes(shape):
    return lax.broadcasted_iota(jnp.int32, shape, len(shape) - 2)


def turn(x, shift):
    shift = shift % x.shape[-1]
    return x if shift == 0 else pltpu.roll(x, shift, x.ndim - 1)


def prepare_kernel(
    tracers, east, north, mixing, count,
    face_e, face_n, inv, low, ratio, first, go_e, go_w, go_n, go_s,
):
    levels, height, width = east.shape
    lane, row = lanes((height, width)), sublanes((height, width))
    depth = count[...]
    zero = jnp.zeros((height, width), F32)
    a_prev, r_prev, low_a = zero, zero, zero
    e_x, w_x, e_c = zero, zero, zero
    for k in range(levels):
        wet = jnp.where(depth > k, 1.0, 0.0)
        wet_e = jnp.where(lane == width - 1, 1.0, turn(wet, -1))
        wet_n = jnp.where(row == height - 1, 1.0, pltpu.roll(wet, height - 1, 0))
        ce = east[k] * wet * wet_e
        face_e[k] = ce
        cn = north[k] * wet * wet_n
        face_n[k] = cn
        go_n[2, k : k + 1, :] = cn[height - 1 :, :]
        e_c = jnp.where(lane == k, turn(ce, k - (width - 1)), e_c)
        for t in range(2):
            x = tracers[t, k]
            at = k + t * (width // 2)
            e_x = jnp.where(lane == at, turn(x, at - (width - 1)), e_x)
            w_x = jnp.where(lane == at, turn(x, at), w_x)
            go_n[t, k : k + 1, :] = x[height - 1 :, :]
            go_s[t, k : k + 1, :] = x[:1, :]
        a = mixing[k] * jnp.where(depth > k + 1, 1.0, 0.0) if k + 1 < levels else zero
        iv = 1.0 / (1.0 + a_prev + a - a_prev * r_prev)
        inv[k] = iv
        low[k] = a_prev * iv
        r_prev = a * iv
        ratio[k] = r_prev
        a_prev = a
    for t in range(2):
        first[t] = tracers[t, 0]
    spare = go_n.shape[1] - levels
    for t in range(3):
        go_n[t, levels:, :] = jnp.zeros((spare, width), F32)
        go_s[t, levels:, :] = jnp.zeros((spare, width), F32)
    go_e[0], go_w[0], go_e[1] = e_x, w_x, e_c
    go_w[1] = jnp.where(lane < depth[:, :1], 1.0, 0.0)
    tall = sublanes((go_s.shape[1], width))
    go_s[2] = jnp.where(tall < depth[:1, :], 1.0, 0.0)


def force_kernel(
    place, index, a0, a1, a2, weights, count, first, go_e, go_w, go_n, go_s,
    forced, out_c0, out_c1, out_r0, out_r1, held, picked,
):
    height, width = count.shape
    blocks = a0.shape[0] // 2
    for s, a in enumerate((a0, a1, a2)):
        held[s] = a[...].astype(F32)
    for y in range(height):
        for s in range(3):
            b = lax.rem(index[3 * y + s], blocks)
            for f in range(2):
                picked[8 * y + f : 8 * y + f + 1, s * 128 : (s + 1) * 128] = held[
                    s, pl.ds(b + f * blocks, 1), :
                ]
    wet = jnp.where(count[...] > 0, 0.5, 0.0)
    for y in range(height):
        got = jnp.dot(
            picked[8 * y : 8 * y + 8].astype(BF16), weights[y], preferred_element_type=F32
        )
        for f in range(2):
            forced[f, y : y + 1, :] = got[f : f + 1, :]
    lane = lanes((height, width))
    e_x, w_x = go_e[0], go_w[0]
    tops, bottoms = [], []
    for t in range(2):
        x = first[t] + wet * forced[t]
        forced[t] = x
        at = t * (width // 2)
        e_x = jnp.where(lane == at, turn(x, at - (width - 1)), e_x)
        w_x = jnp.where(lane == at, turn(x, at), w_x)
        tops.append(x[height - 1 :, :])
        bottoms.append(x[:1, :])
    even_r, even_c = place[0] == 0, place[1] == 0
    out_c0[0] = jnp.where(even_c, e_x, w_x)
    out_c1[0] = jnp.where(even_c, w_x, e_x)
    out_c0[1] = jnp.where(even_c, go_e[1], go_w[1])
    out_c1[1] = jnp.where(even_c, go_w[1], go_e[1])
    out_r0[...] = jnp.where(even_r, go_n[...], go_s[...])
    out_r1[...] = jnp.where(even_r, go_s[...], go_n[...])
    for t in range(2):
        out_r0[t, :1, :] = jnp.where(even_r, tops[t], bottoms[t])
        out_r1[t, :1, :] = jnp.where(even_r, bottoms[t], tops[t])


def step(place, field, level0, face_e, face_n, inv, low, ratio, count,
         c0, c1, r0, r1, s0, s1, q0, q1, solved, out, messages):
    levels, height, width = face_e.shape
    lane, row = lanes((height, width)), sublanes((height, width))
    depth = count[...]
    even_r, even_c = place[0] == 0, place[1] == 0
    x_e = jnp.where(even_c, c0, c1)
    x_w = jnp.where(even_c, c1, c0)
    k_e = jnp.where(even_c, s0, s1)
    k_w = jnp.where(even_c, s1, s0)
    east_end, west_end = lane == width - 1, lane == 0
    north_end, south_end = row == height - 1, row == 0
    value = [None, None]
    for k in range(levels):
        wet = jnp.where(depth > k, 1.0, 0.0)
        ce = face_e[k]
        ce = jnp.where(east_end, ce * turn(k_e, width - 1 - k), ce)
        cw = turn(k_w, -k) * wet
        pa, pb = q0[k : k + 1, :], q1[k : k + 1, :]
        cn = face_n[k]
        cn = jnp.where(north_end, cn * jnp.where(even_r, pa, pb), cn)
        cs = jnp.where(even_r, pb, pa) * wet
        for t in range(2):
            x = level0[t] if (k == 0 and level0 is not None) else field[t, k]
            at = k + t * (width // 2)
            right = jnp.where(east_end, turn(x_e, width - 1 - at), turn(x, -1))
            fe = ce * jnp.where(ce > 0, x, right)
            fw = cw * jnp.where(cw > 0, turn(x_w, -at), x)
            fw = jnp.where(west_end, fw, turn(fe, 1))
            ra, rb = r0[t, k : k + 1, :], r1[t, k : k + 1, :]
            above = jnp.where(north_end, jnp.where(even_r, ra, rb), pltpu.roll(x, height - 1, 0))
            fn = cn * jnp.where(cn > 0, x, above)
            fs = cs * jnp.where(cs > 0, jnp.where(even_r, rb, ra), x)
            fs = jnp.where(south_end, fs, pltpu.roll(fn, 1, 0))
            moved = x - (fe - fw) - (fn - fs)
            now = moved * inv[k]
            if k:
                now = now + low[k] * value[t]
            value[t] = now
            solved[t, k] = now
    zero = jnp.zeros((height, width), F32)
    e_x, w_x = zero, zero
    for k in range(levels - 1, -1, -1):
        for t in range(2):
            if k < levels - 1:
                value[t] = solved[t, k] + ratio[k] * value[t]
            y = value[t]
            out[t, k] = y
            if messages is not None:
                at = k + t * (width // 2)
                e_x = jnp.where(lane == at, turn(y, at - (width - 1)), e_x)
                w_x = jnp.where(lane == at, turn(y, at), w_x)
                top, bottom = y[height - 1 :, :], y[:1, :]
                messages[2][t, k : k + 1, :] = jnp.where(even_r, top, bottom)
                messages[3][t, k : k + 1, :] = jnp.where(even_r, bottom, top)
    if messages is not None:
        messages[0][...] = jnp.where(even_c, e_x, w_x)
        messages[1][...] = jnp.where(even_c, w_x, e_x)
        spare = messages[2].shape[1] - levels
        for t in range(2):
            messages[2][t, levels:, :] = jnp.zeros((spare, width), F32)
            messages[3][t, levels:, :] = jnp.zeros((spare, width), F32)


def first_step_kernel(
    place, tracers, forced, face_e, face_n, inv, low, ratio, count, c0, c1, r0, r1,
    out, out_c0, out_c1, out_r0, out_r1, solved,
):
    step(place, tracers, forced, face_e, face_n, inv, low, ratio, count,
         c0[0], c1[0], r0, r1, c0[1], c1[1], r0.at[2], r1.at[2], solved, out,
         (out_c0, out_c1, out_r0, out_r1))


def second_step_kernel(
    place, field, face_e, face_n, inv, low, ratio, count, c0, c1, r0, r1, p0, p1, u0, u1, out, solved,
):
    step(place, field, None, face_e, face_n, inv, low, ratio, count,
         p0[...], p1[...], u0, u1, c0[1], c1[1], r0.at[2], r1.at[2], solved, out, None)


def remap_kernel(index, a0, a1, a2, weights, out):
    blocks = a0.shape[0]
    for y in range(out.shape[1]):
        rows = []
        for s, a in enumerate((a0, a1, a2)):
            b = lax.rem(index[3 * y + s], blocks)
            rows.append(a[pl.ds(b, 1)][0])
        got = jnp.dot(jnp.concatenate(rows, 1), weights[y], preferred_element_type=F32)
        out[:, y, :] = got


def call(kernel, outs, specs, scratch=(), flops=0, **kw):
    return pl.pallas_call(
        kernel,
        out_shape=outs,
        in_specs=specs,
        out_specs=[VMEM] * len(outs),
        scratch_shapes=list(scratch),
        compiler_params=pltpu.CompilerParams(vmem_limit_bytes=LIMIT),
        interpret=INTERPRET,
        **kw,
    )


def swap(block, axis, pairs):
    return lax.ppermute(block, axis, [(a, b) for a, b in pairs] + [(b, a) for a, b in pairs])


def per_device(
    atm_flux, remap_weights, intersection, tracers, east_speed, north_speed, mixing, level_count
):
    tiles, groups = lax.axis_size("cols"), lax.axis_size("rows")
    levels, height, width = east_speed.shape
    tall = -(-levels // 8) * 8
    sds = lambda *shape, dtype=F32: jax.ShapeDtypeStruct(shape, dtype)

    def from_ahead(block, distance):
        return lax.ppermute(block, "cols", [((i + distance) % tiles, i) for i in range(tiles)])

    cols0 = [(i, i + 1) for i in range(0, tiles, 2)]
    cols1 = [(i, (i + 1) % tiles) for i in range(1, tiles, 2)]
    rows0 = [(i, i + 1) for i in range(0, groups - 1, 2)]
    rows1 = [(i, i + 1) for i in range(1, groups - 1, 2)]

    place = jnp.stack([lax.axis_index("rows") % 2, lax.axis_index("cols") % 2]).astype(jnp.int32)
    index = intersection.reshape(-1)
    weights = remap_weights.reshape(height, -1, width)

    few = jnp.concatenate([atm_flux[:, 0, :], atm_flux[:, 1, :]], 0)
    slots = [tiles // 2 + s - 1 for s in range(3)]
    part = [from_ahead(few, d) for d in slots]
    whole = [from_ahead(atm_flux, d) for d in slots]

    plane = sds(levels, height, width)
    face_e, face_n, inv, low, ratio, first, go_e, go_w, go_n, go_s = call(
        prepare_kernel,
        [plane] * 5
        + [sds(2, height, width)] * 3
        + [sds(3, tall, width)] * 2,
        [VMEM] * 5,
    )(tracers, east_speed, north_speed, mixing, level_count)

    forced, c0, c1, r0, r1 = call(
        force_kernel,
        [sds(2, height, width)] * 3 + [sds(3, tall, width)] * 2,
        [SMEM, SMEM] + [VMEM] * 10,
        [
            pltpu.VMEM((3, 2 * atm_flux.shape[0], width), F32),
            pltpu.VMEM((8 * height, 3 * width), F32),
        ],
    )(place, index, *part, weights, level_count, first, go_e, go_w, go_n, go_s)

    def exchange(c0, c1, r0, r1):
        g0, g1 = swap(r0, "rows", rows0), swap(r1, "rows", rows1)
        return swap(c0, "cols", cols0), swap(c1, "cols", cols1), g0, g1

    c0, c1, r0, r1 = exchange(c0, c1, r0, r1)
    coefficients = (face_e, face_n, inv, low, ratio, level_count)
    field, p0, p1, u0, u1 = call(
        first_step_kernel,
        [sds(2, levels, height, width)] + [sds(height, width)] * 2 + [sds(2, tall, width)] * 2,
        [SMEM] + [VMEM] * 12,
        [pltpu.VMEM((2, levels, height, width), F32)],
    )(place, tracers, forced, *coefficients, c0, c1, r0, r1)
    p0, p1, u0, u1 = exchange(p0, p1, u0, u1)
    (result,) = call(
        second_step_kernel,
        [sds(2, levels, height, width)],
        [SMEM] + [VMEM] * 15,
        [pltpu.VMEM((2, levels, height, width), F32)],
    )(place, field, *coefficients, c0, c1, r0, r1, p0, p1, u0, u1)
    (ocean_flux,) = call(
        remap_kernel,
        [sds(atm_flux.shape[1], height, width)],
        [SMEM] + [VMEM] * 4,
    )(index, *whole, weights)
    return (ocean_flux, result)


def solution(mesh):
    placed = (
        P(("rows", "cols"), None, None),
        P("rows", None, None, "cols"),
        P("rows", "cols", None),
        P(None, None, "rows", "cols"),
        P(None, "rows", "cols"),
        P(None, "rows", "cols"),
        P(None, "rows", "cols"),
        P("rows", "cols"),
    )
    return jax.shard_map(
        per_device,
        mesh=mesh,
        in_specs=placed,
        out_specs=(P(None, "rows", "cols"), P(None, None, "rows", "cols")),
        check_vma=False,
    )
```

profile of v0, /device:TPU:1, one launch (start us, length us, event | category | flops | bytes accessed | tf_op | source)
XLA Modules:
  0.0 111.2 jit_solution(6465243900807008763)
XLA Ops:
  0.6 5.0 %collective-permute-start = (bf16[64,32,128]{2,1,0:T(8,128)(2,1)}, bf16[64,32,128]{2,1,0:T(8,128)(2,1)S(1)}, u32[]{:S(2)}, u32[]{:S(2)}) collective-permute-start(bf16[64,32,128]{2,1,0:T(8,128)(2,1)} %param.8), channel_id=1, source_target_pairs={{15,0},{16,1},{17,2},{18,3},{19,4},{20,5},{21,6},{22,7},{23,8},{24... | collective-permute-start | bytes 1572872 | tf_op jit(solution)/shard_map/ppermute | solution.py:237
  5.6 0.2 collective-permute-start.1
  5.9 4.7 %collective-permute-start.2 = (bf16[64,32,128]{2,1,0:T(8,128)(2,1)}, bf16[64,32,128]{2,1,0:T(8,128)(2,1)S(1)}, u32[]{:S(2)}, u32[]{:S(2)}) collective-permute-start(bf16[64,32,128]{2,1,0:T(8,128)(2,1)} %param.8), channel_id=1, source_target_pairs={{17,0},{18,1},{19,2},{20,3},{21,4},{22,5},{23,6},{24,7},{25,8},{26... | collective-permute-start | bytes 1572872 | tf_op jit(solution)/shard_map/ppermute | solution.py:237
  10.6 1.0 fusion
  11.6 0.1 collective-permute-start.3
  11.7 1.9 %collective-permute-start.4 = (bf16[128,128]{1,0:T(8,128)(2,1)S(1)}, bf16[128,128]{1,0:T(8,128)(2,1)S(1)}, u32[]{:S(2)}, u32[]{:S(2)}) collective-permute-start(bf16[128,128]{1,0:T(8,128)(2,1)S(1)} %pad_maximum_fusion), channel_id=1, source_target_pairs={{16,0},{17,1},{18,2},{19,3},{20,4},{21,5},{22,6},{23,7},{24,8},{25... | collective-permute-start | bytes 98312 | tf_op jit(solution)/shard_map/ppermute | solution.py:237
  13.6 14.8 %collective-permute-done.3.a0 = bf16[128,128]{1,0:T(8,128)(2,1)S(1)} collective-permute-done((bf16[128,128]{1,0:T(8,128)(2,1)S(1)}, bf16[128,128]{1,0:T(8,128)(2,1)S(1)}, u32[]{:S(2)}, u32[]{:S(2)}) %collective-permute-start.3) | collective-permute-done | bytes 32800 | tf_op jit(solution)/shard_map/ppermute | solution.py:237
  28.4 17.7 %collective-permute-start.5 = (bf16[128,128]{1,0:T(8,128)(2,1)S(1)}, bf16[128,128]{1,0:T(8,128)(2,1)S(1)}, u32[]{:S(2)}, u32[]{:S(2)}) collective-permute-start(bf16[128,128]{1,0:T(8,128)(2,1)S(1)} %pad_maximum_fusion), channel_id=1, source_target_pairs={{17,0},{18,1},{19,2},{20,3},{21,4},{22,5},{23,6},{24,7},{25,8},{26... | collective-permute-start | bytes 98312 | tf_op jit(solution)/shard_map/ppermute | solution.py:237
  46.0 0.1 pad_add_fusion.place
  46.1 0.8 copy.13
  46.9 0.1 reshape.10.index
  47.0 1.2 %copy-done.1 = f32[2,62,16,128]{3,2,1,0:T(8,128)S(1)} copy-done((f32[2,62,16,128]{3,2,1,0:T(8,128)S(1)}, f32[2,62,16,128]{3,2,1,0:T(8,128)}, u32[]{:S(2)}) %copy-start.1) | copy-done | bytes 1015832
  48.2 1.0 copy-done.3
  49.2 1.0 copy-done.4
  50.2 1.0 copy-done.5
  51.3 0.7 copy-done.6
  52.0 4.3 %shard_map.96 = (f32[62,16,128]{2,1,0:T(8,128)S(1)}, f32[62,16,128]{2,1,0:T(8,128)S(1)}, f32[62,16,128]{2,1,0:T(8,128)S(1)}, f32[62,16,128]{2,1,0:T(8,128)S(1)},...) custom-call(f32[2,62,16,128]{3,2,1,0:T(8,128)S(1)} %copy-done.1, ...), custom_call_target="tpu_custom_call" | custom-call | tf_op jit(solution)/shard_map/pallas_call | solution.py:254
  56.4 1.0 shard_map.97
  57.4 0.0 collective-permute-start.6
  57.5 2.6 %collective-permute-start.7 = (f32[2,16,128]{2,1,0:T(8,128)S(1)}, f32[2,16,128]{2,1,0:T(8,128)S(1)}, u32[]{:S(2)}, u32[]{:S(2)}) collective-permute-start(f32[2,16,128]{2,1,0:T(8,128)S(1)} %get-tuple-element.34), channel_id=1, source_target_pairs={{1,2},{3,4},{5,6},{7,8},{9,10},{11,12},{13,14},{15,16},{17,18},{19... | collective-permute-start | bytes 49160 | tf_op jit(solution)/shard_map/ppermute | solution.py:225
  60.1 3.6 %collective-permute-start.8 = (f32[3,64,128]{2,1,0:T(8,128)S(1)}, f32[3,64,128]{2,1,0:T(8,128)S(1)}, u32[]{:S(2)}, u32[]{:S(2)}) collective-permute-start(f32[3,64,128]{2,1,0:T(8,128)S(1)} %get-tuple-element.35), channel_id=1, source_target_pairs={{0,32},{64,96},{32,0},{96,64},{1,33},{65,97},{33,1},{97,65},{2,34}... | collective-permute-start | bytes 294920 | tf_op jit(solution)/shard_map/ppermute | solution.py:225
  63.7 2.2 %collective-permute-done.7.c1 = f32[2,16,128]{2,1,0:T(8,128)S(1)} collective-permute-done((f32[2,16,128]{2,1,0:T(8,128)S(1)}, f32[2,16,128]{2,1,0:T(8,128)S(1)}, u32[]{:S(2)}, u32[]{:S(2)}) %collective-permute-start.7) | collective-permute-done | bytes 16416 | tf_op jit(solution)/shard_map/ppermute | solution.py:225
  65.9 6.6 %collective-permute-start.9 = (f32[3,64,128]{2,1,0:T(8,128)S(1)}, f32[3,64,128]{2,1,0:T(8,128)S(1)}, u32[]{:S(2)}, u32[]{:S(2)}) collective-permute-start(f32[3,64,128]{2,1,0:T(8,128)S(1)} %get-tuple-element.36), channel_id=1, source_target_pairs={{32,64},{64,32},{33,65},{65,33},{34,66},{66,34},{35,67},{67,35},{3... | collective-permute-start | bytes 294920 | tf_op jit(solution)/shard_map/ppermute | solution.py:225
  72.5 2.3 %collective-permute-done.9.r1 = f32[3,64,128]{2,1,0:T(8,128)S(1)} collective-permute-done((f32[3,64,128]{2,1,0:T(8,128)S(1)}, f32[3,64,128]{2,1,0:T(8,128)S(1)}, u32[]{:S(2)}, u32[]{:S(2)}) %collective-permute-start.9) | collective-permute-done | bytes 98336 | tf_op jit(solution)/shard_map/ppermute | solution.py:225
  74.8 10.3 %shard_map.98 = (f32[2,62,16,128]{3,2,1,0:T(8,128)S(1)}, f32[16,128]{1,0:T(8,128)S(1)}, f32[16,128]{1,0:T(8,128)S(1)}, f32[2,64,128]{2,1,0:T(8,128)S(1)}, f32[2,64,128]{2,1,0:T(8,128)S(1)}) custom-call(s32[2]{0:T(128)S(1)} %pad_add_fusion.place, f32[2,62,16,128]{3,2,1,0:T(8,128)S(1)} %copy-done.2, f32[2,16,128]{2,1,0:T(8,128)S(1)} %get-tuple-element.27.forced, ...), custom_call_target="tpu_custom_call" | custom-call | tf_op jit(solution)/shard_map/pallas_call | solution.py:278
  85.1 0.1 collective-permute-start.10
  85.2 3.2 %collective-permute-start.11 = (f32[16,128]{1,0:T(8,128)S(1)}, f32[16,128]{1,0:T(8,128)S(1)}, u32[]{:S(2)}, u32[]{:S(2)}) collective-permute-start(f32[16,128]{1,0:T(8,128)S(1)} %get-tuple-element.39), channel_id=1, source_target_pairs={{1,2},{3,4},{5,6},{7,8},{9,10},{11,12},{13,14},{15,16},{17,18},{19... | collective-permute-start | bytes 24584 | tf_op jit(solution)/shard_map/ppermute | solution.py:225
  88.4 5.1 %collective-permute-done.11.p1 = f32[16,128]{1,0:T(8,128)S(1)} collective-permute-done((f32[16,128]{1,0:T(8,128)S(1)}, f32[16,128]{1,0:T(8,128)S(1)}, u32[]{:S(2)}, u32[]{:S(2)}) %collective-permute-start.11) | collective-permute-done | bytes 8224 | tf_op jit(solution)/shard_map/ppermute | solution.py:225
  93.5 4.8 %collective-permute-start.13 = (f32[2,64,128]{2,1,0:T(8,128)S(1)}, f32[2,64,128]{2,1,0:T(8,128)S(1)}, u32[]{:S(2)}, u32[]{:S(2)}) collective-permute-start(f32[2,64,128]{2,1,0:T(8,128)S(1)} %get-tuple-element.41), channel_id=1, source_target_pairs={{32,64},{64,32},{33,65},{65,33},{34,66},{66,34},{35,67},{67,35},{3... | collective-permute-start | bytes 196616 | tf_op jit(solution)/shard_map/ppermute | solution.py:225
  98.3 1.9 %collective-permute-done.13.u1 = f32[2,64,128]{2,1,0:T(8,128)S(1)} collective-permute-done((f32[2,64,128]{2,1,0:T(8,128)S(1)}, f32[2,64,128]{2,1,0:T(8,128)S(1)}, u32[]{:S(2)}, u32[]{:S(2)}) %collective-permute-start.13) | collective-permute-done | bytes 65568 | tf_op jit(solution)/shard_map/ppermute | solution.py:225
  100.2 9.3 %shard_map.99 = f32[2,62,16,128]{3,2,1,0:T(8,128)} custom-call(s32[2]{0:T(128)S(1)} %pad_add_fusion.place, f32[2,62,16,128]{3,2,1,0:T(8,128)S(1)} %get-tuple-element.37.field, f32[62,16,128]{2,1,0:T(8,128)S(1)} %get-tuple-element.28.face_e, f32[62,16,128]{2,1,0:T(8,128)S(1)} %get-tuple-element.29.face_n, f32[62,16,128]{2,1,0:T(8,128)S(1)} %get-tuple-element.30.inv, ...), custom_call_target="tpu_custom_call" | custom-call | tf_op jit(solution)/shard_map/pallas_call | solution.py:285
  109.6 1.7 %shard_map.95 = f32[32,16,128]{2,1,0:T(8,128)} custom-call(s32[48]{0:T(128)S(1)} %reshape.10.index, bf16[64,32,128]{2,1,0:T(8,128)(2,1)S(1)} %collective-permute-done.a0, bf16[64,32,128]{2,1,0:T(8,128)(2,1)S(1)} %collective-permute-done.1.a1, bf16[64,32,128]{2,1,0:T(8,128)(2,1)S(1)} %collective-permute-done.2.a2, bf16[16,384,128]{2,1,0:T(8,128)(2,1)S(1)} %bitcast.10), custom_call_target="tpu_custom_call" | custom-call | tf_op jit(solution)/shard_map/pallas_call | solution.py:291
  (23 shorter events, 0.1 us)
Async XLA Ops:
  0.6 55.7 %copy-start = (bf16[16,3,128,128]{3,2,1,0:T(8,128)(2,1)S(1)}, bf16[16,3,128,128]{3,2,1,0:T(8,128)(2,1)}, u32[]{:S(2)}) copy-start(bf16[16,3,128,128]{3,2,1,0:T(8,128)(2,1)} %param.9) | copy-start | bytes 4718596
  0.6 108.9 %collective-permute-start = (bf16[64,32,128]{2,1,0:T(8,128)(2,1)}, bf16[64,32,128]{2,1,0:T(8,128)(2,1)S(1)}, u32[]{:S(2)}, u32[]{:S(2)}) collective-permute-start(bf16[64,32,128]{2,1,0:T(8,128)(2,1)} %param.8), channel_id=1, source_target_pairs={{15,0},{16,1},{17,2},{18,3},{19,4},{20,5},{21,6},{22,7},{23,8},{24... | collective-permute-start | bytes 1572872 | tf_op jit(solution)/shard_map/ppermute | solution.py:237
  5.6 103.9 %collective-permute-start.1 = (bf16[64,32,128]{2,1,0:T(8,128)(2,1)}, bf16[64,32,128]{2,1,0:T(8,128)(2,1)S(1)}, u32[]{:S(2)}, u32[]{:S(2)}) collective-permute-start(bf16[64,32,128]{2,1,0:T(8,128)(2,1)} %param.8), channel_id=1, source_target_pairs={{16,0},{17,1},{18,2},{19,3},{20,4},{21,5},{22,6},{23,7},{24,8},{25... | collective-permute-start | bytes 1572872 | tf_op jit(solution)/shard_map/ppermute | solution.py:237
  5.9 103.7 %collective-permute-start.2 = (bf16[64,32,128]{2,1,0:T(8,128)(2,1)}, bf16[64,32,128]{2,1,0:T(8,128)(2,1)S(1)}, u32[]{:S(2)}, u32[]{:S(2)}) collective-permute-start(bf16[64,32,128]{2,1,0:T(8,128)(2,1)} %param.8), channel_id=1, source_target_pairs={{17,0},{18,1},{19,2},{20,3},{21,4},{22,5},{23,6},{24,7},{25,8},{26... | collective-permute-start | bytes 1572872 | tf_op jit(solution)/shard_map/ppermute | solution.py:237
  11.6 16.7 %collective-permute-start.3 = (bf16[128,128]{1,0:T(8,128)(2,1)S(1)}, bf16[128,128]{1,0:T(8,128)(2,1)S(1)}, u32[]{:S(2)}, u32[]{:S(2)}) collective-permute-start(bf16[128,128]{1,0:T(8,128)(2,1)S(1)} %pad_maximum_fusion), channel_id=1, source_target_pairs={{15,0},{16,1},{17,2},{18,3},{19,4},{20,5},{21,6},{22,7},{23,8},{24... | collective-permute-start | bytes 98312 | tf_op jit(solution)/shard_map/ppermute | solution.py:237
  11.7 44.6 %collective-permute-start.4 = (bf16[128,128]{1,0:T(8,128)(2,1)S(1)}, bf16[128,128]{1,0:T(8,128)(2,1)S(1)}, u32[]{:S(2)}, u32[]{:S(2)}) collective-permute-start(bf16[128,128]{1,0:T(8,128)(2,1)S(1)} %pad_maximum_fusion), channel_id=1, source_target_pairs={{16,0},{17,1},{18,2},{19,3},{20,4},{21,5},{22,6},{23,7},{24,8},{25... | collective-permute-start | bytes 98312 | tf_op jit(solution)/shard_map/ppermute | solution.py:237
  28.4 28.0 %collective-permute-start.5 = (bf16[128,128]{1,0:T(8,128)(2,1)S(1)}, bf16[128,128]{1,0:T(8,128)(2,1)S(1)}, u32[]{:S(2)}, u32[]{:S(2)}) collective-permute-start(bf16[128,128]{1,0:T(8,128)(2,1)S(1)} %pad_maximum_fusion), channel_id=1, source_target_pairs={{17,0},{18,1},{19,2},{20,3},{21,4},{22,5},{23,6},{24,7},{25,8},{26... | collective-permute-start | bytes 98312 | tf_op jit(solution)/shard_map/ppermute | solution.py:237
  47.0 1.2 %copy-start.1 = (f32[2,62,16,128]{3,2,1,0:T(8,128)S(1)}, f32[2,62,16,128]{3,2,1,0:T(8,128)}, u32[]{:S(2)}) copy-start(f32[2,62,16,128]{3,2,1,0:T(8,128)} %tracers.3) | copy-start | bytes 3047428
  48.2 1.0 copy-start.3
  49.2 1.0 copy-start.4
  50.2 1.0 copy-start.5
  51.3 0.7 copy-start.6
  52.0 4.4 %copy-start.7 = (s32[16,128]{1,0:T(8,128)S(1)}, s32[16,128]{1,0:T(8,128)}, u32[]{:S(2)}) copy-start(s32[16,128]{1,0:T(8,128)} %count.7) | copy-start | bytes 24580
  56.3 18.4 %copy-start.2 = (f32[2,62,16,128]{3,2,1,0:T(8,128)S(1)}, f32[2,62,16,128]{3,2,1,0:T(8,128)}, u32[]{:S(2)}) copy-start(f32[2,62,16,128]{3,2,1,0:T(8,128)} %tracers.3) | copy-start | bytes 3047428
  57.4 2.7 %collective-permute-start.6 = (f32[2,16,128]{2,1,0:T(8,128)S(1)}, f32[2,16,128]{2,1,0:T(8,128)S(1)}, u32[]{:S(2)}, u32[]{:S(2)}) collective-permute-start(f32[2,16,128]{2,1,0:T(8,128)S(1)} %get-tuple-element.33), channel_id=1, source_target_pairs={{0,1},{2,3},{4,5},{6,7},{8,9},{10,11},{12,13},{14,15},{16,17},{18,... | collective-permute-start | bytes 49160 | tf_op jit(solution)/shard_map/ppermute | solution.py:225
  57.5 8.4 %collective-permute-start.7 = (f32[2,16,128]{2,1,0:T(8,128)S(1)}, f32[2,16,128]{2,1,0:T(8,128)S(1)}, u32[]{:S(2)}, u32[]{:S(2)}) collective-permute-start(f32[2,16,128]{2,1,0:T(8,128)S(1)} %get-tuple-element.34), channel_id=1, source_target_pairs={{1,2},{3,4},{5,6},{7,8},{9,10},{11,12},{13,14},{15,16},{17,18},{19... | collective-permute-start | bytes 49160 | tf_op jit(solution)/shard_map/ppermute | solution.py:225
  60.1 12.4 %collective-permute-start.8 = (f32[3,64,128]{2,1,0:T(8,128)S(1)}, f32[3,64,128]{2,1,0:T(8,128)S(1)}, u32[]{:S(2)}, u32[]{:S(2)}) collective-permute-start(f32[3,64,128]{2,1,0:T(8,128)S(1)} %get-tuple-element.35), channel_id=1, source_target_pairs={{0,32},{64,96},{32,0},{96,64},{1,33},{65,97},{33,1},{97,65},{2,34}... | collective-permute-start | bytes 294920 | tf_op jit(solution)/shard_map/ppermute | solution.py:225
  65.9 8.9 %collective-permute-start.9 = (f32[3,64,128]{2,1,0:T(8,128)S(1)}, f32[3,64,128]{2,1,0:T(8,128)S(1)}, u32[]{:S(2)}, u32[]{:S(2)}) collective-permute-start(f32[3,64,128]{2,1,0:T(8,128)S(1)} %get-tuple-element.36), channel_id=1, source_target_pairs={{32,64},{64,32},{33,65},{65,33},{34,66},{66,34},{35,67},{67,35},{3... | collective-permute-start | bytes 294920 | tf_op jit(solution)/shard_map/ppermute | solution.py:225
  85.1 3.3 %collective-permute-start.10 = (f32[16,128]{1,0:T(8,128)S(1)}, f32[16,128]{1,0:T(8,128)S(1)}, u32[]{:S(2)}, u32[]{:S(2)}) collective-permute-start(f32[16,128]{1,0:T(8,128)S(1)} %get-tuple-element.38), channel_id=1, source_target_pairs={{0,1},{2,3},{4,5},{6,7},{8,9},{10,11},{12,13},{14,15},{16,17},{18,... | collective-permute-start | bytes 24584 | tf_op jit(solution)/shard_map/ppermute | solution.py:225
  85.2 8.3 %collective-permute-start.11 = (f32[16,128]{1,0:T(8,128)S(1)}, f32[16,128]{1,0:T(8,128)S(1)}, u32[]{:S(2)}, u32[]{:S(2)}) collective-permute-start(f32[16,128]{1,0:T(8,128)S(1)} %get-tuple-element.39), channel_id=1, source_target_pairs={{1,2},{3,4},{5,6},{7,8},{9,10},{11,12},{13,14},{15,16},{17,18},{19... | collective-permute-start | bytes 24584 | tf_op jit(solution)/shard_map/ppermute | solution.py:225
  88.4 9.9 %collective-permute-start.12 = (f32[2,64,128]{2,1,0:T(8,128)S(1)}, f32[2,64,128]{2,1,0:T(8,128)S(1)}, u32[]{:S(2)}, u32[]{:S(2)}) collective-permute-start(f32[2,64,128]{2,1,0:T(8,128)S(1)} %get-tuple-element.40), channel_id=1, source_target_pairs={{0,32},{64,96},{32,0},{96,64},{1,33},{65,97},{33,1},{97,65},{2,34}... | collective-permute-start | bytes 196616 | tf_op jit(solution)/shard_map/ppermute | solution.py:225
  93.5 6.7 %collective-permute-start.13 = (f32[2,64,128]{2,1,0:T(8,128)S(1)}, f32[2,64,128]{2,1,0:T(8,128)S(1)}, u32[]{:S(2)}, u32[]{:S(2)}) collective-permute-start(f32[2,64,128]{2,1,0:T(8,128)S(1)} %get-tuple-element.41), channel_id=1, source_target_pairs={{32,64},{64,32},{33,65},{65,33},{34,66},{66,34},{35,67},{67,35},{3... | collective-permute-start | bytes 196616 | tf_op jit(solution)/shard_map/ppermute | solution.py:225
where the time goes:
time: 112 us; the launch traced here: 111 us
  starting transfers between devices  50.5 us (45%)
  Pallas kernels  26.7 us (24%)
  waiting for transfers between devices  26.3 us (23%)
  local copies, waits for them, and re-layouts  6.9 us (6%)
    ppermute x6, starting transfers between devices, from_ahead(): lax.ppermute(block, 'cols', [((i + distance) % tiles, i) for i in range(t...  29.5 us
    ppermute x8, starting transfers between devices, swap(): lax.ppermute(block, axis, [(a, b) for a, b in pairs] + [(b, a) for a, b i...  20.9 us
    ppermute x6, waiting for transfers between devices, from_ahead(): lax.ppermute(block, 'cols', [((i + distance) % tiles, i) for i in range(t...  14.8 us
    ppermute x8, waiting for transfers between devices, swap(): lax.ppermute(block, axis, [(a, b) for a, b in pairs] + [(b, a) for a, b i...  11.5 us
    pallas_call x1, Pallas kernels, per_device(): call(first_step_kernel, [sds(2, levels, height, width)] + [sds(height, wi...  10.3 us
    pallas_call x1, Pallas kernels, per_device(): call(second_step_kernel, [sds(2, levels, height, width)], [SMEM] + [VMEM]...  9.34 us
    unnamed x17, local copies, waits for them, and re-layouts  5.78 us
    pallas_call x1, Pallas kernels, per_device(): call(prepare_kernel, [plane] * 5 + [sds(2, height, width)] * 3 + [sds(3,...  4.34 us
  transfers between devices with their start and end apart: 14, of which 5 were waited for; matrix products, arithmetic and copies ran while one was open for 2% of the time, Pallas kernels for 23%

commit v1 on v0

v1 whole, which is shorter than its diff:
```python
import jax
import jax.numpy as jnp
from jax import lax
from jax.experimental import pallas as pl
from jax.experimental.pallas import tpu as pltpu
from jax.sharding import PartitionSpec as P

F32 = jnp.float32
BF16 = jnp.bfloat16
VMEM = pl.BlockSpec(memory_space=pltpu.VMEM)
ANY = pl.BlockSpec(memory_space=pl.ANY)
SMEM = pl.BlockSpec(memory_space=pltpu.SMEM)
LIMIT = 24 * 1024 * 1024


def lanes(shape):
    return lax.broadcasted_iota(jnp.int32, shape, len(shape) - 1)


def sublanes(shape):
    return lax.broadcasted_iota(jnp.int32, shape, len(shape) - 2)


def turn(x, shift):
    shift = shift % x.shape[-1]
    return x if shift == 0 else pltpu.roll(x, shift, x.ndim - 1)


def pack_kernel(tracers, east, north, count, first, tile, tops, bottoms):
    levels, height, width = east.shape
    lane = lanes((height, width))
    depth = count[...]
    packed = [jnp.zeros((height, width), F32) for _ in range(3)]
    for k in range(levels):
        here = (lane >> 1) == k
        for t in range(2):
            x = tracers[t, k]
            packed[t] = jnp.where(here, turn(x, 2 * k + 1), packed[t])
            tops[t, k : k + 1, :] = x[height - 1 :, :]
            bottoms[t, k : k + 1, :] = x[:1, :]
        packed[2] = jnp.where(here, turn(east[k], 2 * k + 1), packed[2])
        tops[2, k : k + 1, :] = north[k, height - 1 :, :]
    for t in range(2):
        first[t] = tracers[t, 0]
        tile[t] = packed[t]
    spare = tops.shape[1] - levels
    for t in range(3):
        tops[t, levels:, :] = jnp.zeros((spare, width), F32)
    for t in range(2):
        bottoms[t, levels:, :] = jnp.zeros((spare, width), F32)
    even = (lane & 1) == 0
    wet_last = jnp.where((lane >> 1) < depth[:, width - 1 :], 1.0, 0.0)
    wet_first = jnp.where((lane >> 1) < depth[:, :1], 1.0, 0.0)
    tile[2] = jnp.where(even, packed[2] * wet_last, wet_first)
    tall = sublanes(tops.shape[1:])
    tops[2] = tops[2] * jnp.where(tall < depth[height - 1 :, :], 1.0, 0.0)
    bottoms[2] = jnp.where(tall < depth[:1, :], 1.0, 0.0)


def solver_kernel(after, east, north, mixing, count, face_e, face_w, face_n, face_s, inv, low, ratio):
    levels, height, width = east.shape
    lane, row = lanes((height, width)), sublanes((height, width))
    depth = count[...]
    depth_e = jnp.where(lane == width - 1, levels, turn(depth, -1))
    depth_n = jnp.where(row == height - 1, levels, pltpu.roll(depth, height - 1, 0))
    depth_e = jnp.minimum(depth, depth_e)
    depth_n = jnp.minimum(depth, depth_n)
    a_prev = r_prev = jnp.zeros((height, width), F32)
    for k in range(levels):
        ce = jnp.where(depth_e > k, east[k], 0.0)
        cn = jnp.where(depth_n > k, north[k], 0.0)
        face_e[k] = ce
        face_w[k] = turn(ce, 1)
        face_n[k] = cn
        face_s[k] = pltpu.roll(cn, 1, 0)
        a = jnp.where(depth > k + 1, mixing[k], 0.0) if k + 1 < levels else jnp.zeros((height, width), F32)
        iv = 1.0 / (1.0 + a_prev + a - a_prev * r_prev)
        inv[k] = iv
        low[k] = a_prev * iv
        r_prev = a * iv
        ratio[k] = r_prev
        a_prev = a


def force_kernel(
    place, index, a0, a1, a2, weights, count, first, tile, tops, bottoms,
    forced, sent, out_r0, out_r1, held, picked,
):
    height, width = count.shape
    blocks = held.shape[1] // 2
    for s, a in enumerate((a0, a1, a2)):
        held[s] = a[: 2 * blocks].astype(F32)
    for y in range(height):
        for s in range(3):
            b = lax.rem(index[3 * y + s], blocks)
            for f in range(2):
                picked[8 * y + f : 8 * y + f + 1, s * 128 : (s + 1) * 128] = held[
                    s, pl.ds(b + f * blocks, 1), :
                ]
    wet = jnp.where(count[...] > 0, 0.5, 0.0)
    for y in range(height):
        got = jnp.dot(
            picked[8 * y : 8 * y + 8].astype(BF16), weights[y], preferred_element_type=F32
        )
        for f in range(2):
            forced[f, y : y + 1, :] = got[f : f + 1, :]
    here = lanes((height, width)) < 2
    even = place[0] == 0
    out_r0[...] = jnp.where(even, tops[...], bottoms[...])
    out_r1[...] = jnp.where(even, bottoms[...], tops[...])
    sent[2] = tile[2]
    for t in range(2):
        x = first[t] + wet * forced[t]
        forced[t] = x
        sent[t] = jnp.where(here, turn(x, 1), tile[t])
        top, bottom = x[height - 1 :, :], x[:1, :]
        out_r0[t, :1, :] = jnp.where(even, top, bottom)
        out_r1[t, :1, :] = jnp.where(even, bottom, top)


def step(place, field, level0, face_e, face_w, face_n, face_s, inv, low, ratio,
         own_c, got_c, own_r, got_r, coef_c, coef_r, solved, edge_n, edge_s, out, messages):
    levels, height, width = face_e.shape
    lane, row = lanes((height, width)), sublanes((height, width))
    even_r, even_c = place[0] == 0, place[1] == 0
    even = (lane & 1) == 0

    def facing(own, pair):
        a, b = pair
        from_e, from_w = jnp.where(even_c, a, b), jnp.where(even_c, b, a)
        theirs = jnp.where(even, from_w, from_e)
        mine = jnp.where(even, turn(own, -1), turn(own, 1))
        return theirs, mine

    c_theirs, c_mine = facing(*coef_c)
    c = c_theirs * c_mine
    edges = []
    for t in range(2):
        theirs, mine = facing(own_c[t], (got_c[0][t], got_c[1][t]))
        flux = c * jnp.where((c > 0) == even, theirs, mine)
        edges.append(jnp.where(even, flux, turn(flux, -2)))

    def row_pair(a, b):
        return jnp.where(even_r, a, b), jnp.where(even_r, b, a)

    own_n, own_s = row_pair(coef_r[0][...], coef_r[1][...])
    from_n, from_s = row_pair(coef_r[2][...], coef_r[3][...])
    cn_row, cs_row = own_n * from_n, own_s * from_s
    for t in range(2):
        own_n, own_s = row_pair(own_r[0][t], own_r[1][t])
        from_n, from_s = row_pair(got_r[0][t], got_r[1][t])
        edge_n[t] = cn_row * jnp.where(cn_row > 0, own_n, from_n)
        edge_s[t] = cs_row * jnp.where(cs_row > 0, from_s, own_s)

    east_end, west_end = lane == width - 1, lane == 0
    north_end, south_end = row == height - 1, row == 0
    value = [None, None]
    for k in range(levels):
        ce, cw, cn, cs = face_e[k], face_w[k], face_n[k], face_s[k]
        for t in range(2):
            x = level0[t] if (k == 0 and level0 is not None) else field[t, k]
            edge = turn(edges[t], -2 * k)
            fe = jnp.where(east_end, edge, ce * jnp.where(ce > 0, x, turn(x, -1)))
            fw = jnp.where(west_end, edge, cw * jnp.where(cw > 0, turn(x, 1), x))
            fn = cn * jnp.where(cn > 0, x, pltpu.roll(x, height - 1, 0))
            fn = jnp.where(north_end, edge_n[t, k : k + 1, :], fn)
            fs = cs * jnp.where(cs > 0, pltpu.roll(x, 1, 0), x)
            fs = jnp.where(south_end, edge_s[t, k : k + 1, :], fs)
            now = (x - (fe - fw) - (fn - fs)) * inv[k]
            if k:
                now = now + low[k] * value[t]
            value[t] = now
            solved[t, k] = now
    packed = [jnp.zeros((height, width), F32)] * 2
    for k in range(levels - 1, -1, -1):
        for t in range(2):
            if k < levels - 1:
                value[t] = solved[t, k] + ratio[k] * value[t]
            y = value[t]
            out[t, k] = y
            if messages is not None:
                packed[t] = jnp.where((lane >> 1) == k, turn(y, 2 * k + 1), packed[t])
                top, bottom = y[height - 1 :, :], y[:1, :]
                messages[1][t, k : k + 1, :] = jnp.where(even_r, top, bottom)
                messages[2][t, k : k + 1, :] = jnp.where(even_r, bottom, top)
    if messages is not None:
        spare = messages[1].shape[1] - levels
        for t in range(2):
            messages[0][t] = packed[t]
            messages[1][t, levels:, :] = jnp.zeros((spare, width), F32)
            messages[2][t, levels:, :] = jnp.zeros((spare, width), F32)


def first_step_kernel(
    place, tracers, forced, face_e, face_w, face_n, face_s, inv, low, ratio,
    c, c0, c1, r0, r1, g0, g1, out, out_c, out_r0, out_r1, solved, edge_n, edge_s,
):
    step(place, tracers, forced, face_e, face_w, face_n, face_s, inv, low, ratio,
         c, (c0, c1), (r0, r1), (g0, g1), (c[2], (c0[2], c1[2])),
         (r0.at[2], r1.at[2], g0.at[2], g1.at[2]), solved, edge_n, edge_s, out, (out_c, out_r0, out_r1))


def second_step_kernel(
    place, field, face_e, face_w, face_n, face_s, inv, low, ratio,
    c, c0, c1, r0, r1, g0, g1, d, d0, d1, u0, u1, h0, h1, out, solved, edge_n, edge_s,
):
    step(place, field, None, face_e, face_w, face_n, face_s, inv, low, ratio,
         d, (d0, d1), (u0, u1), (h0, h1), (c[2], (c0[2], c1[2])),
         (r0.at[2], r1.at[2], g0.at[2], g1.at[2]), solved, edge_n, edge_s, out, None)


def gather_kernel(after, wanted, atm, out0, out1, out2):
    for s, out in enumerate((out0, out1, out2)):
        for y in range(out.shape[0]):
            out[y] = atm[wanted[s * out.shape[0] + y]]


def remap_kernel(a0, a1, a2, weights, out):
    for y in range(out.shape[1]):
        picked = jnp.concatenate([a0[y], a1[y], a2[y]], 1)
        out[:, y, :] = jnp.dot(picked, weights[y], preferred_element_type=F32)


def call(kernel, outs, specs, scratch=(), cost=1):
    return pl.pallas_call(
        kernel,
        out_shape=outs,
        in_specs=specs,
        out_specs=[VMEM] * len(outs),
        scratch_shapes=list(scratch),
        compiler_params=pltpu.CompilerParams(vmem_limit_bytes=LIMIT),
        cost_estimate=pl.CostEstimate(flops=0, bytes_accessed=cost * 3000000, transcendentals=0),
    )


def swap(block, axis, pairs):
    return lax.ppermute(block, axis, [(a, b) for a, b in pairs] + [(b, a) for a, b in pairs])


def per_device(
    atm_flux, remap_weights, intersection, tracers, east_speed, north_speed, mixing, level_count
):
    tiles, groups = lax.axis_size("cols"), lax.axis_size("rows")
    levels, height, width = east_speed.shape
    tall = -(-levels // 8) * 8
    sds = lambda *shape, dtype=F32: jax.ShapeDtypeStruct(shape, dtype)

    def from_ahead(block, distance):
        return lax.ppermute(block, "cols", [((i + distance) % tiles, i) for i in range(tiles)])

    cols0 = [(i, i + 1) for i in range(0, tiles, 2)]
    cols1 = [(i, (i + 1) % tiles) for i in range(1, tiles, 2)]
    rows0 = [(i, i + 1) for i in range(0, groups - 1, 2)]
    rows1 = [(i, i + 1) for i in range(1, groups - 1, 2)]

    place = jnp.stack([lax.axis_index("rows") % 2, lax.axis_index("cols") % 2]).astype(jnp.int32)
    weights = remap_weights.reshape(height, -1, width)

    blocks, fields = atm_flux.shape[:2]
    within = intersection[:, 0, :] % blocks
    asked = jnp.broadcast_to(within.T.reshape(-1, 1), (3 * height, width)).astype(BF16)
    few = jnp.concatenate([atm_flux[:, 0, :], atm_flux[:, 1, :], asked], 0)
    slots = [tiles // 2 + s - 1 for s in range(3)]
    part = [from_ahead(few, d) for d in slots]

    plane = sds(levels, height, width)
    first, tile, tops, bottoms = call(
        pack_kernel,
        [sds(2, height, width), sds(3, height, width)] + [sds(3, tall, width)] * 2,
        [VMEM] * 4,
        cost=2,
    )(tracers, east_speed, north_speed, level_count)

    forced, c, r0, r1 = call(
        force_kernel,
        [sds(2, height, width), sds(3, height, width)] + [sds(3, tall, width)] * 2,
        [SMEM, SMEM] + [VMEM] * 9,
        [pltpu.VMEM((3, 2 * blocks, width), F32), pltpu.VMEM((8 * height, 3 * width), F32)],
        cost=1,
    )(place, within.reshape(-1), *part, weights, level_count, first, tile, tops, bottoms)

    def exchange(c, r0, r1):
        g0, g1 = swap(r0, "rows", rows0), swap(r1, "rows", rows1)
        return swap(c, "cols", cols0), swap(c, "cols", cols1), g0, g1

    c0, c1, g0, g1 = exchange(c, r0, r1)
    coefficients = call(solver_kernel, [plane] * 7, [ANY] + [VMEM] * 4, cost=4)(
        g0, east_speed, north_speed, mixing, level_count
    )
    wanted = jnp.concatenate(
        [part[s][2 * blocks + (2 - s) * height :][:height, 0] for s in range(3)]
    ).astype(jnp.int32)
    found = call(
        gather_kernel,
        [sds(height, fields, width, dtype=BF16)] * 3,
        [ANY, SMEM, VMEM],
        cost=1,
    )(g1, wanted, atm_flux)
    blocks_of = [from_ahead(found[2 - s], slots[s]) for s in range(3)]

    scratch = [pltpu.VMEM((2, levels, height, width), F32)] + [pltpu.VMEM((2, tall, width), F32)] * 2
    field, d, u0, u1 = call(
        first_step_kernel,
        [sds(2, levels, height, width), sds(2, height, width)] + [sds(2, tall, width)] * 2,
        [SMEM] + [VMEM] * 16,
        scratch,
        cost=4,
    )(place, tracers, forced, *coefficients, c, c0, c1, r0, r1, g0, g1)
    d0, d1, h0, h1 = exchange(d, u0, u1)
    (ocean_flux,) = call(remap_kernel, [sds(fields, height, width)], [VMEM] * 4, cost=2)(
        *blocks_of, weights
    )
    (result,) = call(
        second_step_kernel,
        [sds(2, levels, height, width)],
        [SMEM] + [VMEM] * 22,
        scratch,
        cost=3,
    )(place, field, *coefficients, c, c0, c1, r0, r1, g0, g1, d, d0, d1, u0, u1, h0, h1)
    return (ocean_flux, result)


def solution(mesh):
    placed = (
        P(("rows", "cols"), None, None),
        P("rows", None, None, "cols"),
        P("rows", "cols", None),
        P(None, None, "rows", "cols"),
        P(None, "rows", "cols"),
        P(None, "rows", "cols"),
        P(None, "rows", "cols"),
        P("rows", "cols"),
    )
    return jax.shard_map(
        per_device,
        mesh=mesh,
        in_specs=placed,
        out_specs=(P(None, "rows", "cols"), P(None, None, "rows", "cols")),
        check_vma=False,
    )
```

time: 112 us -> 63.8 us (0.57)
  Pallas kernels: 26.7 us -> 8.47 us
  waiting for transfers between devices: 26.3 us -> 10.4 us
  starting transfers between devices: 50.5 us -> 36.4 us
    ppermute x6, waiting for transfers between devices: 14.8 us -> 0.02 us  [from_ahead(): lax.ppermute(block, 'cols', [((i + distance) % tiles, i) for i in range(t...]
    ppermute x6, starting transfers between devices: 29.5 us -> 14.9 us  [from_ahead(): lax.ppermute(block, 'cols', [((i + distance) % tiles, i) for i in range(t...]
    pallas_call x4 -> x6, Pallas kernels: 17.3 us -> 5.81 us  [the longest x1 1.95 us: per_device(): call(first_step_kernel, [sds(2, levels, height, width), sds(2, height, wi...]
    pallas_call x1, Pallas kernels: 9.34 us -> 2.67 us  [per_device(): call(second_step_kernel, [sds(2, levels, height, width)], [SMEM] + [VMEM]...]
    ppermute x8, waiting for transfers between devices: 11.5 us -> 10.4 us  [swap(): lax.ppermute(block, axis, [(a, b) for a, b in pairs] + [(b, a) for a, b i...]
    unnamed x17 -> x23, local copies, waits for them, and re-layouts: 5.78 us -> 4.77 us
  transfers between devices with their start and end apart: 14 -> 14, of which waited for: 5 -> 4; matrix products, arithmetic and copies ran while one was open for 2% -> 2% of each run, Pallas kernels for 23% -> 10%
where the time goes in v1:
time: 63.8 us; the launch traced here: 63.5 us
  starting transfers between devices  36.4 us (57%)
  waiting for transfers between devices  10.4 us (16%)
  Pallas kernels  8.47 us (13%)
  local copies, waits for them, and re-layouts  6.45 us (10%)
  other arithmetic  0.94 us (1%)
  between operations  0.84 us (1%)
    ppermute x8, starting transfers between devices, swap(): lax.ppermute(block, axis, [(a, b) for a, b in pairs] + [(b, a) for a, b i...  21.4 us
    ppermute x6, starting transfers between devices, from_ahead(): lax.ppermute(block, 'cols', [((i + distance) % tiles, i) for i in range(t...  14.9 us
    ppermute x8, waiting for transfers between devices, swap(): lax.ppermute(block, axis, [(a, b) for a, b in pairs] + [(b, a) for a, b i...  10.4 us
    unnamed x23, local copies, waits for them, and re-layouts  4.77 us
    pallas_call x1, Pallas kernels, per_device(): call(second_step_kernel, [sds(2, levels, height, width)], [SMEM] + [VMEM]...  2.67 us
    pallas_call x1, Pallas kernels, per_device(): call(first_step_kernel, [sds(2, levels, height, width), sds(2, height, wi...  1.95 us
  transfers between devices with their start and end apart: 14, of which 4 were waited for; matrix products, arithmetic and copies ran while one was open for 2% of the time, Pallas kernels for 10%

profile of v1, /device:TPU:1, one launch (start us, length us, event | category | flops | bytes accessed | tf_op | source)
XLA Modules:
  0.0 63.5 jit_solution(17072117210031688500)
XLA Ops:
  0.6 1.1 %fusion.4 = (bf16[64,1,128]{2,1,0:T(2,128)(2,1)S(1)}, bf16[64,1,128]{2,1,0:T(2,128)(2,1)S(1)}) fusion(bf16[64,32,128]{2,1,0:T(8,128)(2,1)} %atm.1), kind=kLoop, calls=%fused_computation.18 | loop fusion | bytes 65536 | tf_op jit(solution)/shard_map/slice | solution.py:262
  1.8 0.7 %fusion.2 = bf16[3,16]{1,0:T(4,128)(2,1)S(1)} fusion(s32[16,1,3]{0,1,2:T(1,128)} %param.10), kind=kLoop, calls=%fused_computation.14 | loop fusion | flops 576 | bytes 288 | tf_op jit(solution)/shard_map/convert_element_type | solution.py:261
  2.6 0.1 maximum_maximum_fusion
  2.7 5.0 %collective-permute-start = (bf16[176,128]{1,0:T(8,128)(2,1)S(1)}, bf16[176,128]{1,0:T(8,128)(2,1)S(1)}, u32[]{:S(2)}, u32[]{:S(2)}) collective-permute-start(bf16[176,128]{1,0:T(8,128)(2,1)S(1)} %maximum_maximum_fusion), channel_id=1, source_target_pairs={{15,0},{16,1},{17,2},{18,3},{19,4},{20,5},{21,6},{22,7},{23,8},{24... | collective-permute-start | bytes 135176 | tf_op jit(solution)/shard_map/ppermute | solution.py:249
  7.7 0.2 collective-permute-start.1
  7.9 4.7 %collective-permute-start.2 = (bf16[176,128]{1,0:T(8,128)(2,1)S(1)}, bf16[176,128]{1,0:T(8,128)(2,1)S(1)}, u32[]{:S(2)}, u32[]{:S(2)}) collective-permute-start(bf16[176,128]{1,0:T(8,128)(2,1)S(1)} %maximum_maximum_fusion), channel_id=1, source_target_pairs={{17,0},{18,1},{19,2},{20,3},{21,4},{22,5},{23,6},{24,7},{25,8},{26... | collective-permute-start | bytes 135176 | tf_op jit(solution)/shard_map/ppermute | solution.py:249
  12.6 0.8 %copy.13 = s32[16,1,3]{2,0,1:T(8,128)S(1)} copy(s32[16,1,3]{0,1,2:T(1,128)} %param.10) | data formatting | bytes 384 | tf_op args[2]
  13.6 1.2 %copy-done.1 = f32[2,62,16,128]{3,2,1,0:T(8,128)S(1)} copy-done((f32[2,62,16,128]{3,2,1,0:T(8,128)S(1)}, f32[2,62,16,128]{3,2,1,0:T(8,128)}, u32[]{:S(2)}) %copy-start.1) | copy-done | bytes 1015832
  14.8 1.0 %copy-done.3 = f32[62,16,128]{2,1,0:T(8,128)S(1)} copy-done((f32[62,16,128]{2,1,0:T(8,128)S(1)}, f32[62,16,128]{2,1,0:T(8,128)}, u32[]{:S(2)}) %copy-start.3) | copy-done | bytes 507928
  15.8 1.0 %copy-done.5 = f32[62,16,128]{2,1,0:T(8,128)S(1)} copy-done((f32[62,16,128]{2,1,0:T(8,128)S(1)}, f32[62,16,128]{2,1,0:T(8,128)}, u32[]{:S(2)}) %copy-start.5) | copy-done | bytes 507928
  16.9 0.7 %copy-done.9 = s32[16,128]{1,0:T(8,128)S(1)} copy-done((s32[16,128]{1,0:T(8,128)S(1)}, s32[16,128]{1,0:T(8,128)}, u32[]{:S(2)}) %copy-start.9) | copy-done | bytes 8216
  17.6 0.5 shard_map.95
  18.1 1.0 %shard_map.96 = (f32[2,16,128]{2,1,0:T(8,128)S(1)}, f32[3,16,128]{2,1,0:T(8,128)S(1)}, f32[3,64,128]{2,1,0:T(8,128)S(1)}, f32[3,64,128]{2,1,0:T(8,128)S(1)}) custom-call(s32[2]{0:T(128)S(1)} %pad_add_fusion.place, s32[48]{0:T(128)S(1)} %and_select_fusion.index, bf16[176,128]{1,0:T(8,128)(2,1)S(1)} %collective-permute-done.a0, ...), custom_call_target="tpu_custom_call" | custom-call | bytes 3000000 | tf_op jit(solution)/shard_map/pallas_call | solution.py:274
  19.2 1.3 %collective-permute-start.7 = (f32[3,64,128]{2,1,0:T(8,128)S(1)}, f32[3,64,128]{2,1,0:T(8,128)S(1)}, u32[]{:S(2)}, u32[]{:S(2)}) collective-permute-start(f32[3,64,128]{2,1,0:T(8,128)S(1)} %get-tuple-element.33.r0), channel_id=1, source_target_pairs={{0,32},{64,96},{32,0},{96,64},{1,33},{65,97},{33,1},{97,65},{2,34}... | collective-permute-start | bytes 294920 | tf_op jit(solution)/shard_map/ppermute | solution.py:237
  20.4 2.3 %collective-permute-start.3 = (f32[3,64,128]{2,1,0:T(8,128)S(1)}, f32[3,64,128]{2,1,0:T(8,128)S(1)}, u32[]{:S(2)}, u32[]{:S(2)}) collective-permute-start(f32[3,64,128]{2,1,0:T(8,128)S(1)} %get-tuple-element.28.r1), channel_id=1, source_target_pairs={{32,64},{64,32},{33,65},{65,33},{34,66},{66,34},{35,67},{67,35},{3... | collective-permute-start | bytes 294920 | tf_op jit(solution)/shard_map/ppermute | solution.py:237
  22.7 0.1 slice_reduce_fusion
  22.8 0.1 slice_reduce_fusion.1
  22.9 0.1 slice_reduce_fusion.2
  23.1 4.0 %collective-permute-done.3.after.g1 = f32[3,64,128]{2,1,0:T(8,128)S(1)} collective-permute-done((f32[3,64,128]{2,1,0:T(8,128)S(1)}, f32[3,64,128]{2,1,0:T(8,128)S(1)}, u32[]{:S(2)}, u32[]{:S(2)}) %collective-permute-start.3) | collective-permute-done | bytes 98336 | tf_op jit(solution)/shard_map/ppermute | solution.py:237
  27.1 0.6 shard_map.97
  27.8 1.9 %collective-permute-start.5 = (bf16[16,32,128]{2,1,0:T(8,128)(2,1)S(1)}, bf16[16,32,128]{2,1,0:T(8,128)(2,1)S(1)}, u32[]{:S(2)}, u32[]{:S(2)}) collective-permute-start(bf16[16,32,128]{2,1,0:T(8,128)(2,1)S(1)} %get-tuple-element.30), channel_id=1, source_target_pairs={{16,0},{17,1},{18,2},{19,3},{20,4},{21,5},{22,6},{23,7},{24,8},{25... | collective-permute-start | bytes 393224 | tf_op jit(solution)/shard_map/ppermute | solution.py:249
  29.7 3.0 %collective-permute-start.6 = (bf16[16,32,128]{2,1,0:T(8,128)(2,1)S(1)}, bf16[16,32,128]{2,1,0:T(8,128)(2,1)S(1)}, u32[]{:S(2)}, u32[]{:S(2)}) collective-permute-start(bf16[16,32,128]{2,1,0:T(8,128)(2,1)S(1)} %get-tuple-element.31), channel_id=1, source_target_pairs={{17,0},{18,1},{19,2},{20,3},{21,4},{22,5},{23,6},{24,7},{25,8},{26... | collective-permute-start | bytes 393224 | tf_op jit(solution)/shard_map/ppermute | solution.py:249
  32.7 6.0 %collective-permute-start.9 = (f32[3,16,128]{2,1,0:T(8,128)S(1)}, f32[3,16,128]{2,1,0:T(8,128)S(1)}, u32[]{:S(2)}, u32[]{:S(2)}) collective-permute-start(f32[3,16,128]{2,1,0:T(8,128)S(1)} %get-tuple-element.41.c), channel_id=1, source_target_pairs={{1,2},{3,4},{5,6},{7,8},{9,10},{11,12},{13,14},{15,16},{17,18},{19... | collective-permute-start | bytes 73736 | tf_op jit(solution)/shard_map/ppermute | solution.py:237
  38.7 0.6 %shard_map.99 = (f32[62,16,128]{2,1,0:T(8,128)S(1)}, f32[62,16,128]{2,1,0:T(8,128)S(1)}, f32[62,16,128]{2,1,0:T(8,128)S(1)}, f32[62,16,128]{2,1,0:T(8,128)S(1)},...) custom-call(f32[3,64,128]{2,1,0:T(8,128)S(1)} %collective-permute-done.7.after.g0, ...), custom_call_target="tpu_custom_call" | custom-call | bytes 12000000 | tf_op jit(solution)/shard_map/pallas_call | solution.py:287
  39.4 1.9 %collective-permute-done.9.c1 = f32[3,16,128]{2,1,0:T(8,128)S(1)} collective-permute-done((f32[3,16,128]{2,1,0:T(8,128)S(1)}, f32[3,16,128]{2,1,0:T(8,128)S(1)}, u32[]{:S(2)}, u32[]{:S(2)}) %collective-permute-start.9) | collective-permute-done | bytes 24608 | tf_op jit(solution)/shard_map/ppermute | solution.py:237
  41.3 1.9 %shard_map.100 = (f32[2,62,16,128]{3,2,1,0:T(8,128)S(1)}, f32[2,16,128]{2,1,0:T(8,128)S(1)}, f32[2,64,128]{2,1,0:T(8,128)S(1)}, f32[2,64,128]{2,1,0:T(8,128)S(1)}) custom-call(s32[2]{0:T(128)S(1)} %pad_add_fusion.place, f32[2,62,16,128]{3,2,1,0:T(8,128)S(1)} %copy-done.2, f32[2,16,128]{2,1,0:T(8,128)S(1)} %get-tuple-element.32.forced, ...), custom_call_target="tpu_custom_call" | custom-call | bytes 12000000 | tf_op jit(solution)/shard_map/pallas_call | solution.py:302
  43.4 5.9 %collective-permute-start.11 = (f32[2,16,128]{2,1,0:T(8,128)S(1)}, f32[2,16,128]{2,1,0:T(8,128)S(1)}, u32[]{:S(2)}, u32[]{:S(2)}) collective-permute-start(f32[2,16,128]{2,1,0:T(8,128)S(1)} %get-tuple-element.43.d), channel_id=1, source_target_pairs={{1,2},{3,4},{5,6},{7,8},{9,10},{11,12},{13,14},{15,16},{17,18},{19... | collective-permute-start | bytes 49160 | tf_op jit(solution)/shard_map/ppermute | solution.py:237
  49.2 2.5 %collective-permute-done.11.d1 = f32[2,16,128]{2,1,0:T(8,128)S(1)} collective-permute-done((f32[2,16,128]{2,1,0:T(8,128)S(1)}, f32[2,16,128]{2,1,0:T(8,128)S(1)}, u32[]{:S(2)}, u32[]{:S(2)}) %collective-permute-start.11) | collective-permute-done | bytes 16416 | tf_op jit(solution)/shard_map/ppermute | solution.py:237
  51.7 6.0 %collective-permute-start.13 = (f32[2,64,128]{2,1,0:T(8,128)S(1)}, f32[2,64,128]{2,1,0:T(8,128)S(1)}, u32[]{:S(2)}, u32[]{:S(2)}) collective-permute-start(f32[2,64,128]{2,1,0:T(8,128)S(1)} %get-tuple-element.45.u1), channel_id=1, source_target_pairs={{32,64},{64,32},{33,65},{65,33},{34,66},{66,34},{35,67},{67,35},{3... | collective-permute-start | bytes 196616 | tf_op jit(solution)/shard_map/ppermute | solution.py:237
  57.7 1.9 %collective-permute-done.13.h1 = f32[2,64,128]{2,1,0:T(8,128)S(1)} collective-permute-done((f32[2,64,128]{2,1,0:T(8,128)S(1)}, f32[2,64,128]{2,1,0:T(8,128)S(1)}, u32[]{:S(2)}, u32[]{:S(2)}) %collective-permute-start.13) | collective-permute-done | bytes 65568 | tf_op jit(solution)/shard_map/ppermute | solution.py:237
  59.7 2.7 %shard_map.101 = f32[2,62,16,128]{3,2,1,0:T(8,128)} custom-call(s32[2]{0:T(128)S(1)} %pad_add_fusion.place, f32[2,62,16,128]{3,2,1,0:T(8,128)S(1)} %get-tuple-element.42.field, f32[62,16,128]{2,1,0:T(8,128)S(1)} %get-tuple-element.34.face_e, f32[62,16,128]{2,1,0:T(8,128)S(1)} %get-tuple-element.35.face_w, f32[62,16,128]{2,1,0:T(8,128)S(1)} %get-tuple-element.36.face_n, ...), custom_call_target="tpu_custom_call" | custom-call | bytes 9000000 | tf_op jit(solution)/shard_map/pallas_call | solution.py:313
  62.3 1.1 %shard_map.98 = f32[32,16,128]{2,1,0:T(8,128)} custom-call(bf16[16,32,128]{2,1,0:T(8,128)(2,1)S(1)} %collective-permute-done.4.a0, bf16[16,32,128]{2,1,0:T(8,128)(2,1)S(1)} %collective-permute-done.5.a1, bf16[16,32,128]{2,1,0:T(8,128)(2,1)S(1)} %collective-permute-done.6.a2, bf16[16,384,128]{2,1,0:T(8,128)(2,1)S(1)} %bitcast.18), custom_call_target="tpu_custom_call" | custom-call | bytes 6000000 | tf_op jit(solution)/shard_map/pallas_call | solution.py:310
  (39 shorter events, 0.6 us)
Async XLA Ops:
  0.6 17.5 %copy-start = (bf16[16,3,128,128]{3,2,1,0:T(8,128)(2,1)S(1)}, bf16[16,3,128,128]{3,2,1,0:T(8,128)(2,1)}, u32[]{:S(2)}) copy-start(bf16[16,3,128,128]{3,2,1,0:T(8,128)(2,1)} %param.9) | copy-start | bytes 4718596
  2.7 15.4 %collective-permute-start = (bf16[176,128]{1,0:T(8,128)(2,1)S(1)}, bf16[176,128]{1,0:T(8,128)(2,1)S(1)}, u32[]{:S(2)}, u32[]{:S(2)}) collective-permute-start(bf16[176,128]{1,0:T(8,128)(2,1)S(1)} %maximum_maximum_fusion), channel_id=1, source_target_pairs={{15,0},{16,1},{17,2},{18,3},{19,4},{20,5},{21,6},{22,7},{23,8},{24... | collective-permute-start | bytes 135176 | tf_op jit(solution)/shard_map/ppermute | solution.py:249
  7.7 10.4 %collective-permute-start.1 = (bf16[176,128]{1,0:T(8,128)(2,1)S(1)}, bf16[176,128]{1,0:T(8,128)(2,1)S(1)}, u32[]{:S(2)}, u32[]{:S(2)}) collective-permute-start(bf16[176,128]{1,0:T(8,128)(2,1)S(1)} %maximum_maximum_fusion), channel_id=1, source_target_pairs={{16,0},{17,1},{18,2},{19,3},{20,4},{21,5},{22,6},{23,7},{24,8},{25... | collective-permute-start | bytes 135176 | tf_op jit(solution)/shard_map/ppermute | solution.py:249
  7.9 10.2 %collective-permute-start.2 = (bf16[176,128]{1,0:T(8,128)(2,1)S(1)}, bf16[176,128]{1,0:T(8,128)(2,1)S(1)}, u32[]{:S(2)}, u32[]{:S(2)}) collective-permute-start(bf16[176,128]{1,0:T(8,128)(2,1)S(1)} %maximum_maximum_fusion), channel_id=1, source_target_pairs={{17,0},{18,1},{19,2},{20,3},{21,4},{22,5},{23,6},{24,7},{25,8},{26... | collective-permute-start | bytes 135176 | tf_op jit(solution)/shard_map/ppermute | solution.py:249
  13.6 1.2 %copy-start.1 = (f32[2,62,16,128]{3,2,1,0:T(8,128)S(1)}, f32[2,62,16,128]{3,2,1,0:T(8,128)}, u32[]{:S(2)}) copy-start(f32[2,62,16,128]{3,2,1,0:T(8,128)} %tracers.3) | copy-start | bytes 3047428
  14.8 1.0 %copy-start.3 = (f32[62,16,128]{2,1,0:T(8,128)S(1)}, f32[62,16,128]{2,1,0:T(8,128)}, u32[]{:S(2)}) copy-start(f32[62,16,128]{2,1,0:T(8,128)} %east.3) | copy-start | bytes 1523716
  15.8 1.0 %copy-start.5 = (f32[62,16,128]{2,1,0:T(8,128)S(1)}, f32[62,16,128]{2,1,0:T(8,128)}, u32[]{:S(2)}) copy-start(f32[62,16,128]{2,1,0:T(8,128)} %north.3) | copy-start | bytes 1523716
  16.9 0.7 %copy-start.9 = (s32[16,128]{1,0:T(8,128)S(1)}, s32[16,128]{1,0:T(8,128)}, u32[]{:S(2)}) copy-start(s32[16,128]{1,0:T(8,128)} %count.5) | copy-start | bytes 24580
  17.6 9.5 %copy-start.7 = (bf16[64,32,128]{2,1,0:T(8,128)(2,1)S(1)}, bf16[64,32,128]{2,1,0:T(8,128)(2,1)}, u32[]{:S(2)}) copy-start(bf16[64,32,128]{2,1,0:T(8,128)(2,1)} %atm.1) | copy-start | bytes 1572868
  18.1 20.6 %copy-start.4 = (f32[62,16,128]{2,1,0:T(8,128)S(1)}, f32[62,16,128]{2,1,0:T(8,128)}, u32[]{:S(2)}) copy-start(f32[62,16,128]{2,1,0:T(8,128)} %east.3) | copy-start | bytes 1523716
  18.1 20.6 %copy-start.6 = (f32[62,16,128]{2,1,0:T(8,128)S(1)}, f32[62,16,128]{2,1,0:T(8,128)}, u32[]{:S(2)}) copy-start(f32[62,16,128]{2,1,0:T(8,128)} %north.3) | copy-start | bytes 1523716
  18.1 20.6 %copy-start.8 = (f32[62,16,128]{2,1,0:T(8,128)S(1)}, f32[62,16,128]{2,1,0:T(8,128)}, u32[]{:S(2)}) copy-start(f32[62,16,128]{2,1,0:T(8,128)} %mixing.1) | copy-start | bytes 1523716
  18.1 20.6 %copy-start.10 = (s32[16,128]{1,0:T(8,128)S(1)}, s32[16,128]{1,0:T(8,128)}, u32[]{:S(2)}) copy-start(s32[16,128]{1,0:T(8,128)} %count.5) | copy-start | bytes 24580
  19.2 22.1 %copy-start.2 = (f32[2,62,16,128]{3,2,1,0:T(8,128)S(1)}, f32[2,62,16,128]{3,2,1,0:T(8,128)}, u32[]{:S(2)}) copy-start(f32[2,62,16,128]{3,2,1,0:T(8,128)} %tracers.3) | copy-start | bytes 3047428
  19.2 13.5 %collective-permute-start.7 = (f32[3,64,128]{2,1,0:T(8,128)S(1)}, f32[3,64,128]{2,1,0:T(8,128)S(1)}, u32[]{:S(2)}, u32[]{:S(2)}) collective-permute-start(f32[3,64,128]{2,1,0:T(8,128)S(1)} %get-tuple-element.33.r0), channel_id=1, source_target_pairs={{0,32},{64,96},{32,0},{96,64},{1,33},{65,97},{33,1},{97,65},{2,34}... | collective-permute-start | bytes 294920 | tf_op jit(solution)/shard_map/ppermute | solution.py:237
  20.4 6.6 %collective-permute-start.3 = (f32[3,64,128]{2,1,0:T(8,128)S(1)}, f32[3,64,128]{2,1,0:T(8,128)S(1)}, u32[]{:S(2)}, u32[]{:S(2)}) collective-permute-start(f32[3,64,128]{2,1,0:T(8,128)S(1)} %get-tuple-element.28.r1), channel_id=1, source_target_pairs={{32,64},{64,32},{33,65},{65,33},{34,66},{66,34},{35,67},{67,35},{3... | collective-permute-start | bytes 294920 | tf_op jit(solution)/shard_map/ppermute | solution.py:237
  27.7 34.6 %collective-permute-start.4 = (bf16[16,32,128]{2,1,0:T(8,128)(2,1)S(1)}, bf16[16,32,128]{2,1,0:T(8,128)(2,1)S(1)}, u32[]{:S(2)}, u32[]{:S(2)}) collective-permute-start(bf16[16,32,128]{2,1,0:T(8,128)(2,1)S(1)} %get-tuple-element.29), channel_id=1, source_target_pairs={{15,0},{16,1},{17,2},{18,3},{19,4},{20,5},{21,6},{22,7},{23,8},{24... | collective-permute-start | bytes 393224 | tf_op jit(solution)/shard_map/ppermute | solution.py:249
  27.8 34.6 %collective-permute-start.5 = (bf16[16,32,128]{2,1,0:T(8,128)(2,1)S(1)}, bf16[16,32,128]{2,1,0:T(8,128)(2,1)S(1)}, u32[]{:S(2)}, u32[]{:S(2)}) collective-permute-start(bf16[16,32,128]{2,1,0:T(8,128)(2,1)S(1)} %get-tuple-element.30), channel_id=1, source_target_pairs={{16,0},{17,1},{18,2},{19,3},{20,4},{21,5},{22,6},{23,7},{24,8},{25... | collective-permute-start | bytes 393224 | tf_op jit(solution)/shard_map/ppermute | solution.py:249
  29.7 32.7 %collective-permute-start.6 = (bf16[16,32,128]{2,1,0:T(8,128)(2,1)S(1)}, bf16[16,32,128]{2,1,0:T(8,128)(2,1)S(1)}, u32[]{:S(2)}, u32[]{:S(2)}) collective-permute-start(bf16[16,32,128]{2,1,0:T(8,128)(2,1)S(1)} %get-tuple-element.31), channel_id=1, source_target_pairs={{17,0},{18,1},{19,2},{20,3},{21,4},{22,5},{23,6},{24,7},{25,8},{26... | collective-permute-start | bytes 393224 | tf_op jit(solution)/shard_map/ppermute | solution.py:249
  32.7 6.7 %collective-permute-start.8 = (f32[3,16,128]{2,1,0:T(8,128)S(1)}, f32[3,16,128]{2,1,0:T(8,128)S(1)}, u32[]{:S(2)}, u32[]{:S(2)}) collective-permute-start(f32[3,16,128]{2,1,0:T(8,128)S(1)} %get-tuple-element.41.c), channel_id=1, source_target_pairs={{0,1},{2,3},{4,5},{6,7},{8,9},{10,11},{12,13},{14,15},{16,17},{18,... | collective-permute-start | bytes 73736 | tf_op jit(solution)/shard_map/ppermute | solution.py:237
  32.7 8.6 %collective-permute-start.9 = (f32[3,16,128]{2,1,0:T(8,128)S(1)}, f32[3,16,128]{2,1,0:T(8,128)S(1)}, u32[]{:S(2)}, u32[]{:S(2)}) collective-permute-start(f32[3,16,128]{2,1,0:T(8,128)S(1)} %get-tuple-element.41.c), channel_id=1, source_target_pairs={{1,2},{3,4},{5,6},{7,8},{9,10},{11,12},{13,14},{15,16},{17,18},{19... | collective-permute-start | bytes 73736 | tf_op jit(solution)/shard_map/ppermute | solution.py:237
  43.3 6.0 %collective-permute-start.10 = (f32[2,16,128]{2,1,0:T(8,128)S(1)}, f32[2,16,128]{2,1,0:T(8,128)S(1)}, u32[]{:S(2)}, u32[]{:S(2)}) collective-permute-start(f32[2,16,128]{2,1,0:T(8,128)S(1)} %get-tuple-element.43.d), channel_id=1, source_target_pairs={{0,1},{2,3},{4,5},{6,7},{8,9},{10,11},{12,13},{14,15},{16,17},{18,... | collective-permute-start | bytes 49160 | tf_op jit(solution)/shard_map/ppermute | solution.py:237
  43.4 8.4 %collective-permute-start.11 = (f32[2,16,128]{2,1,0:T(8,128)S(1)}, f32[2,16,128]{2,1,0:T(8,128)S(1)}, u32[]{:S(2)}, u32[]{:S(2)}) collective-permute-start(f32[2,16,128]{2,1,0:T(8,128)S(1)} %get-tuple-element.43.d), channel_id=1, source_target_pairs={{1,2},{3,4},{5,6},{7,8},{9,10},{11,12},{13,14},{15,16},{17,18},{19... | collective-permute-start | bytes 49160 | tf_op jit(solution)/shard_map/ppermute | solution.py:237
  49.2 8.5 %collective-permute-start.12 = (f32[2,64,128]{2,1,0:T(8,128)S(1)}, f32[2,64,128]{2,1,0:T(8,128)S(1)}, u32[]{:S(2)}, u32[]{:S(2)}) collective-permute-start(f32[2,64,128]{2,1,0:T(8,128)S(1)} %get-tuple-element.44.u0), channel_id=1, source_target_pairs={{0,32},{64,96},{32,0},{96,64},{1,33},{65,97},{33,1},{97,65},{2,34}... | collective-permute-start | bytes 196616 | tf_op jit(solution)/shard_map/ppermute | solution.py:237
  51.7 7.9 %collective-permute-start.13 = (f32[2,64,128]{2,1,0:T(8,128)S(1)}, f32[2,64,128]{2,1,0:T(8,128)S(1)}, u32[]{:S(2)}, u32[]{:S(2)}) collective-permute-start(f32[2,64,128]{2,1,0:T(8,128)S(1)} %get-tuple-element.45.u1), channel_id=1, source_target_pairs={{32,64},{64,32},{33,65},{65,33},{34,66},{66,34},{35,67},{67,35},{3... | collective-permute-start | bytes 196616 | tf_op jit(solution)/shard_map/ppermute | solution.py:237

commit v2 on v1

--- a/solution.py
+++ b/solution.py
@@ -11,6 +11,7 @@
 ANY = pl.BlockSpec(memory_space=pl.ANY)
 SMEM = pl.BlockSpec(memory_space=pltpu.SMEM)
 LIMIT = 24 * 1024 * 1024
+FULL = 60 * 1024 * 1024
 
 
 def lanes(shape):
@@ -24,6 +25,25 @@
 def turn(x, shift):
     shift = shift % x.shape[-1]
     return x if shift == 0 else pltpu.roll(x, shift, x.ndim - 1)
+
+
+def ask_kernel(index, atm, out, held, wide, sem):
+    blocks = atm.shape[0]
+    rows = held.shape[1]
+    copy = pltpu.make_async_copy(atm.at[:, :rows, :], held, sem)
+    copy.start()
+    height = index.shape[0]
+    for s in range(3):
+        for y in range(height):
+            at = 2 * blocks + s * height + y
+            b = lax.rem(index[y, 0, s], blocks).astype(F32)
+            wide[at : at + 1, :] = jnp.full((1, wide.shape[1]), b, F32)
+    copy.wait()
+    for b in range(blocks):
+        x = held[b].astype(F32)
+        for f in range(2):
+            wide[b + f * blocks : b + f * blocks + 1, :] = x[f : f + 1, :]
+    out[...] = wide[...].astype(BF16)
 
 
 def pack_kernel(tracers, east, north, count, first, tile, tops, bottoms):
@@ -92,7 +112,7 @@
         held[s] = a[: 2 * blocks].astype(F32)
     for y in range(height):
         for s in range(3):
-            b = lax.rem(index[3 * y + s], blocks)
+            b = lax.rem(index[y, 0, s], blocks)
             for f in range(2):
                 picked[8 * y + f : 8 * y + f + 1, s * 128 : (s + 1) * 128] = held[
                     s, pl.ds(b + f * blocks, 1), :
@@ -221,14 +241,14 @@
         out[:, y, :] = jnp.dot(picked, weights[y], preferred_element_type=F32)
 
 
-def call(kernel, outs, specs, scratch=(), cost=1):
+def call(kernel, outs, specs, scratch=(), cost=1, limit=LIMIT):
     return pl.pallas_call(
         kernel,
         out_shape=outs,
         in_specs=specs,
         out_specs=[VMEM] * len(outs),
         scratch_shapes=list(scratch),
-        compiler_params=pltpu.CompilerParams(vmem_limit_bytes=LIMIT),
+        compiler_params=pltpu.CompilerParams(vmem_limit_bytes=limit),
         cost_estimate=pl.CostEstimate(flops=0, bytes_accessed=cost * 3000000, transcendentals=0),
     )
 
@@ -257,9 +277,18 @@
     weights = remap_weights.reshape(height, -1, width)
 
     blocks, fields = atm_flux.shape[:2]
-    within = intersection[:, 0, :] % blocks
-    asked = jnp.broadcast_to(within.T.reshape(-1, 1), (3 * height, width)).astype(BF16)
-    few = jnp.concatenate([atm_flux[:, 0, :], atm_flux[:, 1, :], asked], 0)
+    (few,) = call(
+        ask_kernel,
+        [sds(2 * blocks + 3 * height, width, dtype=BF16)],
+        [SMEM, ANY],
+        [
+            pltpu.VMEM((blocks, 16, width), BF16),
+            pltpu.VMEM((2 * blocks + 3 * height, width), F32),
+            pltpu.SemaphoreType.DMA,
+        ],
+        cost=1,
+        limit=FULL,
+    )(intersection, atm_flux)
     slots = [tiles // 2 + s - 1 for s in range(3)]
     part = [from_ahead(few, d) for d in slots]
 
@@ -277,7 +306,7 @@
         [SMEM, SMEM] + [VMEM] * 9,
         [pltpu.VMEM((3, 2 * blocks, width), F32), pltpu.VMEM((8 * height, 3 * width), F32)],
         cost=1,
-    )(place, within.reshape(-1), *part, weights, level_count, first, tile, tops, bottoms)
+    )(place, intersection, *part, weights, level_count, first, tile, tops, bottoms)
 
     def exchange(c, r0, r1):
         g0, g1 = swap(r0, "rows", rows0), swap(r1, "rows", rows1)
@@ -285,7 +314,7 @@
 
     c0, c1, g0, g1 = exchange(c, r0, r1)
     coefficients = call(solver_kernel, [plane] * 7, [ANY] + [VMEM] * 4, cost=4)(
-        g0, east_speed, north_speed, mixing, level_count
+        c, east_speed, north_speed, mixing, level_count
     )
     wanted = jnp.concatenate(
         [part[s][2 * blocks + (2 - s) * height :][:height, 0] for s in range(3)]
@@ -295,7 +324,7 @@
         [sds(height, fields, width, dtype=BF16)] * 3,
         [ANY, SMEM, VMEM],
         cost=1,
-    )(g1, wanted, atm_flux)
+    )(c, wanted, atm_flux)
     blocks_of = [from_ahead(found[2 - s], slots[s]) for s in range(3)]
 
     scratch = [pltpu.VMEM((2, levels, height, width), F32)] + [pltpu.VMEM((2, tall, width), F32)] * 2

time: 63.8 us -> 55.1 us (0.86)
  waiting for transfers between devices: 10.4 us -> 4.76 us
  starting transfers between devices: 36.4 us -> 32 us
  Pallas kernels: 8.47 us -> 11 us
  other arithmetic: 0.94 us -> 0.15 us
    ppermute x8, starting transfers between devices: 21.4 us -> 15.4 us  [swap(): lax.ppermute(block, axis, [(a, b) for a, b in pairs] + [(b, a) for a, b i...]
    ppermute x8, waiting for transfers between devices: 10.4 us -> 4.74 us  [swap(): lax.ppermute(block, axis, [(a, b) for a, b in pairs] + [(b, a) for a, b i...]
    pallas_call x0 -> x1, Pallas kernels: none -> 2.41 us  [per_device(): call(ask_kernel, [sds(2 * blocks + 3 * height, width, dtype=BF16)], [SMEM...]
    ppermute x6, starting transfers between devices: 14.9 us -> 16.6 us  [from_ahead(): lax.ppermute(block, 'cols', [((i + distance) % tiles, i) for i in range(t...]
    slice x1 -> x0, local copies, waits for them, and re-layouts: 1.15 us -> none  [per_device(): few = jnp.concatenate([atm_flux[:, 0, :], atm_flux[:, 1, :], asked], 0)]
    unnamed x23 -> x25, local copies, waits for them, and re-layouts: 4.77 us -> 5.59 us
    convert_element_type x1 -> x0, other arithmetic: 0.69 us -> none  [per_device(): jnp.broadcast_to(within.T.reshape(-1, 1), (3 * height, width)).astype(BF16)]
  transfers between devices with their start and end apart: 14 -> 14, of which waited for: 4 -> 1; matrix products, arithmetic and copies ran while one was open for 2% -> 1% of each run, Pallas kernels for 10% -> 9%
where the time goes in v2:
time: 55.1 us; the launch traced here: 54.7 us
  starting transfers between devices  32 us (58%)
  Pallas kernels  11 us (20%)
  local copies, waits for them, and re-layouts  5.94 us (11%)
  waiting for transfers between devices  4.76 us (9%)
  between operations  0.86 us (2%)
    ppermute x6, starting transfers between devices, from_ahead(): lax.ppermute(block, 'cols', [((i + distance) % tiles, i) for i in range(t...  16.6 us
    ppermute x8, starting transfers between devices, swap(): lax.ppermute(block, axis, [(a, b) for a, b in pairs] + [(b, a) for a, b i...  15.4 us
    unnamed x25, local copies, waits for them, and re-layouts  5.59 us
    ppermute x8, waiting for transfers between devices, swap(): lax.ppermute(block, axis, [(a, b) for a, b in pairs] + [(b, a) for a, b i...  4.74 us
    pallas_call x1, Pallas kernels, per_device(): call(second_step_kernel, [sds(2, levels, height, width)], [SMEM] + [VMEM]...  2.67 us
    pallas_call x1, Pallas kernels, per_device(): call(ask_kernel, [sds(2 * blocks + 3 * height, width, dtype=BF16)], [SMEM...  2.41 us
    pallas_call x1, Pallas kernels, per_device(): call(first_step_kernel, [sds(2, levels, height, width), sds(2, height, wi...  1.95 us
    pallas_call x1, Pallas kernels, per_device(): call(force_kernel, [sds(2, height, width), sds(3, height, width)] + [sds(...  1.15 us
  transfers between devices with their start and end apart: 14, of which 1 were waited for; matrix products, arithmetic and copies ran while one was open for 1% of the time, Pallas kernels for 9%

profile of v2, /device:TPU:1, one launch (start us, length us, event | category | flops | bytes accessed | tf_op | source)
XLA Modules:
  0.0 54.7 jit_solution(5833420982791883812)
XLA Ops:
  0.6 1.5 %copy.13.index = s32[16,1,3]{2,1,0:T(1,128)} copy(s32[16,1,3]{0,1,2:T(1,128)} %param.10) | data formatting | bytes 384 | tf_op args[2]
  2.1 2.4 %shard_map.95 = bf16[176,128]{1,0:T(8,128)(2,1)} custom-call(s32[16,1,3]{2,1,0:T(1,128)} %copy.13.index, bf16[64,32,128]{2,1,0:T(8,128)(2,1)} %atm.3), custom_call_target="tpu_custom_call" | custom-call | bytes 3000000 | tf_op jit(solution)/shard_map/pallas_call | solution.py:280
  4.5 5.0 %collective-permute-start = (bf16[176,128]{1,0:T(8,128)(2,1)}, bf16[176,128]{1,0:T(8,128)(2,1)S(1)}, u32[]{:S(2)}, u32[]{:S(2)}) collective-permute-start(bf16[176,128]{1,0:T(8,128)(2,1)} %shard_map.95), channel_id=1, source_target_pairs={{15,0},{16,1},{17,2},{18,3},{19,4},{20,5},{21,6},{22,7},{23,8},{24... | collective-permute-start | bytes 135176 | tf_op jit(solution)/shard_map/ppermute | solution.py:269
  9.5 0.2 collective-permute-start.1
  9.8 4.7 %collective-permute-start.2 = (bf16[176,128]{1,0:T(8,128)(2,1)}, bf16[176,128]{1,0:T(8,128)(2,1)S(1)}, u32[]{:S(2)}, u32[]{:S(2)}) collective-permute-start(bf16[176,128]{1,0:T(8,128)(2,1)} %shard_map.95), channel_id=1, source_target_pairs={{17,0},{18,1},{19,2},{20,3},{21,4},{22,5},{23,6},{24,7},{25,8},{26... | collective-permute-start | bytes 135176 | tf_op jit(solution)/shard_map/ppermute | solution.py:269
  14.6 1.2 %copy-done.1 = f32[2,62,16,128]{3,2,1,0:T(8,128)S(1)} copy-done((f32[2,62,16,128]{3,2,1,0:T(8,128)S(1)}, f32[2,62,16,128]{3,2,1,0:T(8,128)}, u32[]{:S(2)}) %copy-start.1) | copy-done | bytes 1015832
  15.8 1.0 %copy-done.4 = f32[62,16,128]{2,1,0:T(8,128)S(1)} copy-done((f32[62,16,128]{2,1,0:T(8,128)S(1)}, f32[62,16,128]{2,1,0:T(8,128)}, u32[]{:S(2)}) %copy-start.4) | copy-done | bytes 507928
  16.8 1.0 %copy-done.6 = f32[62,16,128]{2,1,0:T(8,128)S(1)} copy-done((f32[62,16,128]{2,1,0:T(8,128)S(1)}, f32[62,16,128]{2,1,0:T(8,128)}, u32[]{:S(2)}) %copy-start.6) | copy-done | bytes 507928
  17.8 0.7 %copy-done.9 = s32[16,128]{1,0:T(8,128)S(1)} copy-done((s32[16,128]{1,0:T(8,128)S(1)}, s32[16,128]{1,0:T(8,128)}, u32[]{:S(2)}) %copy-start.9) | copy-done | bytes 8216
  18.5 0.5 shard_map.96
  19.1 0.1 copy-done.11
  19.2 1.2 %shard_map.97 = (f32[2,16,128]{2,1,0:T(8,128)S(1)}, f32[3,16,128]{2,1,0:T(8,128)S(1)}, f32[3,64,128]{2,1,0:T(8,128)S(1)}, f32[3,64,128]{2,1,0:T(8,128)S(1)}) custom-call(s32[2]{0:T(128)S(1)} %pad_add_fusion.place, s32[16,1,3]{2,1,0:T(1,128)S(1)} %copy-done.11, bf16[176,128]{1,0:T(8,128)(2,1)S(1)} %collective-permute-done.a0, ...), custom_call_target="tpu_custom_call" | custom-call | bytes 3000000 | tf_op jit(solution)/shard_map/pallas_call | solution.py:303
  20.4 4.5 %collective-permute-start.7 = (f32[3,16,128]{2,1,0:T(8,128)S(1)}, f32[3,16,128]{2,1,0:T(8,128)S(1)}, u32[]{:S(2)}, u32[]{:S(2)}) collective-permute-start(f32[3,16,128]{2,1,0:T(8,128)S(1)} %get-tuple-element.28.after.c), channel_id=1, source_target_pairs={{1,2},{3,4},{5,6},{7,8},{9,10},{11,12},{13,14},{15,16},{17,18},{19... | collective-permute-start | bytes 73736 | tf_op jit(solution)/shard_map/ppermute | solution.py:257
  25.0 2.9 %collective-permute-start.8 = (f32[3,64,128]{2,1,0:T(8,128)S(1)}, f32[3,64,128]{2,1,0:T(8,128)S(1)}, u32[]{:S(2)}, u32[]{:S(2)}) collective-permute-start(f32[3,64,128]{2,1,0:T(8,128)S(1)} %get-tuple-element.40.r0), channel_id=1, source_target_pairs={{0,32},{64,96},{32,0},{96,64},{1,33},{65,97},{33,1},{97,65},{2,34}... | collective-permute-start | bytes 294920 | tf_op jit(solution)/shard_map/ppermute | solution.py:257
  27.9 2.1 %collective-permute-start.9 = (f32[3,64,128]{2,1,0:T(8,128)S(1)}, f32[3,64,128]{2,1,0:T(8,128)S(1)}, u32[]{:S(2)}, u32[]{:S(2)}) collective-permute-start(f32[3,64,128]{2,1,0:T(8,128)S(1)} %get-tuple-element.41.r1), channel_id=1, source_target_pairs={{32,64},{64,32},{33,65},{65,33},{34,66},{66,34},{35,67},{67,35},{3... | collective-permute-start | bytes 294920 | tf_op jit(solution)/shard_map/ppermute | solution.py:257
  30.0 0.1 slice_reduce_fusion
  30.1 0.1 slice_reduce_fusion.1
  30.2 0.1 slice_reduce_fusion.2
  30.3 0.1 maximum_convert_fusion.wanted
  30.4 0.6 %shard_map.98 = (bf16[16,32,128]{2,1,0:T(8,128)(2,1)S(1)}, bf16[16,32,128]{2,1,0:T(8,128)(2,1)S(1)}, bf16[16,32,128]{2,1,0:T(8,128)(2,1)S(1)}) custom-call(f32[3,16,128]{2,1,0:T(8,128)S(1)} %get-tuple-element.28.after.c, s32[48]{0:T(128)S(1)} %maximum_convert_fusion.wanted, bf16[64,32,128]{2,1,0:T(8,128)(2,1)S(1)} %copy-done.3), custom_call_target="tpu_custom_call" | custom-call | bytes 3000000 | tf_op jit(solution)/shard_map/pallas_call | solution.py:322
  31.0 0.1 collective-permute-start.3
  31.1 1.9 %collective-permute-start.4 = (bf16[16,32,128]{2,1,0:T(8,128)(2,1)S(1)}, bf16[16,32,128]{2,1,0:T(8,128)(2,1)S(1)}, u32[]{:S(2)}, u32[]{:S(2)}) collective-permute-start(bf16[16,32,128]{2,1,0:T(8,128)(2,1)S(1)} %get-tuple-element.30), channel_id=1, source_target_pairs={{16,0},{17,1},{18,2},{19,3},{20,4},{21,5},{22,6},{23,7},{24,8},{25... | collective-permute-start | bytes 393224 | tf_op jit(solution)/shard_map/ppermute | solution.py:269
  33.0 4.7 %collective-permute-start.5 = (bf16[16,32,128]{2,1,0:T(8,128)(2,1)S(1)}, bf16[16,32,128]{2,1,0:T(8,128)(2,1)S(1)}, u32[]{:S(2)}, u32[]{:S(2)}) collective-permute-start(bf16[16,32,128]{2,1,0:T(8,128)(2,1)S(1)} %get-tuple-element.31), channel_id=1, source_target_pairs={{17,0},{18,1},{19,2},{20,3},{21,4},{22,5},{23,6},{24,7},{25,8},{26... | collective-permute-start | bytes 393224 | tf_op jit(solution)/shard_map/ppermute | solution.py:269
  37.7 0.6 %shard_map.100 = (f32[62,16,128]{2,1,0:T(8,128)S(1)}, f32[62,16,128]{2,1,0:T(8,128)S(1)}, f32[62,16,128]{2,1,0:T(8,128)S(1)}, f32[62,16,128]{2,1,0:T(8,128)S(1)}...) custom-call(f32[3,16,128]{2,1,0:T(8,128)S(1)} %get-tuple-element.28.after.c, ...), custom_call_target="tpu_custom_call" | custom-call | bytes 12000000 | tf_op jit(solution)/shard_map/pallas_call | solution.py:316
  38.4 1.9 %shard_map.101 = (f32[2,62,16,128]{3,2,1,0:T(8,128)S(1)}, f32[2,16,128]{2,1,0:T(8,128)S(1)}, f32[2,64,128]{2,1,0:T(8,128)S(1)}, f32[2,64,128]{2,1,0:T(8,128)S(1)}) custom-call(s32[2]{0:T(128)S(1)} %pad_add_fusion.place, f32[2,62,16,128]{3,2,1,0:T(8,128)S(1)} %copy-done.2, f32[2,16,128]{2,1,0:T(8,128)S(1)} %get-tuple-element.32.forced, ...), custom_call_target="tpu_custom_call" | custom-call | bytes 12000000 | tf_op jit(solution)/shard_map/pallas_call | solution.py:331
  40.3 0.1 collective-permute-start.12
  40.4 3.1 %collective-permute-start.13 = (f32[2,64,128]{2,1,0:T(8,128)S(1)}, f32[2,64,128]{2,1,0:T(8,128)S(1)}, u32[]{:S(2)}, u32[]{:S(2)}) collective-permute-start(f32[2,64,128]{2,1,0:T(8,128)S(1)} %get-tuple-element.45.u1), channel_id=1, source_target_pairs={{32,64},{64,32},{33,65},{65,33},{34,66},{66,34},{35,67},{67,35},{3... | collective-permute-start | bytes 196616 | tf_op jit(solution)/shard_map/ppermute | solution.py:257
  43.5 0.1 collective-permute-start.10
  43.6 2.5 %collective-permute-start.11 = (f32[2,16,128]{2,1,0:T(8,128)S(1)}, f32[2,16,128]{2,1,0:T(8,128)S(1)}, u32[]{:S(2)}, u32[]{:S(2)}) collective-permute-start(f32[2,16,128]{2,1,0:T(8,128)S(1)} %get-tuple-element.43.d), channel_id=1, source_target_pairs={{1,2},{3,4},{5,6},{7,8},{9,10},{11,12},{13,14},{15,16},{17,18},{19... | collective-permute-start | bytes 49160 | tf_op jit(solution)/shard_map/ppermute | solution.py:257
  46.2 1.1 %shard_map.99 = f32[32,16,128]{2,1,0:T(8,128)} custom-call(bf16[16,32,128]{2,1,0:T(8,128)(2,1)S(1)} %collective-permute-done.3.a0, bf16[16,32,128]{2,1,0:T(8,128)(2,1)S(1)} %collective-permute-done.4.a1, bf16[16,32,128]{2,1,0:T(8,128)(2,1)S(1)} %collective-permute-done.5.a2, bf16[16,384,128]{2,1,0:T(8,128)(2,1)S(1)} %bitcast.4), custom_call_target="tpu_custom_call" | custom-call | bytes 6000000 | tf_op jit(solution)/shard_map/pallas_call | solution.py:339
  47.3 4.7 %collective-permute-done.11.d1 = f32[2,16,128]{2,1,0:T(8,128)S(1)} collective-permute-done((f32[2,16,128]{2,1,0:T(8,128)S(1)}, f32[2,16,128]{2,1,0:T(8,128)S(1)}, u32[]{:S(2)}, u32[]{:S(2)}) %collective-permute-start.11) | collective-permute-done | bytes 16416 | tf_op jit(solution)/shard_map/ppermute | solution.py:257
  52.0 2.7 %shard_map.102 = f32[2,62,16,128]{3,2,1,0:T(8,128)} custom-call(s32[2]{0:T(128)S(1)} %pad_add_fusion.place, f32[2,62,16,128]{3,2,1,0:T(8,128)S(1)} %get-tuple-element.42.field, f32[62,16,128]{2,1,0:T(8,128)S(1)} %get-tuple-element.33.face_e, f32[62,16,128]{2,1,0:T(8,128)S(1)} %get-tuple-element.34.face_w, f32[62,16,128]{2,1,0:T(8,128)S(1)} %get-tuple-element.35.face_n, ...), custom_call_target="tpu_custom_call" | custom-call | bytes 9000000 | tf_op jit(solution)/shard_map/pallas_call | solution.py:342
  (34 shorter events, 0.2 us)
Async XLA Ops:
  0.6 18.5 %copy-start = (bf16[16,3,128,128]{3,2,1,0:T(8,128)(2,1)S(1)}, bf16[16,3,128,128]{3,2,1,0:T(8,128)(2,1)}, u32[]{:S(2)}) copy-start(bf16[16,3,128,128]{3,2,1,0:T(8,128)(2,1)} %param.9) | copy-start | bytes 4718596
  4.5 14.6 %collective-permute-start = (bf16[176,128]{1,0:T(8,128)(2,1)}, bf16[176,128]{1,0:T(8,128)(2,1)S(1)}, u32[]{:S(2)}, u32[]{:S(2)}) collective-permute-start(bf16[176,128]{1,0:T(8,128)(2,1)} %shard_map.95), channel_id=1, source_target_pairs={{15,0},{16,1},{17,2},{18,3},{19,4},{20,5},{21,6},{22,7},{23,8},{24... | collective-permute-start | bytes 135176 | tf_op jit(solution)/shard_map/ppermute | solution.py:269
  9.5 9.6 %collective-permute-start.1 = (bf16[176,128]{1,0:T(8,128)(2,1)}, bf16[176,128]{1,0:T(8,128)(2,1)S(1)}, u32[]{:S(2)}, u32[]{:S(2)}) collective-permute-start(bf16[176,128]{1,0:T(8,128)(2,1)} %shard_map.95), channel_id=1, source_target_pairs={{16,0},{17,1},{18,2},{19,3},{20,4},{21,5},{22,6},{23,7},{24,8},{25... | collective-permute-start | bytes 135176 | tf_op jit(solution)/shard_map/ppermute | solution.py:269
  9.8 9.4 %collective-permute-start.2 = (bf16[176,128]{1,0:T(8,128)(2,1)}, bf16[176,128]{1,0:T(8,128)(2,1)S(1)}, u32[]{:S(2)}, u32[]{:S(2)}) collective-permute-start(bf16[176,128]{1,0:T(8,128)(2,1)} %shard_map.95), channel_id=1, source_target_pairs={{17,0},{18,1},{19,2},{20,3},{21,4},{22,5},{23,6},{24,7},{25,8},{26... | collective-permute-start | bytes 135176 | tf_op jit(solution)/shard_map/ppermute | solution.py:269
  14.6 1.2 %copy-start.1 = (f32[2,62,16,128]{3,2,1,0:T(8,128)S(1)}, f32[2,62,16,128]{3,2,1,0:T(8,128)}, u32[]{:S(2)}) copy-start(f32[2,62,16,128]{3,2,1,0:T(8,128)} %tracers.3) | copy-start | bytes 3047428
  15.8 1.0 %copy-start.4 = (f32[62,16,128]{2,1,0:T(8,128)S(1)}, f32[62,16,128]{2,1,0:T(8,128)}, u32[]{:S(2)}) copy-start(f32[62,16,128]{2,1,0:T(8,128)} %east.3) | copy-start | bytes 1523716
  16.8 1.0 %copy-start.6 = (f32[62,16,128]{2,1,0:T(8,128)S(1)}, f32[62,16,128]{2,1,0:T(8,128)}, u32[]{:S(2)}) copy-start(f32[62,16,128]{2,1,0:T(8,128)} %north.3) | copy-start | bytes 1523716
  17.8 0.7 %copy-start.9 = (s32[16,128]{1,0:T(8,128)S(1)}, s32[16,128]{1,0:T(8,128)}, u32[]{:S(2)}) copy-start(s32[16,128]{1,0:T(8,128)} %count.5) | copy-start | bytes 24580
  18.5 0.7 %copy-start.11 = (s32[16,1,3]{2,1,0:T(1,128)S(1)}, s32[16,1,3]{2,1,0:T(1,128)}, u32[]{:S(2)}) copy-start(s32[16,1,3]{2,1,0:T(1,128)} %copy.13.index) | copy-start | bytes 580
  18.5 11.9 %copy-start.3 = (bf16[64,32,128]{2,1,0:T(8,128)(2,1)S(1)}, bf16[64,32,128]{2,1,0:T(8,128)(2,1)}, u32[]{:S(2)}) copy-start(bf16[64,32,128]{2,1,0:T(8,128)(2,1)} %atm.3) | copy-start | bytes 1572868
  19.0 18.6 %copy-start.5 = (f32[62,16,128]{2,1,0:T(8,128)S(1)}, f32[62,16,128]{2,1,0:T(8,128)}, u32[]{:S(2)}) copy-start(f32[62,16,128]{2,1,0:T(8,128)} %east.3) | copy-start | bytes 1523716
  19.1 18.6 %copy-start.7 = (f32[62,16,128]{2,1,0:T(8,128)S(1)}, f32[62,16,128]{2,1,0:T(8,128)}, u32[]{:S(2)}) copy-start(f32[62,16,128]{2,1,0:T(8,128)} %north.3) | copy-start | bytes 1523716
  19.1 18.6 %copy-start.8 = (f32[62,16,128]{2,1,0:T(8,128)S(1)}, f32[62,16,128]{2,1,0:T(8,128)}, u32[]{:S(2)}) copy-start(f32[62,16,128]{2,1,0:T(8,128)} %mixing.1) | copy-start | bytes 1523716
  19.1 18.6 %copy-start.10 = (s32[16,128]{1,0:T(8,128)S(1)}, s32[16,128]{1,0:T(8,128)}, u32[]{:S(2)}) copy-start(s32[16,128]{1,0:T(8,128)} %count.5) | copy-start | bytes 24580
  19.2 19.1 %copy-start.2 = (f32[2,62,16,128]{3,2,1,0:T(8,128)S(1)}, f32[2,62,16,128]{3,2,1,0:T(8,128)}, u32[]{:S(2)}) copy-start(f32[2,62,16,128]{3,2,1,0:T(8,128)} %tracers.3) | copy-start | bytes 3047428
  20.4 10.7 %collective-permute-start.6 = (f32[3,16,128]{2,1,0:T(8,128)S(1)}, f32[3,16,128]{2,1,0:T(8,128)S(1)}, u32[]{:S(2)}, u32[]{:S(2)}) collective-permute-start(f32[3,16,128]{2,1,0:T(8,128)S(1)} %get-tuple-element.28.after.c), channel_id=1, source_target_pairs={{0,1},{2,3},{4,5},{6,7},{8,9},{10,11},{12,13},{14,15},{16,17},{18,... | collective-permute-start | bytes 73736 | tf_op jit(solution)/shard_map/ppermute | solution.py:257
  20.4 12.6 %collective-permute-start.7 = (f32[3,16,128]{2,1,0:T(8,128)S(1)}, f32[3,16,128]{2,1,0:T(8,128)S(1)}, u32[]{:S(2)}, u32[]{:S(2)}) collective-permute-start(f32[3,16,128]{2,1,0:T(8,128)S(1)} %get-tuple-element.28.after.c), channel_id=1, source_target_pairs={{1,2},{3,4},{5,6},{7,8},{9,10},{11,12},{13,14},{15,16},{17,18},{19... | collective-permute-start | bytes 73736 | tf_op jit(solution)/shard_map/ppermute | solution.py:257
  25.0 13.4 %collective-permute-start.8 = (f32[3,64,128]{2,1,0:T(8,128)S(1)}, f32[3,64,128]{2,1,0:T(8,128)S(1)}, u32[]{:S(2)}, u32[]{:S(2)}) collective-permute-start(f32[3,64,128]{2,1,0:T(8,128)S(1)} %get-tuple-element.40.r0), channel_id=1, source_target_pairs={{0,32},{64,96},{32,0},{96,64},{1,33},{65,97},{33,1},{97,65},{2,34}... | collective-permute-start | bytes 294920 | tf_op jit(solution)/shard_map/ppermute | solution.py:257
  27.9 10.4 %collective-permute-start.9 = (f32[3,64,128]{2,1,0:T(8,128)S(1)}, f32[3,64,128]{2,1,0:T(8,128)S(1)}, u32[]{:S(2)}, u32[]{:S(2)}) collective-permute-start(f32[3,64,128]{2,1,0:T(8,128)S(1)} %get-tuple-element.41.r1), channel_id=1, source_target_pairs={{32,64},{64,32},{33,65},{65,33},{34,66},{66,34},{35,67},{67,35},{3... | collective-permute-start | bytes 294920 | tf_op jit(solution)/shard_map/ppermute | solution.py:257
  31.0 12.5 %collective-permute-start.3 = (bf16[16,32,128]{2,1,0:T(8,128)(2,1)S(1)}, bf16[16,32,128]{2,1,0:T(8,128)(2,1)S(1)}, u32[]{:S(2)}, u32[]{:S(2)}) collective-permute-start(bf16[16,32,128]{2,1,0:T(8,128)(2,1)S(1)} %get-tuple-element.29), channel_id=1, source_target_pairs={{15,0},{16,1},{17,2},{18,3},{19,4},{20,5},{21,6},{22,7},{23,8},{24... | collective-permute-start | bytes 393224 | tf_op jit(solution)/shard_map/ppermute | solution.py:269
  31.1 12.5 %collective-permute-start.4 = (bf16[16,32,128]{2,1,0:T(8,128)(2,1)S(1)}, bf16[16,32,128]{2,1,0:T(8,128)(2,1)S(1)}, u32[]{:S(2)}, u32[]{:S(2)}) collective-permute-start(bf16[16,32,128]{2,1,0:T(8,128)(2,1)S(1)} %get-tuple-element.30), channel_id=1, source_target_pairs={{16,0},{17,1},{18,2},{19,3},{20,4},{21,5},{22,6},{23,7},{24,8},{25... | collective-permute-start | bytes 393224 | tf_op jit(solution)/shard_map/ppermute | solution.py:269
  33.0 13.2 %collective-permute-start.5 = (bf16[16,32,128]{2,1,0:T(8,128)(2,1)S(1)}, bf16[16,32,128]{2,1,0:T(8,128)(2,1)S(1)}, u32[]{:S(2)}, u32[]{:S(2)}) collective-permute-start(bf16[16,32,128]{2,1,0:T(8,128)(2,1)S(1)} %get-tuple-element.31), channel_id=1, source_target_pairs={{17,0},{18,1},{19,2},{20,3},{21,4},{22,5},{23,6},{24,7},{25,8},{26... | collective-permute-start | bytes 393224 | tf_op jit(solution)/shard_map/ppermute | solution.py:269
  40.3 11.7 %collective-permute-start.12 = (f32[2,64,128]{2,1,0:T(8,128)S(1)}, f32[2,64,128]{2,1,0:T(8,128)S(1)}, u32[]{:S(2)}, u32[]{:S(2)}) collective-permute-start(f32[2,64,128]{2,1,0:T(8,128)S(1)} %get-tuple-element.44.u0), channel_id=1, source_target_pairs={{0,32},{64,96},{32,0},{96,64},{1,33},{65,97},{33,1},{97,65},{2,34}... | collective-permute-start | bytes 196616 | tf_op jit(solution)/shard_map/ppermute | solution.py:257
  40.4 11.6 %collective-permute-start.13 = (f32[2,64,128]{2,1,0:T(8,128)S(1)}, f32[2,64,128]{2,1,0:T(8,128)S(1)}, u32[]{:S(2)}, u32[]{:S(2)}) collective-permute-start(f32[2,64,128]{2,1,0:T(8,128)S(1)} %get-tuple-element.45.u1), channel_id=1, source_target_pairs={{32,64},{64,32},{33,65},{65,33},{34,66},{66,34},{35,67},{67,35},{3... | collective-permute-start | bytes 196616 | tf_op jit(solution)/shard_map/ppermute | solution.py:257
  43.5 3.8 %collective-permute-start.10 = (f32[2,16,128]{2,1,0:T(8,128)S(1)}, f32[2,16,128]{2,1,0:T(8,128)S(1)}, u32[]{:S(2)}, u32[]{:S(2)}) collective-permute-start(f32[2,16,128]{2,1,0:T(8,128)S(1)} %get-tuple-element.43.d), channel_id=1, source_target_pairs={{0,1},{2,3},{4,5},{6,7},{8,9},{10,11},{12,13},{14,15},{16,17},{18,... | collective-permute-start | bytes 49160 | tf_op jit(solution)/shard_map/ppermute | solution.py:257
  43.6 8.4 %collective-permute-start.11 = (f32[2,16,128]{2,1,0:T(8,128)S(1)}, f32[2,16,128]{2,1,0:T(8,128)S(1)}, u32[]{:S(2)}, u32[]{:S(2)}) collective-permute-start(f32[2,16,128]{2,1,0:T(8,128)S(1)} %get-tuple-element.43.d), channel_id=1, source_target_pairs={{1,2},{3,4},{5,6},{7,8},{9,10},{11,12},{13,14},{15,16},{17,18},{19... | collective-permute-start | bytes 49160 | tf_op jit(solution)/shard_map/ppermute | solution.py:257

commit v3 on v2

--- a/solution.py
+++ b/solution.py
@@ -27,22 +27,33 @@
     return x if shift == 0 else pltpu.roll(x, shift, x.ndim - 1)
 
 
-def ask_kernel(index, atm, out, held, wide, sem):
-    blocks = atm.shape[0]
-    rows = held.shape[1]
-    copy = pltpu.make_async_copy(atm.at[:, :rows, :], held, sem)
-    copy.start()
-    height = index.shape[0]
+def ask_kernel(index_hbm, atm, out, held, wide, index, sems):
+    blocks, rows = held.shape[:2]
+    parts = sems.shape[0] - 1
+    fetch = pltpu.make_async_copy(index_hbm, index, sems.at[parts])
+    fetch.start()
+    share = blocks // parts
+    copies = [
+        pltpu.make_async_copy(
+            atm.at[p * share : (p + 1) * share, :rows, :], held.at[p * share : (p + 1) * share], sems.at[p]
+        )
+        for p in range(parts)
+    ]
+    for copy in copies:
+        copy.start()
+    height = index.shape[2]
+    fetch.wait()
     for s in range(3):
         for y in range(height):
             at = 2 * blocks + s * height + y
-            b = lax.rem(index[y, 0, s], blocks).astype(F32)
+            b = lax.rem(index[s, 0, y], blocks).astype(F32)
             wide[at : at + 1, :] = jnp.full((1, wide.shape[1]), b, F32)
-    copy.wait()
-    for b in range(blocks):
-        x = held[b].astype(F32)
-        for f in range(2):
-            wide[b + f * blocks : b + f * blocks + 1, :] = x[f : f + 1, :]
+    for p in range(parts):
+        copies[p].wait()
+        for b in range(p * share, (p + 1) * share):
+            x = held[b].astype(F32)
+            for f in range(2):
+                wide[b + f * blocks : b + f * blocks + 1, :] = x[f : f + 1, :]
     out[...] = wide[...].astype(BF16)
 
 
@@ -112,7 +123,7 @@
         held[s] = a[: 2 * blocks].astype(F32)
     for y in range(height):
         for s in range(3):
-            b = lax.rem(index[y, 0, s], blocks)
+            b = lax.rem(index[s, 0, y], blocks)
             for f in range(2):
                 picked[8 * y + f : 8 * y + f + 1, s * 128 : (s + 1) * 128] = held[
                     s, pl.ds(b + f * blocks, 1), :
@@ -229,8 +240,8 @@
          (r0.at[2], r1.at[2], g0.at[2], g1.at[2]), solved, edge_n, edge_s, out, None)
 
 
-def gather_kernel(after, wanted, atm, out0, out1, out2):
-    for s, out in enumerate((out0, out1, out2)):
+def gather_kernel(after, wanted, atm, *outs):
+    for s, out in enumerate(outs):
         for y in range(out.shape[0]):
             out[y] = atm[wanted[s * out.shape[0] + y]]
 
@@ -249,7 +260,7 @@
         out_specs=[VMEM] * len(outs),
         scratch_shapes=list(scratch),
         compiler_params=pltpu.CompilerParams(vmem_limit_bytes=limit),
-        cost_estimate=pl.CostEstimate(flops=0, bytes_accessed=cost * 3000000, transcendentals=0),
+        cost_estimate=pl.CostEstimate(flops=cost * 2000000000, bytes_accessed=cost * 3000000, transcendentals=0),
     )
 
 
@@ -277,18 +288,20 @@
     weights = remap_weights.reshape(height, -1, width)
 
     blocks, fields = atm_flux.shape[:2]
+    index = intersection.transpose(2, 1, 0)
     (few,) = call(
         ask_kernel,
         [sds(2 * blocks + 3 * height, width, dtype=BF16)],
-        [SMEM, ANY],
+        [ANY, ANY],
         [
             pltpu.VMEM((blocks, 16, width), BF16),
             pltpu.VMEM((2 * blocks + 3 * height, width), F32),
-            pltpu.SemaphoreType.DMA,
+            pltpu.SMEM((3, 1, height), jnp.int32),
+            pltpu.SemaphoreType.DMA((5,)),
         ],
         cost=1,
         limit=FULL,
-    )(intersection, atm_flux)
+    )(index, atm_flux)
     slots = [tiles // 2 + s - 1 for s in range(3)]
     part = [from_ahead(few, d) for d in slots]
 
@@ -306,7 +319,7 @@
         [SMEM, SMEM] + [VMEM] * 9,
         [pltpu.VMEM((3, 2 * blocks, width), F32), pltpu.VMEM((8 * height, 3 * width), F32)],
         cost=1,
-    )(place, intersection, *part, weights, level_count, first, tile, tops, bottoms)
+    )(place, index, *part, weights, level_count, first, tile, tops, bottoms)
 
     def exchange(c, r0, r1):
         g0, g1 = swap(r0, "rows", rows0), swap(r1, "rows", rows1)
@@ -316,17 +329,21 @@
     coefficients = call(solver_kernel, [plane] * 7, [ANY] + [VMEM] * 4, cost=4)(
         c, east_speed, north_speed, mixing, level_count
     )
-    wanted = jnp.concatenate(
-        [part[s][2 * blocks + (2 - s) * height :][:height, 0] for s in range(3)]
-    ).astype(jnp.int32)
-    found = call(
-        gather_kernel,
-        [sds(height, fields, width, dtype=BF16)] * 3,
-        [ANY, SMEM, VMEM],
-        cost=1,
-    )(c, wanted, atm_flux)
-    blocks_of = [from_ahead(found[2 - s], slots[s]) for s in range(3)]
-
+    def wanted(*which):
+        return jnp.concatenate(
+            [part[s][2 * blocks + (2 - s) * height :][:height, 0] for s in which]
+        ).astype(jnp.int32)
+
+    def answers(after, *which):
+        found = call(
+            gather_kernel,
+            [sds(height, fields, width, dtype=BF16)] * len(which),
+            [ANY, SMEM, VMEM],
+            cost=1,
+        )(after, wanted(*which), atm_flux)
+        return [from_ahead(block, slots[2 - s]) for s, block in zip(which, found)]
+
+    blocks2, blocks1, blocks0 = answers(c, 0, 1, 2)
     scratch = [pltpu.VMEM((2, levels, height, width), F32)] + [pltpu.VMEM((2, tall, width), F32)] * 2
     field, d, u0, u1 = call(
         first_step_kernel,
@@ -337,7 +354,7 @@
     )(place, tracers, forced, *coefficients, c, c0, c1, r0, r1, g0, g1)
     d0, d1, h0, h1 = exchange(d, u0, u1)
     (ocean_flux,) = call(remap_kernel, [sds(fields, height, width)], [VMEM] * 4, cost=2)(
-        *blocks_of, weights
+        blocks0, blocks1, blocks2, weights
     )
     (result,) = call(
         second_step_kernel,

time: 55.1 us -> 49.7 us (0.902)
  local copies, waits for them, and re-layouts: 5.94 us -> 0.38 us
  starting transfers between devices: 32 us -> 34.9 us
  waiting for transfers between devices: 4.76 us -> 2.79 us
  Pallas kernels: 11 us -> 10.3 us
    unnamed x25 -> x16, local copies, waits for them, and re-layouts: 5.59 us -> 0.04 us
    ppermute x8, starting transfers between devices: 15.4 us -> 18.4 us  [swap(): lax.ppermute(block, axis, [(a, b) for a, b in pairs] + [(b, a) for a, b i...]
    ppermute x8, waiting for transfers between devices: 4.74 us -> 1.93 us  [swap(): lax.ppermute(block, axis, [(a, b) for a, b in pairs] + [(b, a) for a, b i...]
    ppermute x6, waiting for transfers between devices: 0.02 us -> 0.86 us  [from_ahead(): lax.ppermute(block, 'cols', [((i + distance) % tiles, i) for i in range(t...]
    pallas_call x2, Pallas kernels: 3.01 us -> 2.35 us  [the longest x1 1.76 us: per_device(): call(ask_kernel, [sds(2 * blocks + 3 * height, width, dtype=BF16)], [ANY,...]
  transfers between devices with their start and end apart: 14 -> 14, of which waited for: 1 -> 2; matrix products, arithmetic and copies ran while one was open for 1% -> 1% of each run, Pallas kernels for 9% -> 10%
where the time goes in v3:
time: 49.7 us; the launch traced here: 49.3 us
  starting transfers between devices  34.9 us (70%)
  Pallas kernels  10.3 us (21%)
  waiting for transfers between devices  2.79 us (6%)
  between operations  0.79 us (2%)
    ppermute x8, starting transfers between devices, swap(): lax.ppermute(block, axis, [(a, b) for a, b in pairs] + [(b, a) for a, b i...  18.4 us
    ppermute x6, starting transfers between devices, from_ahead(): lax.ppermute(block, 'cols', [((i + distance) % tiles, i) for i in range(t...  16.5 us
    pallas_call x1, Pallas kernels, per_device(): call(second_step_kernel, [sds(2, levels, height, width)], [SMEM] + [VMEM]...  2.65 us
    pallas_call x1, Pallas kernels, per_device(): call(first_step_kernel, [sds(2, levels, height, width), sds(2, height, wi...  1.93 us
    ppermute x8, waiting for transfers between devices, swap(): lax.ppermute(block, axis, [(a, b) for a, b in pairs] + [(b, a) for a, b i...  1.93 us
    pallas_call x1, Pallas kernels, per_device(): call(ask_kernel, [sds(2 * blocks + 3 * height, width, dtype=BF16)], [ANY,...  1.76 us
    pallas_call x1, Pallas kernels, per_device(): call(remap_kernel, [sds(fields, height, width)], [VMEM] * 4, cost=2)  1.12 us
    pallas_call x1, Pallas kernels, per_device(): call(force_kernel, [sds(2, height, width), sds(3, height, width)] + [sds(...  1.05 us
  transfers between devices with their start and end apart: 14, of which 2 were waited for; matrix products, arithmetic and copies ran while one was open for 1% of the time, Pallas kernels for 10%

profile of v3, /device:TPU:1, one launch (start us, length us, event | category | flops | bytes accessed | tf_op | source)
XLA Modules:
  0.0 49.3 jit_solution(8416747151658798228)
XLA Ops:
  0.7 1.8 %shard_map.95 = bf16[176,128]{1,0:T(8,128)(2,1)} custom-call(s32[3,1,16]{2,1,0:T(1,128)} %bitcast.6, bf16[64,32,128]{2,1,0:T(8,128)(2,1)} %atm.3), custom_call_target="tpu_custom_call" | custom-call | flops 2000000000 | bytes 3000000 | tf_op jit(solution)/shard_map/pallas_call | solution.py:292
  2.4 5.0 %collective-permute-start = (bf16[176,128]{1,0:T(8,128)(2,1)}, bf16[176,128]{1,0:T(8,128)(2,1)S(1)}, u32[]{:S(2)}, u32[]{:S(2)}) collective-permute-start(bf16[176,128]{1,0:T(8,128)(2,1)} %shard_map.95), channel_id=1, source_target_pairs={{15,0},{16,1},{17,2},{18,3},{19,4},{20,5},{21,6},{22,7},{23,8},{24... | collective-permute-start | bytes 135176 | tf_op jit(solution)/shard_map/ppermute | solution.py:280
  7.4 0.2 collective-permute-start.1
  7.7 4.7 %collective-permute-start.2 = (bf16[176,128]{1,0:T(8,128)(2,1)}, bf16[176,128]{1,0:T(8,128)(2,1)S(1)}, u32[]{:S(2)}, u32[]{:S(2)}) collective-permute-start(bf16[176,128]{1,0:T(8,128)(2,1)} %shard_map.95), channel_id=1, source_target_pairs={{17,0},{18,1},{19,2},{20,3},{21,4},{22,5},{23,6},{24,7},{25,8},{26... | collective-permute-start | bytes 135176 | tf_op jit(solution)/shard_map/ppermute | solution.py:280
  12.4 0.0 copy-start
  12.4 0.0 copy-start.7
  12.4 0.5 %shard_map.96 = (f32[2,16,128]{2,1,0:T(8,128)S(1)}, f32[3,16,128]{2,1,0:T(8,128)S(1)}, f32[3,64,128]{2,1,0:T(8,128)S(1)}, f32[3,64,128]{2,1,0:T(8,128)S(1)}) custom-call(f32[2,62,16,128]{3,2,1,0:T(8,128)S(1)} %copy-done.1, f32[62,16,128]{2,1,0:T(8,128)S(1)} %copy-done.3, f32[62,16,128]{2,1,0:T(8,128)S(1)} %copy-done.4, s32[16,128]{1,0:T(8,128)S(1)} %copy-done.6), custom_call_target="tpu_custom_call" | custom-call | flops 4000000000 | bytes 6000000 | tf_op jit(solution)/shard_map/pallas_call | solution.py:309
  12.9 0.1 pad_add_fusion.place
  13.0 0.0 collective-permute-done.a0
  13.0 0.0 collective-permute-done.1.a1
  13.0 0.8 %collective-permute-done.2.a2 = bf16[176,128]{1,0:T(8,128)(2,1)S(1)} collective-permute-done((bf16[176,128]{1,0:T(8,128)(2,1)}, bf16[176,128]{1,0:T(8,128)(2,1)S(1)}, u32[]{:S(2)}, u32[]{:S(2)}) %collective-permute-start.2) | collective-permute-done | bytes 45088 | tf_op jit(solution)/shard_map/ppermute | solution.py:280
  13.9 1.0 %shard_map.97 = (f32[2,16,128]{2,1,0:T(8,128)S(1)}, f32[3,16,128]{2,1,0:T(8,128)S(1)}, f32[3,64,128]{2,1,0:T(8,128)S(1)}, f32[3,64,128]{2,1,0:T(8,128)S(1)}) custom-call(s32[2]{0:T(128)S(1)} %pad_add_fusion.place, s32[3,1,16]{2,1,0:T(1,128)S(1)} %bitcast.7, bf16[176,128]{1,0:T(8,128)(2,1)S(1)} %collective-permute-done.a0, ...), custom_call_target="tpu_custom_call" | custom-call | flops 2000000000 | bytes 3000000 | tf_op jit(solution)/shard_map/pallas_call | solution.py:316
  14.9 1.4 %collective-permute-start.6 = (f32[3,16,128]{2,1,0:T(8,128)S(1)}, f32[3,16,128]{2,1,0:T(8,128)S(1)}, u32[]{:S(2)}, u32[]{:S(2)}) collective-permute-start(f32[3,16,128]{2,1,0:T(8,128)S(1)} %get-tuple-element.28.after.c), channel_id=1, source_target_pairs={{0,1},{2,3},{4,5},{6,7},{8,9},{10,11},{12,13},{14,15},{16,17},{18,... | collective-permute-start | bytes 73736 | tf_op jit(solution)/shard_map/ppermute | solution.py:268
  16.3 6.4 %collective-permute-start.7 = (f32[3,16,128]{2,1,0:T(8,128)S(1)}, f32[3,16,128]{2,1,0:T(8,128)S(1)}, u32[]{:S(2)}, u32[]{:S(2)}) collective-permute-start(f32[3,16,128]{2,1,0:T(8,128)S(1)} %get-tuple-element.28.after.c), channel_id=1, source_target_pairs={{1,2},{3,4},{5,6},{7,8},{9,10},{11,12},{13,14},{15,16},{17,18},{19... | collective-permute-start | bytes 73736 | tf_op jit(solution)/shard_map/ppermute | solution.py:268
  22.8 0.6 %shard_map.100 = (f32[62,16,128]{2,1,0:T(8,128)S(1)}, f32[62,16,128]{2,1,0:T(8,128)S(1)}, f32[62,16,128]{2,1,0:T(8,128)S(1)}, f32[62,16,128]{2,1,0:T(8,128)S(1)}...) custom-call(f32[3,16,128]{2,1,0:T(8,128)S(1)} %get-tuple-element.28.after.c, ...), custom_call_target="tpu_custom_call" | custom-call | flops 8000000000 | bytes 12000000 | tf_op jit(solution)/shard_map/pallas_call | solution.py:329
  23.4 3.0 %collective-permute-start.8 = (f32[3,64,128]{2,1,0:T(8,128)S(1)}, f32[3,64,128]{2,1,0:T(8,128)S(1)}, u32[]{:S(2)}, u32[]{:S(2)}) collective-permute-start(f32[3,64,128]{2,1,0:T(8,128)S(1)} %get-tuple-element.40.r0), channel_id=1, source_target_pairs={{0,32},{64,96},{32,0},{96,64},{1,33},{65,97},{33,1},{97,65},{2,34}... | collective-permute-start | bytes 294920 | tf_op jit(solution)/shard_map/ppermute | solution.py:268
  26.4 2.1 %collective-permute-start.9 = (f32[3,64,128]{2,1,0:T(8,128)S(1)}, f32[3,64,128]{2,1,0:T(8,128)S(1)}, u32[]{:S(2)}, u32[]{:S(2)}) collective-permute-start(f32[3,64,128]{2,1,0:T(8,128)S(1)} %get-tuple-element.41.r1), channel_id=1, source_target_pairs={{32,64},{64,32},{33,65},{65,33},{34,66},{66,34},{35,67},{67,35},{3... | collective-permute-start | bytes 294920 | tf_op jit(solution)/shard_map/ppermute | solution.py:268
  28.6 0.1 slice_reduce_fusion
  28.7 0.1 slice_reduce_fusion.1
  28.8 0.1 slice_reduce_fusion.2
  28.9 0.1 maximum_convert_fusion.wanted
  29.0 0.6 %shard_map.98 = (bf16[16,32,128]{2,1,0:T(8,128)(2,1)S(1)}, bf16[16,32,128]{2,1,0:T(8,128)(2,1)S(1)}, bf16[16,32,128]{2,1,0:T(8,128)(2,1)S(1)}) custom-call(f32[3,16,128]{2,1,0:T(8,128)S(1)} %get-tuple-element.28.after.c, s32[48]{0:T(128)S(1)} %maximum_convert_fusion.wanted, bf16[64,32,128]{2,1,0:T(8,128)(2,1)S(1)} %copy-done.2), custom_call_target="tpu_custom_call" | custom-call | flops 2000000000 | bytes 3000000 | tf_op jit(solution)/shard_map/pallas_call | solution.py:338
  29.6 0.1 collective-permute-start.3
  29.7 1.8 %collective-permute-start.4 = (bf16[16,32,128]{2,1,0:T(8,128)(2,1)S(1)}, bf16[16,32,128]{2,1,0:T(8,128)(2,1)S(1)}, u32[]{:S(2)}, u32[]{:S(2)}) collective-permute-start(bf16[16,32,128]{2,1,0:T(8,128)(2,1)S(1)} %get-tuple-element.30), channel_id=1, source_target_pairs={{16,0},{17,1},{18,2},{19,3},{20,4},{21,5},{22,6},{23,7},{24,8},{25... | collective-permute-start | bytes 393224 | tf_op jit(solution)/shard_map/ppermute | solution.py:280
  31.5 4.7 %collective-permute-start.5 = (bf16[16,32,128]{2,1,0:T(8,128)(2,1)S(1)}, bf16[16,32,128]{2,1,0:T(8,128)(2,1)S(1)}, u32[]{:S(2)}, u32[]{:S(2)}) collective-permute-start(bf16[16,32,128]{2,1,0:T(8,128)(2,1)S(1)} %get-tuple-element.31), channel_id=1, source_target_pairs={{17,0},{18,1},{19,2},{20,3},{21,4},{22,5},{23,6},{24,7},{25,8},{26... | collective-permute-start | bytes 393224 | tf_op jit(solution)/shard_map/ppermute | solution.py:280
  36.2 1.9 %shard_map.101 = (f32[2,62,16,128]{3,2,1,0:T(8,128)S(1)}, f32[2,16,128]{2,1,0:T(8,128)S(1)}, f32[2,64,128]{2,1,0:T(8,128)S(1)}, f32[2,64,128]{2,1,0:T(8,128)S(1)}) custom-call(s32[2]{0:T(128)S(1)} %pad_add_fusion.place, f32[2,62,16,128]{3,2,1,0:T(8,128)S(1)} %copy-done.1, f32[2,16,128]{2,1,0:T(8,128)S(1)} %get-tuple-element.32.forced, ...), custom_call_target="tpu_custom_call" | custom-call | flops 8000000000 | bytes 12000000 | tf_op jit(solution)/shard_map/pallas_call | solution.py:348
  38.1 0.1 collective-permute-start.10
  38.2 1.1 %collective-permute-start.11 = (f32[2,16,128]{2,1,0:T(8,128)S(1)}, f32[2,16,128]{2,1,0:T(8,128)S(1)}, u32[]{:S(2)}, u32[]{:S(2)}) collective-permute-start(f32[2,16,128]{2,1,0:T(8,128)S(1)} %get-tuple-element.43.d), channel_id=1, source_target_pairs={{1,2},{3,4},{5,6},{7,8},{9,10},{11,12},{13,14},{15,16},{17,18},{19... | collective-permute-start | bytes 49160 | tf_op jit(solution)/shard_map/ppermute | solution.py:268
  39.3 4.3 %collective-permute-start.13 = (f32[2,64,128]{2,1,0:T(8,128)S(1)}, f32[2,64,128]{2,1,0:T(8,128)S(1)}, u32[]{:S(2)}, u32[]{:S(2)}) collective-permute-start(f32[2,64,128]{2,1,0:T(8,128)S(1)} %get-tuple-element.45.u1), channel_id=1, source_target_pairs={{32,64},{64,32},{33,65},{65,33},{34,66},{66,34},{35,67},{67,35},{3... | collective-permute-start | bytes 196616 | tf_op jit(solution)/shard_map/ppermute | solution.py:268
  43.6 1.1 %shard_map.99 = f32[32,16,128]{2,1,0:T(8,128)} custom-call(bf16[16,32,128]{2,1,0:T(8,128)(2,1)S(1)} %collective-permute-done.3.a0, bf16[16,32,128]{2,1,0:T(8,128)(2,1)S(1)} %collective-permute-done.4.a1, bf16[16,32,128]{2,1,0:T(8,128)(2,1)S(1)} %collective-permute-done.5.a2, bf16[16,384,128]{2,1,0:T(8,128)(2,1)S(1)} %bitcast.5), custom_call_target="tpu_custom_call" | custom-call | flops 4000000000 | bytes 6000000 | tf_op jit(solution)/shard_map/pallas_call | solution.py:356
  44.7 1.9 %collective-permute-done.11.d1 = f32[2,16,128]{2,1,0:T(8,128)S(1)} collective-permute-done((f32[2,16,128]{2,1,0:T(8,128)S(1)}, f32[2,16,128]{2,1,0:T(8,128)S(1)}, u32[]{:S(2)}, u32[]{:S(2)}) %collective-permute-start.11) | collective-permute-done | bytes 16416 | tf_op jit(solution)/shard_map/ppermute | solution.py:268
  46.6 2.7 %shard_map.102 = f32[2,62,16,128]{3,2,1,0:T(8,128)} custom-call(s32[2]{0:T(128)S(1)} %pad_add_fusion.place, f32[2,62,16,128]{3,2,1,0:T(8,128)S(1)} %get-tuple-element.42.field, f32[62,16,128]{2,1,0:T(8,128)S(1)} %get-tuple-element.33.face_e, f32[62,16,128]{2,1,0:T(8,128)S(1)} %get-tuple-element.34.face_w, f32[62,16,128]{2,1,0:T(8,128)S(1)} %get-tuple-element.35.face_n, ...), custom_call_target="tpu_custom_call" | custom-call | flops 6000000000 | bytes 9000000 | tf_op jit(solution)/shard_map/pallas_call | solution.py:359
  (25 shorter events, 0.1 us)
Async XLA Ops:
  0.6 11.7 %copy-start.1 = (f32[2,62,16,128]{3,2,1,0:T(8,128)S(1)}, f32[2,62,16,128]{3,2,1,0:T(8,128)}, u32[]{:S(2)}) copy-start(f32[2,62,16,128]{3,2,1,0:T(8,128)} %tracers.3) | copy-start | bytes 3047428
  0.6 11.7 %copy-start.3 = (f32[62,16,128]{2,1,0:T(8,128)S(1)}, f32[62,16,128]{2,1,0:T(8,128)}, u32[]{:S(2)}) copy-start(f32[62,16,128]{2,1,0:T(8,128)} %east.3) | copy-start | bytes 1523716
  0.7 11.7 %copy-start.4 = (f32[62,16,128]{2,1,0:T(8,128)S(1)}, f32[62,16,128]{2,1,0:T(8,128)}, u32[]{:S(2)}) copy-start(f32[62,16,128]{2,1,0:T(8,128)} %north.3) | copy-start | bytes 1523716
  0.7 11.7 %copy-start.6 = (s32[16,128]{1,0:T(8,128)S(1)}, s32[16,128]{1,0:T(8,128)}, u32[]{:S(2)}) copy-start(s32[16,128]{1,0:T(8,128)} %count.5) | copy-start | bytes 24580
  2.4 10.6 %collective-permute-start = (bf16[176,128]{1,0:T(8,128)(2,1)}, bf16[176,128]{1,0:T(8,128)(2,1)S(1)}, u32[]{:S(2)}, u32[]{:S(2)}) collective-permute-start(bf16[176,128]{1,0:T(8,128)(2,1)} %shard_map.95), channel_id=1, source_target_pairs={{15,0},{16,1},{17,2},{18,3},{19,4},{20,5},{21,6},{22,7},{23,8},{24... | collective-permute-start | bytes 135176 | tf_op jit(solution)/shard_map/ppermute | solution.py:280
  7.4 5.6 %collective-permute-start.1 = (bf16[176,128]{1,0:T(8,128)(2,1)}, bf16[176,128]{1,0:T(8,128)(2,1)S(1)}, u32[]{:S(2)}, u32[]{:S(2)}) collective-permute-start(bf16[176,128]{1,0:T(8,128)(2,1)} %shard_map.95), channel_id=1, source_target_pairs={{16,0},{17,1},{18,2},{19,3},{20,4},{21,5},{22,6},{23,7},{24,8},{25... | collective-permute-start | bytes 135176 | tf_op jit(solution)/shard_map/ppermute | solution.py:280
  7.7 6.2 %collective-permute-start.2 = (bf16[176,128]{1,0:T(8,128)(2,1)}, bf16[176,128]{1,0:T(8,128)(2,1)S(1)}, u32[]{:S(2)}, u32[]{:S(2)}) collective-permute-start(bf16[176,128]{1,0:T(8,128)(2,1)} %shard_map.95), channel_id=1, source_target_pairs={{17,0},{18,1},{19,2},{20,3},{21,4},{22,5},{23,6},{24,7},{25,8},{26... | collective-permute-start | bytes 135176 | tf_op jit(solution)/shard_map/ppermute | solution.py:280
  12.4 1.5 %copy-start = (bf16[16,3,128,128]{3,2,1,0:T(8,128)(2,1)S(1)}, bf16[16,3,128,128]{3,2,1,0:T(8,128)(2,1)}, u32[]{:S(2)}) copy-start(bf16[16,3,128,128]{3,2,1,0:T(8,128)(2,1)} %param.9) | copy-start | bytes 4718596
  12.4 1.5 %copy-start.7 = (s32[16,1,3]{0,1,2:T(1,128)S(1)}, s32[16,1,3]{0,1,2:T(1,128)}, u32[]{:S(2)}) copy-start(s32[16,1,3]{0,1,2:T(1,128)} %param.10) | copy-start | bytes 580
  13.9 8.9 %copy-start.5 = (f32[62,16,128]{2,1,0:T(8,128)S(1)}, f32[62,16,128]{2,1,0:T(8,128)}, u32[]{:S(2)}) copy-start(f32[62,16,128]{2,1,0:T(8,128)} %mixing.1) | copy-start | bytes 1523716
  14.9 14.0 %copy-start.2 = (bf16[64,32,128]{2,1,0:T(8,128)(2,1)S(1)}, bf16[64,32,128]{2,1,0:T(8,128)(2,1)}, u32[]{:S(2)}) copy-start(bf16[64,32,128]{2,1,0:T(8,128)(2,1)} %atm.3) | copy-start | bytes 1572868
  14.9 14.7 %collective-permute-start.6 = (f32[3,16,128]{2,1,0:T(8,128)S(1)}, f32[3,16,128]{2,1,0:T(8,128)S(1)}, u32[]{:S(2)}, u32[]{:S(2)}) collective-permute-start(f32[3,16,128]{2,1,0:T(8,128)S(1)} %get-tuple-element.28.after.c), channel_id=1, source_target_pairs={{0,1},{2,3},{4,5},{6,7},{8,9},{10,11},{12,13},{14,15},{16,17},{18,... | collective-permute-start | bytes 73736 | tf_op jit(solution)/shard_map/ppermute | solution.py:268
  16.3 15.2 %collective-permute-start.7 = (f32[3,16,128]{2,1,0:T(8,128)S(1)}, f32[3,16,128]{2,1,0:T(8,128)S(1)}, u32[]{:S(2)}, u32[]{:S(2)}) collective-permute-start(f32[3,16,128]{2,1,0:T(8,128)S(1)} %get-tuple-element.28.after.c), channel_id=1, source_target_pairs={{1,2},{3,4},{5,6},{7,8},{9,10},{11,12},{13,14},{15,16},{17,18},{19... | collective-permute-start | bytes 73736 | tf_op jit(solution)/shard_map/ppermute | solution.py:268
  23.4 12.8 %collective-permute-start.8 = (f32[3,64,128]{2,1,0:T(8,128)S(1)}, f32[3,64,128]{2,1,0:T(8,128)S(1)}, u32[]{:S(2)}, u32[]{:S(2)}) collective-permute-start(f32[3,64,128]{2,1,0:T(8,128)S(1)} %get-tuple-element.40.r0), channel_id=1, source_target_pairs={{0,32},{64,96},{32,0},{96,64},{1,33},{65,97},{33,1},{97,65},{2,34}... | collective-permute-start | bytes 294920 | tf_op jit(solution)/shard_map/ppermute | solution.py:268
  26.4 9.8 %collective-permute-start.9 = (f32[3,64,128]{2,1,0:T(8,128)S(1)}, f32[3,64,128]{2,1,0:T(8,128)S(1)}, u32[]{:S(2)}, u32[]{:S(2)}) collective-permute-start(f32[3,64,128]{2,1,0:T(8,128)S(1)} %get-tuple-element.41.r1), channel_id=1, source_target_pairs={{32,64},{64,32},{33,65},{65,33},{34,66},{66,34},{35,67},{67,35},{3... | collective-permute-start | bytes 294920 | tf_op jit(solution)/shard_map/ppermute | solution.py:268
  29.6 9.7 %collective-permute-start.3 = (bf16[16,32,128]{2,1,0:T(8,128)(2,1)S(1)}, bf16[16,32,128]{2,1,0:T(8,128)(2,1)S(1)}, u32[]{:S(2)}, u32[]{:S(2)}) collective-permute-start(bf16[16,32,128]{2,1,0:T(8,128)(2,1)S(1)} %get-tuple-element.29), channel_id=1, source_target_pairs={{15,0},{16,1},{17,2},{18,3},{19,4},{20,5},{21,6},{22,7},{23,8},{24... | collective-permute-start | bytes 393224 | tf_op jit(solution)/shard_map/ppermute | solution.py:280
  29.7 9.6 %collective-permute-start.4 = (bf16[16,32,128]{2,1,0:T(8,128)(2,1)S(1)}, bf16[16,32,128]{2,1,0:T(8,128)(2,1)S(1)}, u32[]{:S(2)}, u32[]{:S(2)}) collective-permute-start(bf16[16,32,128]{2,1,0:T(8,128)(2,1)S(1)} %get-tuple-element.30), channel_id=1, source_target_pairs={{16,0},{17,1},{18,2},{19,3},{20,4},{21,5},{22,6},{23,7},{24,8},{25... | collective-permute-start | bytes 393224 | tf_op jit(solution)/shard_map/ppermute | solution.py:280
  31.5 12.1 %collective-permute-start.5 = (bf16[16,32,128]{2,1,0:T(8,128)(2,1)S(1)}, bf16[16,32,128]{2,1,0:T(8,128)(2,1)S(1)}, u32[]{:S(2)}, u32[]{:S(2)}) collective-permute-start(bf16[16,32,128]{2,1,0:T(8,128)(2,1)S(1)} %get-tuple-element.31), channel_id=1, source_target_pairs={{17,0},{18,1},{19,2},{20,3},{21,4},{22,5},{23,6},{24,7},{25,8},{26... | collective-permute-start | bytes 393224 | tf_op jit(solution)/shard_map/ppermute | solution.py:280
  38.1 6.6 %collective-permute-start.10 = (f32[2,16,128]{2,1,0:T(8,128)S(1)}, f32[2,16,128]{2,1,0:T(8,128)S(1)}, u32[]{:S(2)}, u32[]{:S(2)}) collective-permute-start(f32[2,16,128]{2,1,0:T(8,128)S(1)} %get-tuple-element.43.d), channel_id=1, source_target_pairs={{0,1},{2,3},{4,5},{6,7},{8,9},{10,11},{12,13},{14,15},{16,17},{18,... | collective-permute-start | bytes 49160 | tf_op jit(solution)/shard_map/ppermute | solution.py:268
  38.2 8.4 %collective-permute-start.11 = (f32[2,16,128]{2,1,0:T(8,128)S(1)}, f32[2,16,128]{2,1,0:T(8,128)S(1)}, u32[]{:S(2)}, u32[]{:S(2)}) collective-permute-start(f32[2,16,128]{2,1,0:T(8,128)S(1)} %get-tuple-element.43.d), channel_id=1, source_target_pairs={{1,2},{3,4},{5,6},{7,8},{9,10},{11,12},{13,14},{15,16},{17,18},{19... | collective-permute-start | bytes 49160 | tf_op jit(solution)/shard_map/ppermute | solution.py:268
  39.3 7.3 %collective-permute-start.12 = (f32[2,64,128]{2,1,0:T(8,128)S(1)}, f32[2,64,128]{2,1,0:T(8,128)S(1)}, u32[]{:S(2)}, u32[]{:S(2)}) collective-permute-start(f32[2,64,128]{2,1,0:T(8,128)S(1)} %get-tuple-element.44.u0), channel_id=1, source_target_pairs={{0,32},{64,96},{32,0},{96,64},{1,33},{65,97},{33,1},{97,65},{2,34}... | collective-permute-start | bytes 196616 | tf_op jit(solution)/shard_map/ppermute | solution.py:268
  39.3 7.3 %collective-permute-start.13 = (f32[2,64,128]{2,1,0:T(8,128)S(1)}, f32[2,64,128]{2,1,0:T(8,128)S(1)}, u32[]{:S(2)}, u32[]{:S(2)}) collective-permute-start(f32[2,64,128]{2,1,0:T(8,128)S(1)} %get-tuple-element.45.u1), channel_id=1, source_target_pairs={{32,64},{64,32},{33,65},{65,33},{34,66},{66,34},{35,67},{67,35},{3... | collective-permute-start | bytes 196616 | tf_op jit(solution)/shard_map/ppermute | solution.py:268

commit v4 on v3

--- a/solution.py
+++ b/solution.py
@@ -115,12 +115,16 @@
 
 def force_kernel(
     place, index, a0, a1, a2, weights, count, first, tile, tops, bottoms,
-    forced, sent, out_r0, out_r1, held, picked,
+    forced, sent, out_r0, out_r1, wanted, held, picked,
 ):
     height, width = count.shape
     blocks = held.shape[1] // 2
     for s, a in enumerate((a0, a1, a2)):
         held[s] = a[: 2 * blocks].astype(F32)
+        start = 2 * blocks + (2 - s) * height
+        asked = a[start : start + height].astype(F32)
+        own = lanes((height, width)) == sublanes((height, width))
+        wanted[s : s + 1, :] = jnp.sum(jnp.where(own, asked, 0.0), 0, keepdims=True).astype(jnp.int32)
     for y in range(height):
         for s in range(3):
             b = lax.rem(index[s, 0, y], blocks)
@@ -240,10 +244,10 @@
          (r0.at[2], r1.at[2], g0.at[2], g1.at[2]), solved, edge_n, edge_s, out, None)
 
 
-def gather_kernel(after, wanted, atm, *outs):
+def gather_kernel(wanted, atm, *outs):
     for s, out in enumerate(outs):
         for y in range(out.shape[0]):
-            out[y] = atm[wanted[s * out.shape[0] + y]]
+            out[y] = atm[wanted[s, y]]
 
 
 def remap_kernel(a0, a1, a2, weights, out):
@@ -313,9 +317,11 @@
         cost=2,
     )(tracers, east_speed, north_speed, level_count)
 
-    forced, c, r0, r1 = call(
+    forced, c, r0, r1, wanted = call(
         force_kernel,
-        [sds(2, height, width), sds(3, height, width)] + [sds(3, tall, width)] * 2,
+        [sds(2, height, width), sds(3, height, width)]
+        + [sds(3, tall, width)] * 2
+        + [sds(3, width, dtype=jnp.int32)],
         [SMEM, SMEM] + [VMEM] * 9,
         [pltpu.VMEM((3, 2 * blocks, width), F32), pltpu.VMEM((8 * height, 3 * width), F32)],
         cost=1,
@@ -326,24 +332,19 @@
         return swap(c, "cols", cols0), swap(c, "cols", cols1), g0, g1
 
     c0, c1, g0, g1 = exchange(c, r0, r1)
-    coefficients = call(solver_kernel, [plane] * 7, [ANY] + [VMEM] * 4, cost=4)(
-        c, east_speed, north_speed, mixing, level_count
-    )
-    def wanted(*which):
-        return jnp.concatenate(
-            [part[s][2 * blocks + (2 - s) * height :][:height, 0] for s in which]
-        ).astype(jnp.int32)
-
-    def answers(after, *which):
+    coefficients = call(solver_kernel, [plane] * 7, [ANY] + [VMEM] * 4, cost=1)(
+        first, east_speed, north_speed, mixing, level_count
+    )
+    def answers(*which):
         found = call(
             gather_kernel,
             [sds(height, fields, width, dtype=BF16)] * len(which),
-            [ANY, SMEM, VMEM],
+            [SMEM, VMEM],
             cost=1,
-        )(after, wanted(*which), atm_flux)
+        )(wanted, atm_flux)
         return [from_ahead(block, slots[2 - s]) for s, block in zip(which, found)]
 
-    blocks2, blocks1, blocks0 = answers(c, 0, 1, 2)
+    blocks2, blocks1, blocks0 = answers(0, 1, 2)
     scratch = [pltpu.VMEM((2, levels, height, width), F32)] + [pltpu.VMEM((2, tall, width), F32)] * 2
     field, d, u0, u1 = call(
         first_step_kernel,

time: 49.7 us -> 48.7 us (0.980)
  starting transfers between devices: 34.9 us -> 33.8 us
  waiting for transfers between devices: 2.79 us -> 1.92 us
  local copies, waits for them, and re-layouts: 0.38 us -> 1.23 us
    unnamed x16, local copies, waits for them, and re-layouts: 0.04 us -> 1.23 us
    ppermute x8, starting transfers between devices: 18.4 us -> 17.3 us  [swap(): lax.ppermute(block, axis, [(a, b) for a, b in pairs] + [(b, a) for a, b i...]
    ppermute x6, waiting for transfers between devices: 0.86 us -> 0.02 us  [from_ahead(): lax.ppermute(block, 'cols', [((i + distance) % tiles, i) for i in range(t...]
  transfers between devices with their start and end apart: 14 -> 14, of which waited for: 2 -> 1; matrix products, arithmetic and copies ran while one was open for 1% -> 0% of each run, Pallas kernels for 10% -> 10%
where the time goes in v4:
time: 48.7 us; the launch traced here: 48.1 us
  starting transfers between devices  33.8 us (69%)
  Pallas kernels  10.3 us (21%)
  waiting for transfers between devices  1.92 us (4%)
  local copies, waits for them, and re-layouts  1.23 us (3%)
  between operations  0.79 us (2%)
    ppermute x8, starting transfers between devices, swap(): lax.ppermute(block, axis, [(a, b) for a, b in pairs] + [(b, a) for a, b i...  17.3 us
    ppermute x6, starting transfers between devices, from_ahead(): lax.ppermute(block, 'cols', [((i + distance) % tiles, i) for i in range(t...  16.5 us
    pallas_call x1, Pallas kernels, per_device(): call(second_step_kernel, [sds(2, levels, height, width)], [SMEM] + [VMEM]...  2.68 us
    pallas_call x1, Pallas kernels, per_device(): call(first_step_kernel, [sds(2, levels, height, width), sds(2, height, wi...  1.94 us
    ppermute x8, waiting for transfers between devices, swap(): lax.ppermute(block, axis, [(a, b) for a, b in pairs] + [(b, a) for a, b i...  1.9 us
    pallas_call x1, Pallas kernels, per_device(): call(ask_kernel, [sds(2 * blocks + 3 * height, width, dtype=BF16)], [ANY,...  1.76 us
    unnamed x16, local copies, waits for them, and re-layouts  1.23 us
    pallas_call x1, Pallas kernels, per_device(): call(remap_kernel, [sds(fields, height, width)], [VMEM] * 4, cost=2)  1.12 us
  transfers between devices with their start and end apart: 14, of which 1 were waited for; matrix products, arithmetic and copies ran while one was open for 0% of the time, Pallas kernels for 10%

profile of v4, /device:TPU:1, one launch (start us, length us, event | category | flops | bytes accessed | tf_op | source)
XLA Modules:
  0.0 48.1 jit_solution(7803958902108886346)
XLA Ops:
  0.7 1.8 %shard_map.95 = bf16[176,128]{1,0:T(8,128)(2,1)} custom-call(s32[3,1,16]{2,1,0:T(1,128)} %bitcast.6, bf16[64,32,128]{2,1,0:T(8,128)(2,1)} %atm.3), custom_call_target="tpu_custom_call" | custom-call | flops 2000000000 | bytes 3000000 | tf_op jit(solution)/shard_map/pallas_call | solution.py:296
  2.4 5.0 %collective-permute-start = (bf16[176,128]{1,0:T(8,128)(2,1)}, bf16[176,128]{1,0:T(8,128)(2,1)S(1)}, u32[]{:S(2)}, u32[]{:S(2)}) collective-permute-start(bf16[176,128]{1,0:T(8,128)(2,1)} %shard_map.95), channel_id=1, source_target_pairs={{15,0},{16,1},{17,2},{18,3},{19,4},{20,5},{21,6},{22,7},{23,8},{24... | collective-permute-start | bytes 135176 | tf_op jit(solution)/shard_map/ppermute | solution.py:284
  7.4 0.2 collective-permute-start.1
  7.7 4.7 %collective-permute-start.2 = (bf16[176,128]{1,0:T(8,128)(2,1)}, bf16[176,128]{1,0:T(8,128)(2,1)S(1)}, u32[]{:S(2)}, u32[]{:S(2)}) collective-permute-start(bf16[176,128]{1,0:T(8,128)(2,1)} %shard_map.95), channel_id=1, source_target_pairs={{17,0},{18,1},{19,2},{20,3},{21,4},{22,5},{23,6},{24,7},{25,8},{26... | collective-permute-start | bytes 135176 | tf_op jit(solution)/shard_map/ppermute | solution.py:284
  12.4 0.0 copy-start.5
  12.4 0.5 %shard_map.96 = (f32[2,16,128]{2,1,0:T(8,128)S(1)}, f32[3,16,128]{2,1,0:T(8,128)S(1)}, f32[3,64,128]{2,1,0:T(8,128)S(1)}, f32[3,64,128]{2,1,0:T(8,128)S(1)}) custom-call(f32[2,62,16,128]{3,2,1,0:T(8,128)S(1)} %copy-done.1, f32[62,16,128]{2,1,0:T(8,128)S(1)} %copy-done.3, f32[62,16,128]{2,1,0:T(8,128)S(1)} %copy-done.4, s32[16,128]{1,0:T(8,128)S(1)} %copy-done.6), custom_call_target="tpu_custom_call" | custom-call | flops 4000000000 | bytes 6000000 | tf_op jit(solution)/shard_map/pallas_call | solution.py:313
  12.9 0.5 %copy-done.5 = f32[62,16,128]{2,1,0:T(8,128)S(1)} copy-done((f32[62,16,128]{2,1,0:T(8,128)S(1)}, f32[62,16,128]{2,1,0:T(8,128)}, u32[]{:S(2)}) %copy-start.5) | copy-done | bytes 507928
  13.4 0.6 %shard_map.100 = (f32[62,16,128]{2,1,0:T(8,128)S(1)}, f32[62,16,128]{2,1,0:T(8,128)S(1)}, f32[62,16,128]{2,1,0:T(8,128)S(1)}, f32[62,16,128]{2,1,0:T(8,128)S(1)}...) custom-call(f32[2,16,128]{2,1,0:T(8,128)S(1)} %get-tuple-element.25.first.after, ...), custom_call_target="tpu_custom_call" | custom-call | flops 2000000000 | bytes 3000000 | tf_op jit(solution)/shard_map/pallas_call | solution.py:335
  14.1 0.1 pad_add_fusion.place
  14.2 0.0 collective-permute-done.a0
  14.2 0.0 collective-permute-done.1.a1
  14.2 0.7 %copy-done = bf16[16,3,128,128]{3,2,1,0:T(8,128)(2,1)S(1)} copy-done((bf16[16,3,128,128]{3,2,1,0:T(8,128)(2,1)S(1)}, bf16[16,3,128,128]{3,2,1,0:T(8,128)(2,1)}, u32[]{:S(2)}) %copy-start) | copy-done | bytes 1572888
  14.8 1.0 %shard_map.97 = (f32[2,16,128]{2,1,0:T(8,128)S(1)}, f32[3,16,128]{2,1,0:T(8,128)S(1)}, f32[3,64,128]{2,1,0:T(8,128)S(1)}, f32[3,64,128]{2,1,0:T(8,128)S(1)}, s32[3,128]{1,0:T(4,128)S(1)}) custom-call(s32[2]{0:T(128)S(1)} %pad_add_fusion.place, s32[3,1,16]{2,1,0:T(1,128)S(1)} %bitcast.7, bf16[176,128]{1,0:T(8,128)(2,1)S(1)} %collective-permute-done.a0, ...), custom_call_target="tpu_custom_call" | custom-call | flops 2000000000 | bytes 3000000 | tf_op jit(solution)/shard_map/pallas_call | solution.py:320
  15.9 0.4 collective-permute-start.6
  16.3 6.4 %collective-permute-start.7 = (f32[3,16,128]{2,1,0:T(8,128)S(1)}, f32[3,16,128]{2,1,0:T(8,128)S(1)}, u32[]{:S(2)}, u32[]{:S(2)}) collective-permute-start(f32[3,16,128]{2,1,0:T(8,128)S(1)} %get-tuple-element.41.c), channel_id=1, source_target_pairs={{1,2},{3,4},{5,6},{7,8},{9,10},{11,12},{13,14},{15,16},{17,18},{19... | collective-permute-start | bytes 73736 | tf_op jit(solution)/shard_map/ppermute | solution.py:272
  22.7 2.9 %collective-permute-start.8 = (f32[3,64,128]{2,1,0:T(8,128)S(1)}, f32[3,64,128]{2,1,0:T(8,128)S(1)}, u32[]{:S(2)}, u32[]{:S(2)}) collective-permute-start(f32[3,64,128]{2,1,0:T(8,128)S(1)} %get-tuple-element.42.r0), channel_id=1, source_target_pairs={{0,32},{64,96},{32,0},{96,64},{1,33},{65,97},{33,1},{97,65},{2,34}... | collective-permute-start | bytes 294920 | tf_op jit(solution)/shard_map/ppermute | solution.py:272
  25.7 2.1 %collective-permute-start.9 = (f32[3,64,128]{2,1,0:T(8,128)S(1)}, f32[3,64,128]{2,1,0:T(8,128)S(1)}, u32[]{:S(2)}, u32[]{:S(2)}) collective-permute-start(f32[3,64,128]{2,1,0:T(8,128)S(1)} %get-tuple-element.43.r1), channel_id=1, source_target_pairs={{32,64},{64,32},{33,65},{65,33},{34,66},{66,34},{35,67},{67,35},{3... | collective-permute-start | bytes 294920 | tf_op jit(solution)/shard_map/ppermute | solution.py:272
  27.8 0.6 %shard_map.98 = (bf16[16,32,128]{2,1,0:T(8,128)(2,1)S(1)}, bf16[16,32,128]{2,1,0:T(8,128)(2,1)S(1)}, bf16[16,32,128]{2,1,0:T(8,128)(2,1)S(1)}) custom-call(s32[3,128]{1,0:T(4,128)S(1)} %get-tuple-element.29.wanted, bf16[64,32,128]{2,1,0:T(8,128)(2,1)S(1)} %copy-done.2), custom_call_target="tpu_custom_call" | custom-call | flops 2000000000 | bytes 3000000 | tf_op jit(solution)/shard_map/pallas_call | solution.py:339
  28.4 0.1 collective-permute-start.3
  28.5 1.8 %collective-permute-start.4 = (bf16[16,32,128]{2,1,0:T(8,128)(2,1)S(1)}, bf16[16,32,128]{2,1,0:T(8,128)(2,1)S(1)}, u32[]{:S(2)}, u32[]{:S(2)}) collective-permute-start(bf16[16,32,128]{2,1,0:T(8,128)(2,1)S(1)} %get-tuple-element.31), channel_id=1, source_target_pairs={{16,0},{17,1},{18,2},{19,3},{20,4},{21,5},{22,6},{23,7},{24,8},{25... | collective-permute-start | bytes 393224 | tf_op jit(solution)/shard_map/ppermute | solution.py:284
  30.3 0.0 collective-permute-done.7.c1
  30.3 4.7 %collective-permute-start.5 = (bf16[16,32,128]{2,1,0:T(8,128)(2,1)S(1)}, bf16[16,32,128]{2,1,0:T(8,128)(2,1)S(1)}, u32[]{:S(2)}, u32[]{:S(2)}) collective-permute-start(bf16[16,32,128]{2,1,0:T(8,128)(2,1)S(1)} %get-tuple-element.32), channel_id=1, source_target_pairs={{17,0},{18,1},{19,2},{20,3},{21,4},{22,5},{23,6},{24,7},{25,8},{26... | collective-permute-start | bytes 393224 | tf_op jit(solution)/shard_map/ppermute | solution.py:284
  35.0 1.9 %shard_map.101 = (f32[2,62,16,128]{3,2,1,0:T(8,128)S(1)}, f32[2,16,128]{2,1,0:T(8,128)S(1)}, f32[2,64,128]{2,1,0:T(8,128)S(1)}, f32[2,64,128]{2,1,0:T(8,128)S(1)}) custom-call(s32[2]{0:T(128)S(1)} %pad_add_fusion.place, f32[2,62,16,128]{3,2,1,0:T(8,128)S(1)} %copy-done.1, f32[2,16,128]{2,1,0:T(8,128)S(1)} %get-tuple-element.33.forced, ...), custom_call_target="tpu_custom_call" | custom-call | flops 8000000000 | bytes 12000000 | tf_op jit(solution)/shard_map/pallas_call | solution.py:349
  37.0 0.1 collective-permute-start.10
  37.1 1.1 %collective-permute-start.11 = (f32[2,16,128]{2,1,0:T(8,128)S(1)}, f32[2,16,128]{2,1,0:T(8,128)S(1)}, u32[]{:S(2)}, u32[]{:S(2)}) collective-permute-start(f32[2,16,128]{2,1,0:T(8,128)S(1)} %get-tuple-element.45.d), channel_id=1, source_target_pairs={{1,2},{3,4},{5,6},{7,8},{9,10},{11,12},{13,14},{15,16},{17,18},{19... | collective-permute-start | bytes 49160 | tf_op jit(solution)/shard_map/ppermute | solution.py:272
  38.1 0.0 collective-permute-done.3.a0
  38.1 0.0 collective-permute-start.12
  38.1 0.0 collective-permute-done.4.a1
  38.1 4.3 %collective-permute-start.13 = (f32[2,64,128]{2,1,0:T(8,128)S(1)}, f32[2,64,128]{2,1,0:T(8,128)S(1)}, u32[]{:S(2)}, u32[]{:S(2)}) collective-permute-start(f32[2,64,128]{2,1,0:T(8,128)S(1)} %get-tuple-element.47.u1), channel_id=1, source_target_pairs={{32,64},{64,32},{33,65},{65,33},{34,66},{66,34},{35,67},{67,35},{3... | collective-permute-start | bytes 196616 | tf_op jit(solution)/shard_map/ppermute | solution.py:272
  42.4 1.1 %shard_map.99 = f32[32,16,128]{2,1,0:T(8,128)} custom-call(bf16[16,32,128]{2,1,0:T(8,128)(2,1)S(1)} %collective-permute-done.3.a0, bf16[16,32,128]{2,1,0:T(8,128)(2,1)S(1)} %collective-permute-done.4.a1, bf16[16,32,128]{2,1,0:T(8,128)(2,1)S(1)} %collective-permute-done.5.a2, bf16[16,384,128]{2,1,0:T(8,128)(2,1)S(1)} %bitcast.5), custom_call_target="tpu_custom_call" | custom-call | flops 4000000000 | bytes 6000000 | tf_op jit(solution)/shard_map/pallas_call | solution.py:357
  43.6 1.9 %collective-permute-done.11.d1 = f32[2,16,128]{2,1,0:T(8,128)S(1)} collective-permute-done((f32[2,16,128]{2,1,0:T(8,128)S(1)}, f32[2,16,128]{2,1,0:T(8,128)S(1)}, u32[]{:S(2)}, u32[]{:S(2)}) %collective-permute-start.11) | collective-permute-done | bytes 16416 | tf_op jit(solution)/shard_map/ppermute | solution.py:272
  45.5 2.7 %shard_map.102 = f32[2,62,16,128]{3,2,1,0:T(8,128)} custom-call(s32[2]{0:T(128)S(1)} %pad_add_fusion.place, f32[2,62,16,128]{3,2,1,0:T(8,128)S(1)} %get-tuple-element.44.field, f32[62,16,128]{2,1,0:T(8,128)S(1)} %get-tuple-element.34.face_e, f32[62,16,128]{2,1,0:T(8,128)S(1)} %get-tuple-element.35.face_w, f32[62,16,128]{2,1,0:T(8,128)S(1)} %get-tuple-element.36.face_n, ...), custom_call_target="tpu_custom_call" | custom-call | flops 6000000000 | bytes 9000000 | tf_op jit(solution)/shard_map/pallas_call | solution.py:360
  (21 shorter events, 0.0 us)
Async XLA Ops:
  0.6 11.7 %copy-start.1 = (f32[2,62,16,128]{3,2,1,0:T(8,128)S(1)}, f32[2,62,16,128]{3,2,1,0:T(8,128)}, u32[]{:S(2)}) copy-start(f32[2,62,16,128]{3,2,1,0:T(8,128)} %tracers.3) | copy-start | bytes 3047428
  0.6 11.7 %copy-start.3 = (f32[62,16,128]{2,1,0:T(8,128)S(1)}, f32[62,16,128]{2,1,0:T(8,128)}, u32[]{:S(2)}) copy-start(f32[62,16,128]{2,1,0:T(8,128)} %east.3) | copy-start | bytes 1523716
  0.7 11.7 %copy-start.4 = (f32[62,16,128]{2,1,0:T(8,128)S(1)}, f32[62,16,128]{2,1,0:T(8,128)}, u32[]{:S(2)}) copy-start(f32[62,16,128]{2,1,0:T(8,128)} %north.3) | copy-start | bytes 1523716
  0.7 11.7 %copy-start.6 = (s32[16,128]{1,0:T(8,128)S(1)}, s32[16,128]{1,0:T(8,128)}, u32[]{:S(2)}) copy-start(s32[16,128]{1,0:T(8,128)} %count.5) | copy-start | bytes 24580
  2.4 11.7 %collective-permute-start = (bf16[176,128]{1,0:T(8,128)(2,1)}, bf16[176,128]{1,0:T(8,128)(2,1)S(1)}, u32[]{:S(2)}, u32[]{:S(2)}) collective-permute-start(bf16[176,128]{1,0:T(8,128)(2,1)} %shard_map.95), channel_id=1, source_target_pairs={{15,0},{16,1},{17,2},{18,3},{19,4},{20,5},{21,6},{22,7},{23,8},{24... | collective-permute-start | bytes 135176 | tf_op jit(solution)/shard_map/ppermute | solution.py:284
  7.4 6.7 %collective-permute-start.1 = (bf16[176,128]{1,0:T(8,128)(2,1)}, bf16[176,128]{1,0:T(8,128)(2,1)S(1)}, u32[]{:S(2)}, u32[]{:S(2)}) collective-permute-start(bf16[176,128]{1,0:T(8,128)(2,1)} %shard_map.95), channel_id=1, source_target_pairs={{16,0},{17,1},{18,2},{19,3},{20,4},{21,5},{22,6},{23,7},{24,8},{25... | collective-permute-start | bytes 135176 | tf_op jit(solution)/shard_map/ppermute | solution.py:284
  7.7 6.5 %collective-permute-start.2 = (bf16[176,128]{1,0:T(8,128)(2,1)}, bf16[176,128]{1,0:T(8,128)(2,1)S(1)}, u32[]{:S(2)}, u32[]{:S(2)}) collective-permute-start(bf16[176,128]{1,0:T(8,128)(2,1)} %shard_map.95), channel_id=1, source_target_pairs={{17,0},{18,1},{19,2},{20,3},{21,4},{22,5},{23,6},{24,7},{25,8},{26... | collective-permute-start | bytes 135176 | tf_op jit(solution)/shard_map/ppermute | solution.py:284
  12.4 1.0 %copy-start.5 = (f32[62,16,128]{2,1,0:T(8,128)S(1)}, f32[62,16,128]{2,1,0:T(8,128)}, u32[]{:S(2)}) copy-start(f32[62,16,128]{2,1,0:T(8,128)} %mixing.1) | copy-start | bytes 1523716
  13.4 1.4 %copy-start = (bf16[16,3,128,128]{3,2,1,0:T(8,128)(2,1)S(1)}, bf16[16,3,128,128]{3,2,1,0:T(8,128)(2,1)}, u32[]{:S(2)}) copy-start(bf16[16,3,128,128]{3,2,1,0:T(8,128)(2,1)} %param.9) | copy-start | bytes 4718596
  13.4 1.4 %copy-start.7 = (s32[16,1,3]{0,1,2:T(1,128)S(1)}, s32[16,1,3]{0,1,2:T(1,128)}, u32[]{:S(2)}) copy-start(s32[16,1,3]{0,1,2:T(1,128)} %param.10) | copy-start | bytes 580
  14.8 13.0 %copy-start.2 = (bf16[64,32,128]{2,1,0:T(8,128)(2,1)S(1)}, bf16[64,32,128]{2,1,0:T(8,128)(2,1)}, u32[]{:S(2)}) copy-start(bf16[64,32,128]{2,1,0:T(8,128)(2,1)} %atm.3) | copy-start | bytes 1572868
  15.9 12.6 %collective-permute-start.6 = (f32[3,16,128]{2,1,0:T(8,128)S(1)}, f32[3,16,128]{2,1,0:T(8,128)S(1)}, u32[]{:S(2)}, u32[]{:S(2)}) collective-permute-start(f32[3,16,128]{2,1,0:T(8,128)S(1)} %get-tuple-element.41.c), channel_id=1, source_target_pairs={{0,1},{2,3},{4,5},{6,7},{8,9},{10,11},{12,13},{14,15},{16,17},{18,... | collective-permute-start | bytes 73736 | tf_op jit(solution)/shard_map/ppermute | solution.py:272
  16.3 14.0 %collective-permute-start.7 = (f32[3,16,128]{2,1,0:T(8,128)S(1)}, f32[3,16,128]{2,1,0:T(8,128)S(1)}, u32[]{:S(2)}, u32[]{:S(2)}) collective-permute-start(f32[3,16,128]{2,1,0:T(8,128)S(1)} %get-tuple-element.41.c), channel_id=1, source_target_pairs={{1,2},{3,4},{5,6},{7,8},{9,10},{11,12},{13,14},{15,16},{17,18},{19... | collective-permute-start | bytes 73736 | tf_op jit(solution)/shard_map/ppermute | solution.py:272
  22.7 12.3 %collective-permute-start.8 = (f32[3,64,128]{2,1,0:T(8,128)S(1)}, f32[3,64,128]{2,1,0:T(8,128)S(1)}, u32[]{:S(2)}, u32[]{:S(2)}) collective-permute-start(f32[3,64,128]{2,1,0:T(8,128)S(1)} %get-tuple-element.42.r0), channel_id=1, source_target_pairs={{0,32},{64,96},{32,0},{96,64},{1,33},{65,97},{33,1},{97,65},{2,34}... | collective-permute-start | bytes 294920 | tf_op jit(solution)/shard_map/ppermute | solution.py:272
  25.7 9.3 %collective-permute-start.9 = (f32[3,64,128]{2,1,0:T(8,128)S(1)}, f32[3,64,128]{2,1,0:T(8,128)S(1)}, u32[]{:S(2)}, u32[]{:S(2)}) collective-permute-start(f32[3,64,128]{2,1,0:T(8,128)S(1)} %get-tuple-element.43.r1), channel_id=1, source_target_pairs={{32,64},{64,32},{33,65},{65,33},{34,66},{66,34},{35,67},{67,35},{3... | collective-permute-start | bytes 294920 | tf_op jit(solution)/shard_map/ppermute | solution.py:272
  28.4 9.7 %collective-permute-start.3 = (bf16[16,32,128]{2,1,0:T(8,128)(2,1)S(1)}, bf16[16,32,128]{2,1,0:T(8,128)(2,1)S(1)}, u32[]{:S(2)}, u32[]{:S(2)}) collective-permute-start(bf16[16,32,128]{2,1,0:T(8,128)(2,1)S(1)} %get-tuple-element.30), channel_id=1, source_target_pairs={{15,0},{16,1},{17,2},{18,3},{19,4},{20,5},{21,6},{22,7},{23,8},{24... | collective-permute-start | bytes 393224 | tf_op jit(solution)/shard_map/ppermute | solution.py:284
  28.5 9.6 %collective-permute-start.4 = (bf16[16,32,128]{2,1,0:T(8,128)(2,1)S(1)}, bf16[16,32,128]{2,1,0:T(8,128)(2,1)S(1)}, u32[]{:S(2)}, u32[]{:S(2)}) collective-permute-start(bf16[16,32,128]{2,1,0:T(8,128)(2,1)S(1)} %get-tuple-element.31), channel_id=1, source_target_pairs={{16,0},{17,1},{18,2},{19,3},{20,4},{21,5},{22,6},{23,7},{24,8},{25... | collective-permute-start | bytes 393224 | tf_op jit(solution)/shard_map/ppermute | solution.py:284
  30.3 12.1 %collective-permute-start.5 = (bf16[16,32,128]{2,1,0:T(8,128)(2,1)S(1)}, bf16[16,32,128]{2,1,0:T(8,128)(2,1)S(1)}, u32[]{:S(2)}, u32[]{:S(2)}) collective-permute-start(bf16[16,32,128]{2,1,0:T(8,128)(2,1)S(1)} %get-tuple-element.32), channel_id=1, source_target_pairs={{17,0},{18,1},{19,2},{20,3},{21,4},{22,5},{23,6},{24,7},{25,8},{26... | collective-permute-start | bytes 393224 | tf_op jit(solution)/shard_map/ppermute | solution.py:284
  37.0 6.6 %collective-permute-start.10 = (f32[2,16,128]{2,1,0:T(8,128)S(1)}, f32[2,16,128]{2,1,0:T(8,128)S(1)}, u32[]{:S(2)}, u32[]{:S(2)}) collective-permute-start(f32[2,16,128]{2,1,0:T(8,128)S(1)} %get-tuple-element.45.d), channel_id=1, source_target_pairs={{0,1},{2,3},{4,5},{6,7},{8,9},{10,11},{12,13},{14,15},{16,17},{18,... | collective-permute-start | bytes 49160 | tf_op jit(solution)/shard_map/ppermute | solution.py:272
  37.1 8.4 %collective-permute-start.11 = (f32[2,16,128]{2,1,0:T(8,128)S(1)}, f32[2,16,128]{2,1,0:T(8,128)S(1)}, u32[]{:S(2)}, u32[]{:S(2)}) collective-permute-start(f32[2,16,128]{2,1,0:T(8,128)S(1)} %get-tuple-element.45.d), channel_id=1, source_target_pairs={{1,2},{3,4},{5,6},{7,8},{9,10},{11,12},{13,14},{15,16},{17,18},{19... | collective-permute-start | bytes 49160 | tf_op jit(solution)/shard_map/ppermute | solution.py:272
  38.1 7.3 %collective-permute-start.12 = (f32[2,64,128]{2,1,0:T(8,128)S(1)}, f32[2,64,128]{2,1,0:T(8,128)S(1)}, u32[]{:S(2)}, u32[]{:S(2)}) collective-permute-start(f32[2,64,128]{2,1,0:T(8,128)S(1)} %get-tuple-element.46.u0), channel_id=1, source_target_pairs={{0,32},{64,96},{32,0},{96,64},{1,33},{65,97},{33,1},{97,65},{2,34}... | collective-permute-start | bytes 196616 | tf_op jit(solution)/shard_map/ppermute | solution.py:272
  38.1 7.3 %collective-permute-start.13 = (f32[2,64,128]{2,1,0:T(8,128)S(1)}, f32[2,64,128]{2,1,0:T(8,128)S(1)}, u32[]{:S(2)}, u32[]{:S(2)}) collective-permute-start(f32[2,64,128]{2,1,0:T(8,128)S(1)} %get-tuple-element.47.u1), channel_id=1, source_target_pairs={{32,64},{64,32},{33,65},{65,33},{34,66},{66,34},{35,67},{67,35},{3... | collective-permute-start | bytes 196616 | tf_op jit(solution)/shard_map/ppermute | solution.py:272

commit v5 on v4

--- a/solution.py
+++ b/solution.py
@@ -1,3 +1,5 @@
+import functools
+
 import jax
 import jax.numpy as jnp
 from jax import lax
@@ -244,16 +246,22 @@
          (r0.at[2], r1.at[2], g0.at[2], g1.at[2]), solved, edge_n, edge_s, out, None)
 
 
-def gather_kernel(wanted, atm, *outs):
-    for s, out in enumerate(outs):
+def gather_kernel(which, after, wanted, atm, *outs):
+    for s, out in zip(which, outs):
         for y in range(out.shape[0]):
             out[y] = atm[wanted[s, y]]
 
 
-def remap_kernel(a0, a1, a2, weights, out):
+def outer_kernel(a0, a2, weights, out):
     for y in range(out.shape[1]):
-        picked = jnp.concatenate([a0[y], a1[y], a2[y]], 1)
-        out[:, y, :] = jnp.dot(picked, weights[y], preferred_element_type=F32)
+        got = jnp.dot(a0[y], weights[y, :128], preferred_element_type=F32)
+        out[:, y, :] = got + jnp.dot(a2[y], weights[y, 256:], preferred_element_type=F32)
+
+
+def inner_kernel(outer, a1, weights, out):
+    for y in range(out.shape[1]):
+        got = jnp.dot(a1[y], weights[y, 128:256], preferred_element_type=F32)
+        out[:, y, :] = outer[:, y, :] + got
 
 
 def call(kernel, outs, specs, scratch=(), cost=1, limit=LIMIT):
@@ -335,16 +343,16 @@
     coefficients = call(solver_kernel, [plane] * 7, [ANY] + [VMEM] * 4, cost=1)(
         first, east_speed, north_speed, mixing, level_count
     )
-    def answers(*which):
+    def answers(after, *which):
         found = call(
-            gather_kernel,
+            functools.partial(gather_kernel, which),
             [sds(height, fields, width, dtype=BF16)] * len(which),
-            [SMEM, VMEM],
+            [ANY, SMEM, VMEM],
             cost=1,
-        )(wanted, atm_flux)
+        )(after, wanted, atm_flux)
         return [from_ahead(block, slots[2 - s]) for s, block in zip(which, found)]
 
-    blocks2, blocks1, blocks0 = answers(0, 1, 2)
+    blocks2, blocks0 = answers(c, 0, 2)
     scratch = [pltpu.VMEM((2, levels, height, width), F32)] + [pltpu.VMEM((2, tall, width), F32)] * 2
     field, d, u0, u1 = call(
         first_step_kernel,
@@ -354,9 +362,10 @@
         cost=4,
     )(place, tracers, forced, *coefficients, c, c0, c1, r0, r1, g0, g1)
     d0, d1, h0, h1 = exchange(d, u0, u1)
-    (ocean_flux,) = call(remap_kernel, [sds(fields, height, width)], [VMEM] * 4, cost=2)(
-        blocks0, blocks1, blocks2, weights
-    )
+    (outer,) = call(outer_kernel, [sds(fields, height, width)], [VMEM] * 3, cost=1)(
+        blocks0, blocks2, weights
+    )
+    (blocks1,) = answers(d, 1)
     (result,) = call(
         second_step_kernel,
         [sds(2, levels, height, width)],
@@ -364,6 +373,9 @@
         scratch,
         cost=3,
     )(place, field, *coefficients, c, c0, c1, r0, r1, g0, g1, d, d0, d1, u0, u1, h0, h1)
+    (ocean_flux,) = call(inner_kernel, [sds(fields, height, width)], [VMEM] * 3, cost=1)(
+        outer, blocks1, weights
+    )
     return (ocean_flux, result)
 
 

time: 48.7 us -> 48.5 us (level)
  waiting for transfers between devices: 1.92 us -> 0.69 us
  Pallas kernels: 10.3 us -> 11.2 us
    ppermute x6, starting transfers between devices: 16.5 us -> 18 us  [from_ahead(): lax.ppermute(block, 'cols', [((i + distance) % tiles, i) for i in range(t...]
    ppermute x8, waiting for transfers between devices: 1.9 us -> 0.68 us  [swap(): lax.ppermute(block, axis, [(a, b) for a, b in pairs] + [(b, a) for a, b i...]
    ppermute x8, starting transfers between devices: 17.3 us -> 16.3 us  [swap(): lax.ppermute(block, axis, [(a, b) for a, b in pairs] + [(b, a) for a, b i...]
    pallas_call x2 -> x4, Pallas kernels: 1.73 us -> 2.67 us  [the longest x2 1.18 us: answers(): call(functools.partial(gather_kernel, which), [sds(height, fields, width,...]
  transfers between devices with their start and end apart: 14 -> 14, of which waited for: 1 -> 1; matrix products, arithmetic and copies ran while one was open for 0% -> 0% of each run, Pallas kernels for 10% -> 15%
where the time goes in v5:
time: 48.5 us; the launch traced here: 48.3 us
  starting transfers between devices  34.2 us (71%)
  Pallas kernels  11.2 us (23%)
  local copies, waits for them, and re-layouts  1.24 us (3%)
  between operations  0.83 us (2%)
  waiting for transfers between devices  0.69 us (1%)
    ppermute x6, starting transfers between devices, from_ahead(): lax.ppermute(block, 'cols', [((i + distance) % tiles, i) for i in range(t...  18 us
    ppermute x8, starting transfers between devices, swap(): lax.ppermute(block, axis, [(a, b) for a, b in pairs] + [(b, a) for a, b i...  16.3 us
    pallas_call x1, Pallas kernels, per_device(): call(second_step_kernel, [sds(2, levels, height, width)], [SMEM] + [VMEM]...  2.67 us
    pallas_call x1, Pallas kernels, per_device(): call(first_step_kernel, [sds(2, levels, height, width), sds(2, height, wi...  1.94 us
    pallas_call x1, Pallas kernels, per_device(): call(ask_kernel, [sds(2 * blocks + 3 * height, width, dtype=BF16)], [ANY,...  1.76 us
    unnamed x16, local copies, waits for them, and re-layouts  1.24 us
    pallas_call x2, Pallas kernels, answers(): call(functools.partial(gather_kernel, which), [sds(height, fields, width,...  1.18 us
    pallas_call x1, Pallas kernels, per_device(): call(inner_kernel, [sds(fields, height, width)], [VMEM] * 3, cost=1)  1.08 us
  transfers between devices with their start and end apart: 14, of which 1 were waited for; matrix products, arithmetic and copies ran while one was open for 0% of the time, Pallas kernels for 15%

profile of v5, /device:TPU:1, one launch (start us, length us, event | category | flops | bytes accessed | tf_op | source)
XLA Modules:
  0.0 48.3 jit_solution(1151896682012840536)
XLA Ops:
  0.7 1.8 %shard_map.95 = bf16[176,128]{1,0:T(8,128)(2,1)} custom-call(s32[3,1,16]{2,1,0:T(1,128)} %bitcast.7, bf16[64,32,128]{2,1,0:T(8,128)(2,1)} %atm.5), custom_call_target="tpu_custom_call" | custom-call | flops 2000000000 | bytes 3000000 | tf_op jit(solution)/shard_map/pallas_call | solution.py:304
  2.4 5.0 %collective-permute-start = (bf16[176,128]{1,0:T(8,128)(2,1)}, bf16[176,128]{1,0:T(8,128)(2,1)S(1)}, u32[]{:S(2)}, u32[]{:S(2)}) collective-permute-start(bf16[176,128]{1,0:T(8,128)(2,1)} %shard_map.95), channel_id=1, source_target_pairs={{15,0},{16,1},{17,2},{18,3},{19,4},{20,5},{21,6},{22,7},{23,8},{24... | collective-permute-start | bytes 135176 | tf_op jit(solution)/shard_map/ppermute | solution.py:292
  7.4 0.2 collective-permute-start.1
  7.7 4.7 %collective-permute-start.2 = (bf16[176,128]{1,0:T(8,128)(2,1)}, bf16[176,128]{1,0:T(8,128)(2,1)S(1)}, u32[]{:S(2)}, u32[]{:S(2)}) collective-permute-start(bf16[176,128]{1,0:T(8,128)(2,1)} %shard_map.95), channel_id=1, source_target_pairs={{17,0},{18,1},{19,2},{20,3},{21,4},{22,5},{23,6},{24,7},{25,8},{26... | collective-permute-start | bytes 135176 | tf_op jit(solution)/shard_map/ppermute | solution.py:292
  12.4 0.0 copy-start.5
  12.4 0.5 %shard_map.96 = (f32[2,16,128]{2,1,0:T(8,128)S(1)}, f32[3,16,128]{2,1,0:T(8,128)S(1)}, f32[3,64,128]{2,1,0:T(8,128)S(1)}, f32[3,64,128]{2,1,0:T(8,128)S(1)}) custom-call(f32[2,62,16,128]{3,2,1,0:T(8,128)S(1)} %copy-done.1, f32[62,16,128]{2,1,0:T(8,128)S(1)} %copy-done.3, f32[62,16,128]{2,1,0:T(8,128)S(1)} %copy-done.4, s32[16,128]{1,0:T(8,128)S(1)} %copy-done.6), custom_call_target="tpu_custom_call" | custom-call | flops 4000000000 | bytes 6000000 | tf_op jit(solution)/shard_map/pallas_call | solution.py:321
  12.9 0.5 %copy-done.5 = f32[62,16,128]{2,1,0:T(8,128)S(1)} copy-done((f32[62,16,128]{2,1,0:T(8,128)S(1)}, f32[62,16,128]{2,1,0:T(8,128)}, u32[]{:S(2)}) %copy-start.5) | copy-done | bytes 507928
  13.4 0.6 %shard_map.100 = (f32[62,16,128]{2,1,0:T(8,128)S(1)}, f32[62,16,128]{2,1,0:T(8,128)S(1)}, f32[62,16,128]{2,1,0:T(8,128)S(1)}, f32[62,16,128]{2,1,0:T(8,128)S(1)}...) custom-call(f32[2,16,128]{2,1,0:T(8,128)S(1)} %get-tuple-element.24.first.after, ...), custom_call_target="tpu_custom_call" | custom-call | flops 2000000000 | bytes 3000000 | tf_op jit(solution)/shard_map/pallas_call | solution.py:343
  14.1 0.1 pad_add_fusion.place
  14.1 0.0 collective-permute-done.a0
  14.2 0.0 collective-permute-done.1.a1
  14.2 0.0 collective-permute-done.2.a2
  14.2 0.7 %copy-done = bf16[16,3,128,128]{3,2,1,0:T(8,128)(2,1)S(1)} copy-done((bf16[16,3,128,128]{3,2,1,0:T(8,128)(2,1)S(1)}, bf16[16,3,128,128]{3,2,1,0:T(8,128)(2,1)}, u32[]{:S(2)}) %copy-start) | copy-done | bytes 1572888
  14.8 1.0 %shard_map.97 = (f32[2,16,128]{2,1,0:T(8,128)S(1)}, f32[3,16,128]{2,1,0:T(8,128)S(1)}, f32[3,64,128]{2,1,0:T(8,128)S(1)}, f32[3,64,128]{2,1,0:T(8,128)S(1)}, s32[3,128]{1,0:T(4,128)S(1)}) custom-call(s32[2]{0:T(128)S(1)} %pad_add_fusion.place, s32[3,1,16]{2,1,0:T(1,128)S(1)} %bitcast.8, bf16[176,128]{1,0:T(8,128)(2,1)S(1)} %collective-permute-done.a0, ...), custom_call_target="tpu_custom_call" | custom-call | flops 2000000000 | bytes 3000000 | tf_op jit(solution)/shard_map/pallas_call | solution.py:328
  15.9 0.4 collective-permute-start.5
  16.3 6.4 %collective-permute-start.6 = (f32[3,16,128]{2,1,0:T(8,128)S(1)}, f32[3,16,128]{2,1,0:T(8,128)S(1)}, u32[]{:S(2)}, u32[]{:S(2)}) collective-permute-start(f32[3,16,128]{2,1,0:T(8,128)S(1)} %get-tuple-element.28.after.c), channel_id=1, source_target_pairs={{1,2},{3,4},{5,6},{7,8},{9,10},{11,12},{13,14},{15,16},{17,18},{19... | collective-permute-start | bytes 73736 | tf_op jit(solution)/shard_map/ppermute | solution.py:280
  22.7 2.9 %collective-permute-start.7 = (f32[3,64,128]{2,1,0:T(8,128)S(1)}, f32[3,64,128]{2,1,0:T(8,128)S(1)}, u32[]{:S(2)}, u32[]{:S(2)}) collective-permute-start(f32[3,64,128]{2,1,0:T(8,128)S(1)} %get-tuple-element.40.r0), channel_id=1, source_target_pairs={{0,32},{64,96},{32,0},{96,64},{1,33},{65,97},{33,1},{97,65},{2,34}... | collective-permute-start | bytes 294920 | tf_op jit(solution)/shard_map/ppermute | solution.py:280
  25.7 2.1 %collective-permute-start.8 = (f32[3,64,128]{2,1,0:T(8,128)S(1)}, f32[3,64,128]{2,1,0:T(8,128)S(1)}, u32[]{:S(2)}, u32[]{:S(2)}) collective-permute-start(f32[3,64,128]{2,1,0:T(8,128)S(1)} %get-tuple-element.41.r1), channel_id=1, source_target_pairs={{32,64},{64,32},{33,65},{65,33},{34,66},{66,34},{35,67},{67,35},{3... | collective-permute-start | bytes 294920 | tf_op jit(solution)/shard_map/ppermute | solution.py:280
  27.8 0.6 %shard_map.98 = (bf16[16,32,128]{2,1,0:T(8,128)(2,1)S(1)}, bf16[16,32,128]{2,1,0:T(8,128)(2,1)S(1)}) custom-call(f32[3,16,128]{2,1,0:T(8,128)S(1)} %get-tuple-element.28.after.c, s32[3,128]{1,0:T(4,128)S(1)} %get-tuple-element.29.wanted, bf16[64,32,128]{2,1,0:T(8,128)(2,1)S(1)} %copy-done.2), custom_call_target="tpu_custom_call" | custom-call | flops 2000000000 | bytes 3000000 | tf_op jit(solution)/shard_map/pallas_call | solution.py:347
  28.4 0.1 collective-permute-start.3
  28.5 4.8 %collective-permute-start.4 = (bf16[16,32,128]{2,1,0:T(8,128)(2,1)S(1)}, bf16[16,32,128]{2,1,0:T(8,128)(2,1)S(1)}, u32[]{:S(2)}, u32[]{:S(2)}) collective-permute-start(bf16[16,32,128]{2,1,0:T(8,128)(2,1)S(1)} %get-tuple-element.31), channel_id=1, source_target_pairs={{17,0},{18,1},{19,2},{20,3},{21,4},{22,5},{23,6},{24,7},{25,8},{26... | collective-permute-start | bytes 393224 | tf_op jit(solution)/shard_map/ppermute | solution.py:292
  33.3 1.9 %shard_map.101 = (f32[2,62,16,128]{3,2,1,0:T(8,128)S(1)}, f32[2,16,128]{2,1,0:T(8,128)S(1)}, f32[2,64,128]{2,1,0:T(8,128)S(1)}, f32[2,64,128]{2,1,0:T(8,128)S(1)}) custom-call(s32[2]{0:T(128)S(1)} %pad_add_fusion.place, f32[2,62,16,128]{3,2,1,0:T(8,128)S(1)} %copy-done.1, f32[2,16,128]{2,1,0:T(8,128)S(1)} %get-tuple-element.32.forced, ...), custom_call_target="tpu_custom_call" | custom-call | flops 8000000000 | bytes 12000000 | tf_op jit(solution)/shard_map/pallas_call | solution.py:357
  35.2 0.1 collective-permute-start.10
  35.3 1.5 %collective-permute-start.11 = (f32[2,16,128]{2,1,0:T(8,128)S(1)}, f32[2,16,128]{2,1,0:T(8,128)S(1)}, u32[]{:S(2)}, u32[]{:S(2)}) collective-permute-start(f32[2,16,128]{2,1,0:T(8,128)S(1)} %get-tuple-element.42.after.d), channel_id=1, source_target_pairs={{1,2},{3,4},{5,6},{7,8},{9,10},{11,12},{13,14},{15,16},{17,18},{19... | collective-permute-start | bytes 49160 | tf_op jit(solution)/shard_map/ppermute | solution.py:280
  36.9 0.5 %collective-permute-start.12 = (f32[2,64,128]{2,1,0:T(8,128)S(1)}, f32[2,64,128]{2,1,0:T(8,128)S(1)}, u32[]{:S(2)}, u32[]{:S(2)}) collective-permute-start(f32[2,64,128]{2,1,0:T(8,128)S(1)} %get-tuple-element.44.u0), channel_id=1, source_target_pairs={{0,32},{64,96},{32,0},{96,64},{1,33},{65,97},{33,1},{97,65},{2,34}... | collective-permute-start | bytes 196616 | tf_op jit(solution)/shard_map/ppermute | solution.py:280
  37.4 0.6 %shard_map.102 = bf16[16,32,128]{2,1,0:T(8,128)(2,1)S(1)} custom-call(f32[2,16,128]{2,1,0:T(8,128)S(1)} %get-tuple-element.42.after.d, s32[3,128]{1,0:T(4,128)S(1)} %get-tuple-element.29.wanted, bf16[64,32,128]{2,1,0:T(8,128)(2,1)S(1)} %copy-done.2), custom_call_target="tpu_custom_call" | custom-call | flops 2000000000 | bytes 3000000 | tf_op jit(solution)/shard_map/pallas_call | solution.py:347
  38.0 2.2 %collective-permute-start.13 = (f32[2,64,128]{2,1,0:T(8,128)S(1)}, f32[2,64,128]{2,1,0:T(8,128)S(1)}, u32[]{:S(2)}, u32[]{:S(2)}) collective-permute-start(f32[2,64,128]{2,1,0:T(8,128)S(1)} %get-tuple-element.45.u1), channel_id=1, source_target_pairs={{32,64},{64,32},{33,65},{65,33},{34,66},{66,34},{35,67},{67,35},{3... | collective-permute-start | bytes 196616 | tf_op jit(solution)/shard_map/ppermute | solution.py:280
  40.2 3.2 %collective-permute-start.9 = (bf16[16,32,128]{2,1,0:T(8,128)(2,1)S(1)}, bf16[16,32,128]{2,1,0:T(8,128)(2,1)S(1)}, u32[]{:S(2)}, u32[]{:S(2)}) collective-permute-start(bf16[16,32,128]{2,1,0:T(8,128)(2,1)S(1)} %shard_map.102), channel_id=1, source_target_pairs={{16,0},{17,1},{18,2},{19,3},{20,4},{21,5},{22,6},{23,7},{24,8},{25... | collective-permute-start | bytes 393224 | tf_op jit(solution)/shard_map/ppermute | solution.py:292
  43.4 0.4 shard_map.99.outer
  43.9 0.7 %collective-permute-done.13.h1 = f32[2,64,128]{2,1,0:T(8,128)S(1)} collective-permute-done((f32[2,64,128]{2,1,0:T(8,128)S(1)}, f32[2,64,128]{2,1,0:T(8,128)S(1)}, u32[]{:S(2)}, u32[]{:S(2)}) %collective-permute-start.13) | collective-permute-done | bytes 65568 | tf_op jit(solution)/shard_map/ppermute | solution.py:280
  44.5 2.7 %shard_map.104 = f32[2,62,16,128]{3,2,1,0:T(8,128)} custom-call(s32[2]{0:T(128)S(1)} %pad_add_fusion.place, f32[2,62,16,128]{3,2,1,0:T(8,128)S(1)} %get-tuple-element.43.field, f32[62,16,128]{2,1,0:T(8,128)S(1)} %get-tuple-element.33.face_e, f32[62,16,128]{2,1,0:T(8,128)S(1)} %get-tuple-element.34.face_w, f32[62,16,128]{2,1,0:T(8,128)S(1)} %get-tuple-element.35.face_n, ...), custom_call_target="tpu_custom_call" | custom-call | flops 6000000000 | bytes 9000000 | tf_op jit(solution)/shard_map/pallas_call | solution.py:369
  47.2 1.1 %shard_map.103 = f32[32,16,128]{2,1,0:T(8,128)} custom-call(f32[32,16,128]{2,1,0:T(8,128)S(1)} %shard_map.99.outer, bf16[16,32,128]{2,1,0:T(8,128)(2,1)S(1)} %collective-permute-done.9.a1, bf16[16,384,128]{2,1,0:T(8,128)(2,1)S(1)} %bitcast.6), custom_call_target="tpu_custom_call" | custom-call | flops 2000000000 | bytes 3000000 | tf_op jit(solution)/shard_map/pallas_call | solution.py:376
  (23 shorter events, 0.1 us)
Async XLA Ops:
  0.6 11.7 %copy-start.1 = (f32[2,62,16,128]{3,2,1,0:T(8,128)S(1)}, f32[2,62,16,128]{3,2,1,0:T(8,128)}, u32[]{:S(2)}) copy-start(f32[2,62,16,128]{3,2,1,0:T(8,128)} %tracers.3) | copy-start | bytes 3047428
  0.6 11.7 %copy-start.3 = (f32[62,16,128]{2,1,0:T(8,128)S(1)}, f32[62,16,128]{2,1,0:T(8,128)}, u32[]{:S(2)}) copy-start(f32[62,16,128]{2,1,0:T(8,128)} %east.3) | copy-start | bytes 1523716
  0.7 11.7 %copy-start.4 = (f32[62,16,128]{2,1,0:T(8,128)S(1)}, f32[62,16,128]{2,1,0:T(8,128)}, u32[]{:S(2)}) copy-start(f32[62,16,128]{2,1,0:T(8,128)} %north.3) | copy-start | bytes 1523716
  0.7 11.7 %copy-start.6 = (s32[16,128]{1,0:T(8,128)S(1)}, s32[16,128]{1,0:T(8,128)}, u32[]{:S(2)}) copy-start(s32[16,128]{1,0:T(8,128)} %count.5) | copy-start | bytes 24580
  2.4 11.7 %collective-permute-start = (bf16[176,128]{1,0:T(8,128)(2,1)}, bf16[176,128]{1,0:T(8,128)(2,1)S(1)}, u32[]{:S(2)}, u32[]{:S(2)}) collective-permute-start(bf16[176,128]{1,0:T(8,128)(2,1)} %shard_map.95), channel_id=1, source_target_pairs={{15,0},{16,1},{17,2},{18,3},{19,4},{20,5},{21,6},{22,7},{23,8},{24... | collective-permute-start | bytes 135176 | tf_op jit(solution)/shard_map/ppermute | solution.py:292
  7.4 6.7 %collective-permute-start.1 = (bf16[176,128]{1,0:T(8,128)(2,1)}, bf16[176,128]{1,0:T(8,128)(2,1)S(1)}, u32[]{:S(2)}, u32[]{:S(2)}) collective-permute-start(bf16[176,128]{1,0:T(8,128)(2,1)} %shard_map.95), channel_id=1, source_target_pairs={{16,0},{17,1},{18,2},{19,3},{20,4},{21,5},{22,6},{23,7},{24,8},{25... | collective-permute-start | bytes 135176 | tf_op jit(solution)/shard_map/ppermute | solution.py:292
  7.7 6.5 %collective-permute-start.2 = (bf16[176,128]{1,0:T(8,128)(2,1)}, bf16[176,128]{1,0:T(8,128)(2,1)S(1)}, u32[]{:S(2)}, u32[]{:S(2)}) collective-permute-start(bf16[176,128]{1,0:T(8,128)(2,1)} %shard_map.95), channel_id=1, source_target_pairs={{17,0},{18,1},{19,2},{20,3},{21,4},{22,5},{23,6},{24,7},{25,8},{26... | collective-permute-start | bytes 135176 | tf_op jit(solution)/shard_map/ppermute | solution.py:292
  12.4 1.0 %copy-start.5 = (f32[62,16,128]{2,1,0:T(8,128)S(1)}, f32[62,16,128]{2,1,0:T(8,128)}, u32[]{:S(2)}) copy-start(f32[62,16,128]{2,1,0:T(8,128)} %mixing.1) | copy-start | bytes 1523716
  13.4 1.4 %copy-start = (bf16[16,3,128,128]{3,2,1,0:T(8,128)(2,1)S(1)}, bf16[16,3,128,128]{3,2,1,0:T(8,128)(2,1)}, u32[]{:S(2)}) copy-start(bf16[16,3,128,128]{3,2,1,0:T(8,128)(2,1)} %param.9) | copy-start | bytes 4718596
  13.4 1.4 %copy-start.7 = (s32[16,1,3]{0,1,2:T(1,128)S(1)}, s32[16,1,3]{0,1,2:T(1,128)}, u32[]{:S(2)}) copy-start(s32[16,1,3]{0,1,2:T(1,128)} %param.10) | copy-start | bytes 580
  14.8 13.0 %copy-start.2 = (bf16[64,32,128]{2,1,0:T(8,128)(2,1)S(1)}, bf16[64,32,128]{2,1,0:T(8,128)(2,1)}, u32[]{:S(2)}) copy-start(bf16[64,32,128]{2,1,0:T(8,128)(2,1)} %atm.5) | copy-start | bytes 1572868
  15.9 12.6 %collective-permute-start.5 = (f32[3,16,128]{2,1,0:T(8,128)S(1)}, f32[3,16,128]{2,1,0:T(8,128)S(1)}, u32[]{:S(2)}, u32[]{:S(2)}) collective-permute-start(f32[3,16,128]{2,1,0:T(8,128)S(1)} %get-tuple-element.28.after.c), channel_id=1, source_target_pairs={{0,1},{2,3},{4,5},{6,7},{8,9},{10,11},{12,13},{14,15},{16,17},{18,... | collective-permute-start | bytes 73736 | tf_op jit(solution)/shard_map/ppermute | solution.py:280
  16.3 17.0 %collective-permute-start.6 = (f32[3,16,128]{2,1,0:T(8,128)S(1)}, f32[3,16,128]{2,1,0:T(8,128)S(1)}, u32[]{:S(2)}, u32[]{:S(2)}) collective-permute-start(f32[3,16,128]{2,1,0:T(8,128)S(1)} %get-tuple-element.28.after.c), channel_id=1, source_target_pairs={{1,2},{3,4},{5,6},{7,8},{9,10},{11,12},{13,14},{15,16},{17,18},{19... | collective-permute-start | bytes 73736 | tf_op jit(solution)/shard_map/ppermute | solution.py:280
  22.7 10.5 %collective-permute-start.7 = (f32[3,64,128]{2,1,0:T(8,128)S(1)}, f32[3,64,128]{2,1,0:T(8,128)S(1)}, u32[]{:S(2)}, u32[]{:S(2)}) collective-permute-start(f32[3,64,128]{2,1,0:T(8,128)S(1)} %get-tuple-element.40.r0), channel_id=1, source_target_pairs={{0,32},{64,96},{32,0},{96,64},{1,33},{65,97},{33,1},{97,65},{2,34}... | collective-permute-start | bytes 294920 | tf_op jit(solution)/shard_map/ppermute | solution.py:280
  25.7 7.6 %collective-permute-start.8 = (f32[3,64,128]{2,1,0:T(8,128)S(1)}, f32[3,64,128]{2,1,0:T(8,128)S(1)}, u32[]{:S(2)}, u32[]{:S(2)}) collective-permute-start(f32[3,64,128]{2,1,0:T(8,128)S(1)} %get-tuple-element.41.r1), channel_id=1, source_target_pairs={{32,64},{64,32},{33,65},{65,33},{34,66},{66,34},{35,67},{67,35},{3... | collective-permute-start | bytes 294920 | tf_op jit(solution)/shard_map/ppermute | solution.py:280
  28.4 9.5 %collective-permute-start.3 = (bf16[16,32,128]{2,1,0:T(8,128)(2,1)S(1)}, bf16[16,32,128]{2,1,0:T(8,128)(2,1)S(1)}, u32[]{:S(2)}, u32[]{:S(2)}) collective-permute-start(bf16[16,32,128]{2,1,0:T(8,128)(2,1)S(1)} %get-tuple-element.30), channel_id=1, source_target_pairs={{15,0},{16,1},{17,2},{18,3},{19,4},{20,5},{21,6},{22,7},{23,8},{24... | collective-permute-start | bytes 393224 | tf_op jit(solution)/shard_map/ppermute | solution.py:292
  28.5 11.7 %collective-permute-start.4 = (bf16[16,32,128]{2,1,0:T(8,128)(2,1)S(1)}, bf16[16,32,128]{2,1,0:T(8,128)(2,1)S(1)}, u32[]{:S(2)}, u32[]{:S(2)}) collective-permute-start(bf16[16,32,128]{2,1,0:T(8,128)(2,1)S(1)} %get-tuple-element.31), channel_id=1, source_target_pairs={{17,0},{18,1},{19,2},{20,3},{21,4},{22,5},{23,6},{24,7},{25,8},{26... | collective-permute-start | bytes 393224 | tf_op jit(solution)/shard_map/ppermute | solution.py:292
  35.2 8.6 %collective-permute-start.10 = (f32[2,16,128]{2,1,0:T(8,128)S(1)}, f32[2,16,128]{2,1,0:T(8,128)S(1)}, u32[]{:S(2)}, u32[]{:S(2)}) collective-permute-start(f32[2,16,128]{2,1,0:T(8,128)S(1)} %get-tuple-element.42.after.d), channel_id=1, source_target_pairs={{0,1},{2,3},{4,5},{6,7},{8,9},{10,11},{12,13},{14,15},{16,17},{18,... | collective-permute-start | bytes 49160 | tf_op jit(solution)/shard_map/ppermute | solution.py:280
  35.3 8.5 %collective-permute-start.11 = (f32[2,16,128]{2,1,0:T(8,128)S(1)}, f32[2,16,128]{2,1,0:T(8,128)S(1)}, u32[]{:S(2)}, u32[]{:S(2)}) collective-permute-start(f32[2,16,128]{2,1,0:T(8,128)S(1)} %get-tuple-element.42.after.d), channel_id=1, source_target_pairs={{1,2},{3,4},{5,6},{7,8},{9,10},{11,12},{13,14},{15,16},{17,18},{19... | collective-permute-start | bytes 49160 | tf_op jit(solution)/shard_map/ppermute | solution.py:280
  36.9 7.0 %collective-permute-start.12 = (f32[2,64,128]{2,1,0:T(8,128)S(1)}, f32[2,64,128]{2,1,0:T(8,128)S(1)}, u32[]{:S(2)}, u32[]{:S(2)}) collective-permute-start(f32[2,64,128]{2,1,0:T(8,128)S(1)} %get-tuple-element.44.u0), channel_id=1, source_target_pairs={{0,32},{64,96},{32,0},{96,64},{1,33},{65,97},{33,1},{97,65},{2,34}... | collective-permute-start | bytes 196616 | tf_op jit(solution)/shard_map/ppermute | solution.py:280
  38.0 6.6 %collective-permute-start.13 = (f32[2,64,128]{2,1,0:T(8,128)S(1)}, f32[2,64,128]{2,1,0:T(8,128)S(1)}, u32[]{:S(2)}, u32[]{:S(2)}) collective-permute-start(f32[2,64,128]{2,1,0:T(8,128)S(1)} %get-tuple-element.45.u1), channel_id=1, source_target_pairs={{32,64},{64,32},{33,65},{65,33},{34,66},{66,34},{35,67},{67,35},{3... | collective-permute-start | bytes 196616 | tf_op jit(solution)/shard_map/ppermute | solution.py:280
  40.2 7.0 %collective-permute-start.9 = (bf16[16,32,128]{2,1,0:T(8,128)(2,1)S(1)}, bf16[16,32,128]{2,1,0:T(8,128)(2,1)S(1)}, u32[]{:S(2)}, u32[]{:S(2)}) collective-permute-start(bf16[16,32,128]{2,1,0:T(8,128)(2,1)S(1)} %shard_map.102), channel_id=1, source_target_pairs={{16,0},{17,1},{18,2},{19,3},{20,4},{21,5},{22,6},{23,7},{24,8},{25... | collective-permute-start | bytes 393224 | tf_op jit(solution)/shard_map/ppermute | solution.py:292
